TPU v7x, 32 devices: a whole 2x2x4 slice. The times are simulated.
32 devices in a mesh: dp: 8 (over z, x), tensor: 4 (over y, core).
Axes of the slice: x: 2, y: 2, z: 4, core: 2. Of those that a mesh axis runs over, the one named last changes fastest.
Arguments:
- block_input: bfloat16 [16384, 2048], P('dp'), may hold values from -6 to 6
- cotangent: bfloat16 [16384, 2048], P('dp')
- segment_ids: int32 [8, 2048], P('dp'), may hold values from 0 to 15, never falling along the last dimension, each value on 1 to 1024 neighbouring positions
- w_in: float32 [2048, 7, 2048], P('dp', None, 'tensor')
- w_in_m: float32 [2048, 7, 2048], P('dp', None, 'tensor'), may hold values from -0.00024414062 to 0.00024414062
- w_in_v: float32 [2048, 7, 2048], P('dp', None, 'tensor'), may hold values from 1.0490417e-09 to 4.172325e-09
- w_outs: float32 [2048, 5, 2048], P('dp', None, 'tensor')
- w_outs_m: float32 [2048, 5, 2048], P('dp', None, 'tensor'), may hold values from -0.00024414062 to 0.00024414062
- w_outs_v: float32 [2048, 5, 2048], P('dp', None, 'tensor'), may hold values from 1.0490417e-09 to 4.172325e-09
- in_bias: float32 [7, 32, 64], P(None, 'tensor', 'dp'), may hold values from -1.5 to 1.5
- in_bias_m: float32 [7, 32, 64], P(None, 'tensor', 'dp'), may hold values from -0.00024414062 to 0.00024414062
- in_bias_v: float32 [7, 32, 64], P(None, 'tensor', 'dp'), may hold values from 1.0490417e-09 to 4.172325e-09
- vectors: float32 [4, 2048], P(None, 'dp')
- vectors_m: float32 [4, 2048], P(None, 'dp'), may hold values from -0.0009765625 to 0.0009765625
- vectors_v: float32 [4, 2048], P(None, 'dp'), may hold values from 1.66893e-08 to 6.67572e-08
Outputs:
- output: bfloat16 [16384, 2048], P('dp')
- block_input_gradient: bfloat16 [16384, 2048], P('dp')
- grad_norm: float32 [], replicated
- new_w_in: float32 [2048, 7, 2048], P('dp', None, 'tensor')
- new_w_in_m: float32 [2048, 7, 2048], P('dp', None, 'tensor')
- new_w_in_v: float32 [2048, 7, 2048], P('dp', None, 'tensor')
- new_w_outs: float32 [2048, 5, 2048], P('dp', None, 'tensor')
- new_w_outs_m: float32 [2048, 5, 2048], P('dp', None, 'tensor')
- new_w_outs_v: float32 [2048, 5, 2048], P('dp', None, 'tensor')
- new_in_bias: float32 [7, 32, 64], P(None, 'tensor', 'dp')
- new_in_bias_m: float32 [7, 32, 64], P(None, 'tensor', 'dp')
- new_in_bias_v: float32 [7, 32, 64], P(None, 'tensor', 'dp')
- new_vectors: float32 [4, 2048], P(None, 'dp')
- new_vectors_m: float32 [4, 2048], P(None, 'dp')
- new_vectors_v: float32 [4, 2048], P(None, 'dp')
Inputs may be any that keep to these rules, and one draw needn't show every extreme that they name: `segment_ids`: along each packed row of 2048 tokens the ids never fall; a document is a run of equal ids within one row.
All inputs are finite; a program needn't handle non-finite values.
Results may differ from a plain program's by a relative error of at most 0.006.
The roundings to bfloat16 on the way count: a program that leaves them out, or rounds other values in their place, can miss the bound.
Values may be sent and summed in bfloat16 or wider, within the bound.
No kernel may reach another device: no remote copies, remote signals or barrier semaphores. Data moves between devices by JAX's collectives and lax.ppermute only.
A program may use at most 384 MiB of HBM per device.

v0:
```python
from functools import partial

import jax
import jax.numpy as jnp
from jax import lax
from jax.sharding import PartitionSpec as P

HDIM = 64
ROT = 32
STEP = 10


BETA_ONE = 0.9
BETA_TWO = 0.95
EPSILON = 1e-08
CLIP_AT = 1.0
RATE_MATRIX = 0.06
RATE_VECTOR = 0.6
DECAY_MATRIX = 0.1


def rotate(values, cosines, sines):
    half = cosines.shape[-1]
    first = values[..., :half]
    second = values[..., half : 2 * half]
    return jnp.concatenate(
        [
            first * cosines - second * sines,
            second * cosines + first * sines,
            values[..., 2 * half :],
        ],
        -1,
    )


def row_angles(segment_ids):
    row_count, length = segment_ids.shape
    place = jnp.arange(length, dtype=jnp.int32)
    boundary = jnp.concatenate(
        [jnp.ones((row_count, 1), jnp.bool_), segment_ids[:, 1:] != segment_ids[:, :-1]], 1
    )
    start = lax.cummax(jnp.where(boundary, place[None, :], 0), axis=1)
    offset = (place[None, :] - start).astype(jnp.float32).reshape(row_count * length)
    freq = 10000.0 ** (-jnp.arange(ROT // 2, dtype=jnp.float32) * 2.0 / ROT)
    theta = offset[:, None] * freq[None, :]
    return (jnp.cos(theta)[:, None, :], jnp.sin(theta)[:, None, :])


def block_scores(query, keys, seg_query, seg_keys, first, scale):
    scores = jnp.einsum("qhd,khd->hqk", query, keys, preferred_element_type=jnp.float32) * scale
    rows_here = first + jnp.arange(query.shape[0], dtype=jnp.int32)
    columns = jnp.arange(keys.shape[0], dtype=jnp.int32)
    allowed = (seg_query[:, None] == seg_keys[None, :]) & (rows_here[:, None] >= columns[None, :])
    return jnp.where(allowed[None], scores, -1e30)


def adamw(weight, first, second, grad, factor, rate, decay):
    clipped = grad * factor
    first = BETA_ONE * first + (1.0 - BETA_ONE) * clipped
    second = BETA_TWO * second + (1.0 - BETA_TWO) * clipped * clipped
    first_hat = first / (1.0 - BETA_ONE**STEP)
    second_hat = second / (1.0 - BETA_TWO**STEP)
    weight = weight - rate * (first_hat / (jnp.sqrt(second_hat) + EPSILON) + decay * weight)
    return (weight, first, second)


def contract_rows(left, right):
    return lax.dot_general(
        left, right, (((0,), (0,)), ((), ())), preferred_element_type=jnp.float32
    )


def contract_cols(left, right):
    return lax.dot_general(
        left, right, (((1,), (1,)), ((), ())), preferred_element_type=jnp.float32
    )


def layer_norm_backward(
    normalized_gradient, norm_gain, standardized_input, inverse_deviation, cotangent
):
    scaled_rows = normalized_gradient * norm_gain
    ln_grad = inverse_deviation * (
        scaled_rows
        - jnp.mean(scaled_rows, -1, keepdims=True)
        - standardized_input * jnp.mean(scaled_rows * standardized_input, -1, keepdims=True)
    )
    grad_rows = (cotangent.astype(jnp.float32) + ln_grad).astype(jnp.bfloat16)
    output_total = jnp.sum(cotangent, 0, dtype=jnp.float32)
    vector_rows = jnp.stack(
        [
            jnp.sum(normalized_gradient * standardized_input, 0),
            jnp.sum(normalized_gradient, 0),
            output_total,
            output_total,
        ],
        0,
    )
    return (grad_rows, vector_rows)


def body(
    block_input,
    cotangent,
    segment_ids,
    w_in,
    w_in_m,
    w_in_v,
    w_outs,
    w_outs_m,
    w_outs_v,
    in_bias,
    in_bias_m,
    in_bias_v,
    vectors,
    vectors_m,
    vectors_v,
):
    tensor_count = lax.axis_size("tensor")
    in_full, outs_full, bias_full, vector_complete = (
        lax.all_gather(w_in.astype(jnp.bfloat16), "dp", axis=0, tiled=True),
        lax.all_gather(w_outs.astype(jnp.bfloat16), "dp", axis=0, tiled=True),
        lax.all_gather(in_bias.astype(jnp.bfloat16), "dp", axis=2, tiled=True),
        lax.all_gather(vectors.astype(jnp.bfloat16), "dp", axis=1, tiled=True),
    )
    tokens, width = block_input.shape
    local = in_full.shape[2]
    heads_here = local // HDIM
    row_count, length = segment_ids.shape
    block = min(512, length)
    scale = HDIM ** (-0.5)
    x_float = block_input.astype(jnp.float32)
    row_mean = jnp.mean(x_float, -1, keepdims=True)
    centered_rows = x_float - row_mean
    row_variance = jnp.mean(centered_rows * centered_rows, -1, keepdims=True)
    inverse_deviation = lax.rsqrt(row_variance + 1e-05)
    standardized_input = centered_rows * inverse_deviation
    norm_gain = vector_complete[0].astype(jnp.float32)
    normalized_rows = (
        standardized_input * norm_gain + vector_complete[1].astype(jnp.float32)
    ).astype(jnp.bfloat16)
    in_flat = in_full.reshape(width, 7 * local)
    z_flat = jnp.dot(
        normalized_rows, in_flat, preferred_element_type=jnp.float32
    ) + bias_full.reshape(7 * local).astype(jnp.float32)
    z_all = z_flat.reshape(tokens, 7, local)
    cosines, sines = row_angles(segment_ids)
    query = rotate(z_all[:, 0].reshape(tokens, heads_here, HDIM), cosines, sines).astype(
        jnp.bfloat16
    )
    keys = rotate(z_all[:, 1].reshape(tokens, heads_here, HDIM), cosines, sines).astype(
        jnp.bfloat16
    )
    vals = z_all[:, 2].reshape(tokens, heads_here, HDIM).astype(jnp.bfloat16)
    mixed_parts = []
    saved_lse = []
    row = 0
    base = row * length
    for first in range(0, length, block):
        end = first + block
        scores = block_scores(
            query[base + first : base + end],
            keys[base : base + end],
            segment_ids[row, first:end],
            segment_ids[row, :end],
            first,
            scale,
        )
        top = jnp.max(scores, -1, keepdims=True)
        lse = top + jnp.log(jnp.sum(jnp.exp(scores - top), -1, keepdims=True))
        probs = jnp.exp(scores - lse).astype(jnp.bfloat16)
        mixed_parts.append(
            jnp.einsum(
                "hqk,khd->qhd", probs, vals[base : base + end], preferred_element_type=jnp.float32
            )
        )
        saved_lse.append(lse)
    attn = jnp.concatenate(mixed_parts, 0).reshape(tokens, local).astype(jnp.bfloat16)
    hidden_pre = z_all[:, 3:].reshape(tokens, 4 * local)
    hidden_float, gelu_pull = jax.vjp(partial(jax.nn.gelu, approximate=True), hidden_pre)
    joined = jnp.concatenate([attn, hidden_float.astype(jnp.bfloat16)], 1)
    outs_flat = outs_full.reshape(width, 5 * local)
    partial_sum = contract_cols(joined, outs_flat)
    dense_bias = vector_complete[2].astype(jnp.float32)
    second_bias = vector_complete[3].astype(jnp.float32)
    summed = lax.psum(partial_sum, "tensor")
    output = (x_float + summed + dense_bias + second_bias).astype(jnp.bfloat16)
    d_joined = jnp.dot(cotangent, outs_flat, preferred_element_type=jnp.float32)
    d_attn = d_joined[:, :local].astype(jnp.bfloat16).reshape(tokens, heads_here, HDIM)
    d_pre = gelu_pull(d_joined[:, local:])[0]
    d_query_parts = []
    count = 0
    row = 0
    base = row * length
    d_keys_row = jnp.zeros((length, heads_here, HDIM), jnp.float32)
    d_vals_row = jnp.zeros((length, heads_here, HDIM), jnp.float32)
    for first in range(0, length, block):
        end = first + block
        query_block = query[base + first : base + end]
        key_block = keys[base : base + end]
        scores = block_scores(
            query_block,
            key_block,
            segment_ids[row, first:end],
            segment_ids[row, :end],
            first,
            scale,
        )
        probs = jnp.exp(scores - saved_lse[count])
        count = count + 1
        grad_block = d_attn[base + first : base + end]
        d_probs = jnp.einsum(
            "qhd,khd->hqk", grad_block, vals[base : base + end], preferred_element_type=jnp.float32
        )
        delta = jnp.sum(probs * d_probs, -1, keepdims=True)
        d_scores = (probs * (d_probs - delta)).astype(jnp.bfloat16)
        d_query_parts.append(
            jnp.einsum("hqk,khd->qhd", d_scores, key_block, preferred_element_type=jnp.float32)
            * scale
        )
        d_keys_row = d_keys_row.at[:end].add(
            jnp.einsum("hqk,qhd->khd", d_scores, query_block, preferred_element_type=jnp.float32)
            * scale
        )
        d_vals_row = d_vals_row.at[:end].add(
            jnp.einsum(
                "hqk,qhd->khd",
                probs.astype(jnp.bfloat16),
                grad_block,
                preferred_element_type=jnp.float32,
            )
        )
    d_query = rotate(jnp.concatenate(d_query_parts, 0), cosines, -sines).reshape(tokens, 1, local)
    d_keys = rotate(d_keys_row, cosines, -sines).reshape(tokens, 1, local)
    d_vals = d_vals_row.reshape(tokens, 1, local)
    d_z = jnp.concatenate([d_query, d_keys, d_vals, d_pre.reshape(tokens, 4, local)], 1)
    d_z = d_z.astype(jnp.bfloat16).reshape(tokens, 7 * local)
    normed_terms = contract_cols(d_z, in_flat)
    normalized_gradient = lax.psum(normed_terms, "tensor")
    block_input_gradient, vector_gradient = layer_norm_backward(
        normalized_gradient, norm_gain, standardized_input, inverse_deviation, cotangent
    )
    d_bias = jnp.sum(d_z, 0, dtype=jnp.float32).reshape(7, heads_here, HDIM)
    d_w_in = contract_rows(normalized_rows, d_z).reshape(width, 7, local)
    d_w_outs = contract_rows(cotangent, joined).reshape(width, 5, local)
    g_in, g_outs, g_bias, g_vec = (
        lax.psum_scatter(d_w_in, "dp", scatter_dimension=0, tiled=True),
        lax.psum_scatter(d_w_outs, "dp", scatter_dimension=0, tiled=True),
        lax.psum_scatter(d_bias, "dp", scatter_dimension=2, tiled=True),
        lax.psum_scatter(vector_gradient, "dp", scatter_dimension=1, tiled=True),
    )
    local_squares = (
        jnp.sum(g_in * g_in)
        + jnp.sum(g_outs * g_outs)
        + jnp.sum(g_bias * g_bias)
        + jnp.sum(g_vec * g_vec) * (1.0 / tensor_count)
    )
    grad_norm = jnp.sqrt(lax.psum(local_squares, ("dp", "tensor")))
    factor = CLIP_AT / jnp.maximum(grad_norm, CLIP_AT)
    new_in = adamw(w_in, w_in_m, w_in_v, g_in, factor, RATE_MATRIX, DECAY_MATRIX)
    new_outs = adamw(w_outs, w_outs_m, w_outs_v, g_outs, factor, RATE_MATRIX, DECAY_MATRIX)
    new_bias = adamw(in_bias, in_bias_m, in_bias_v, g_bias, factor, RATE_VECTOR, 0.0)
    new_vec = adamw(vectors, vectors_m, vectors_v, g_vec, factor, RATE_VECTOR, 0.0)
    return (
        output,
        block_input_gradient,
        grad_norm,
        new_in[0],
        new_in[1],
        new_in[2],
        new_outs[0],
        new_outs[1],
        new_outs[2],
        new_bias[0],
        new_bias[1],
        new_bias[2],
        new_vec[0],
        new_vec[1],
        new_vec[2],
    )


def solution(mesh):
    placed = (
        P("dp", None),
        P("dp", None),
        P("dp", None),
        P("dp", None, "tensor"),
        P("dp", None, "tensor"),
        P("dp", None, "tensor"),
        P("dp", None, "tensor"),
        P("dp", None, "tensor"),
        P("dp", None, "tensor"),
        P(None, "tensor", "dp"),
        P(None, "tensor", "dp"),
        P(None, "tensor", "dp"),
        P(None, "dp"),
        P(None, "dp"),
        P(None, "dp"),
    )
    return jax.shard_map(
        body,
        mesh=mesh,
        in_specs=placed,
        out_specs=(
            P("dp", None),
            P("dp", None),
            P(),
            P("dp", None, "tensor"),
            P("dp", None, "tensor"),
            P("dp", None, "tensor"),
            P("dp", None, "tensor"),
            P("dp", None, "tensor"),
            P("dp", None, "tensor"),
            P(None, "tensor", "dp"),
            P(None, "tensor", "dp"),
            P(None, "tensor", "dp"),
            P(None, "dp"),
            P(None, "dp"),
            P(None, "dp"),
        ),
        check_vma=False,
    )
```

profile of v0, /device:TPU:0, one launch (start us, length us, event | category | flops | bytes accessed | tf_op | source)
XLA Modules:
  0.0 2521.5 jit_solution(6360360772745429993)
XLA Ops:
  14.7 33.2 %all_gather.14 = bf16[7,8,64]{1,0,2:T(8,128)(2,1)S(1)} all-gather(bf16[7,8,8]{1,0,2:T(8,128)(2,1)S(1)} %copy.119), channel_id=1, replica_groups=mesh['dp'=8,'tensor'=4] {'dp'}, dimensions={2}, use_global_device_ids=true | all-gather | bytes 8064 | tf_op jit(solution)/shard_map/all_gather | solution.py:123
  48.2 30.0 %all_gather.12 = bf16[4,2048]{1,0:T(4,128)(2,1)S(1)} all-gather(bf16[4,256]{1,0:T(4,128)(2,1)S(1)} %convert_element_type.110), channel_id=1, replica_groups=mesh['dp'=8,'tensor'=4] {'dp'}, dimensions={1}, use_global_device_ids=true | all-gather | bytes 18432 | tf_op jit(solution)/shard_map/all_gather | solution.py:124
  97.3 68.9 %all-gather.5.cloned.1.call-done = bf16[2048,5,512]{0,2,1:T(8,128)(2,1)} async-done(((bf16[256,5,512]{0,2,1:T(8,128)(2,1)}), bf16[2048,5,512]{0,2,1:T(8,128)(2,1)}) %all-gather.5.cloned.1.call-update) | async-done | bytes 10485776 | tf_op jit(solution)/shard_map/all_gather | solution.py:122
  166.2 29.2 %fusion.118 = (bf16[2048,2560]{1,0:T(8,128)(2,1)S(1)}, f32[2048,2560]{1,0:T(8,128)}) fusion(bf16[2048,2048]{1,0:T(8,128)(2,1)} %param.36, bf16[2048,2560]{0,1:T(8,128)(2,1)} %bitcast.205), kind=kOutput, calls=%fused_computation.205 | convolution fusion | flops 21480079360 | bytes 50331648 | tf_op jit(solution)/shard_map/dot_general | solution.py:188
  199.6 169.6 %all-gather.3.cloned.1.call-done = bf16[2048,7,512]{2,0,1:T(8,128)(2,1)} async-done(((bf16[256,7,512]{2,0,1:T(8,128)(2,1)}), bf16[2048,7,512]{2,0,1:T(8,128)(2,1)}) %all-gather.3.cloned.1.call-update) | async-done | bytes 14680080 | tf_op jit(solution)/shard_map/all_gather | solution.py:121
  369.2 19.2 copy.118
  388.4 40.5 %convolution_add_fusion = f32[2048,3584]{1,0:T(8,128)} fusion(bf16[2048,3584]{0,1:T(8,128)(2,1)} %bitcast.159, f32[3584]{0:T(1024)S(1)} %reshape.759, bf16[2048,2048]{1,0:T(8,128)(2,1)} %param.35, f32[2048]{0:T(1024)S(1)} %bitcast.202, f32[2048]{0:T(1024)S(1)} %bitcast.188, f32[2048]{0:T(1024)S(1)} %add_rsqrt_fusion, f32[2048]{0:T(1024)S(1)} %broadcast_multiply_fusion.2), kind=kOutput, calls=%fused_computation.27 | convolution fusion | flops 30097276928 | bytes 52475904 | tf_op jit(solution)/shard_map/dot_general | solution.py:143
  428.9 30.2 %copy.121 = f32[2048,3584]{0,1:T(8,128)} copy(f32[2048,3584]{1,0:T(8,128)} %convolution_add_fusion) | data formatting | bytes 58720256 | tf_op jit(solution)/shard_map/add | solution.py:143
  463.4 19.7 convert.47
  521.3 17.7 copy.145
  583.2 15.1 fusion.22
  649.8 15.5 multiply_reduce_fusion.1
  681.2 16.1 multiply_convert_fusion.2
  712.7 14.9 multiply_convert_fusion.1
  743.6 15.4 fusion
  759.0 15.3 exponential_reduce_fusion
  774.4 15.2 fusion.75
  789.6 25.2 multiply_reduce_fusion
  814.8 16.6 bitcast_add_fusion
  838.2 27.9 %multiply_convert_fusion = bf16[8,512,2048]{2,1,0:T(8,128)(2,1)} fusion(f32[8,512,2048]{2,1,0:T(8,128)} %get-tuple-element.196, f32[8,512,2048]{2,1,0:T(8,128)} %get-tuple-element.180, f32[8,512]{1,0:T(8,128)S(1)} %get-tuple-element.195, f32[8,512]{1,0:T(8,128)S(1)} %log_add_fusion, pred[512,2048]{1,0:T(8,128)(4,1)S(1)} %copy-done.5), kind=kLoop, calls=%fused_computation | loop fusion | flops 50331648 | bytes 84967424 | tf_op jit(solution)/shard_map/convert_element_type | solution.py:216
  898.3 29.3 %fusion.32 = f32[2048,2048]{1,0:T(8,128)} fusion(bf16[2048,2560]{0,1:T(8,128)(2,1)} %bitcast.206, bf16[2048,2048]{1,0:T(8,128)(2,1)} %multiply_convert_fusion.3, bf16[2048,512]{1,0:T(8,128)(2,1)} %copy.124), kind=kOutput, calls=%fused_computation.67 | convolution fusion | flops 21495808000 | bytes 37748736 | tf_op jit(solution)/shard_map/dot_general | solution.py:74
  939.4 38.3 %convolution_bitcast_fusion = f32[2048,2048]{1,0:T(8,128)} fusion(bf16[2048,7,512]{2,0,1:T(8,128)(2,1)} %get-tuple-element.146, bf16[2048,7,512]{2,0,1:T(8,128)(2,1)} %all-gather.3.cloned.1.call-done), kind=kOutput, calls=%fused_computation.59 | convolution fusion | flops 30064771072 | bytes 46137344 | tf_op jit(solution)/shard_map/dot_general | solution.py:74
  977.8 557.3 %all-reduce.6.cloned.1.call-done = (f32[2048,2048]{1,0:T(8,128)}, f32[2048,2048]{1,0:T(8,128)}) async-done(((f32[2048,2048]{1,0:T(8,128)}, f32[2048,2048]{1,0:T(8,128)}), (f32[2048,2048]{1,0:T(8,128)}, f32[2048,2048]{1,0:T(8,128)})) %all-reduce.6.cloned.1.call-update) | async-done | bytes 33554448 | tf_op jit(solution)/shard_map/psum | solution.py:186
  1548.3 21.6 convert_reduce_fusion.2
  1571.3 29.3 %fusion.31 = f32[2560,2048]{1,0:T(8,128)} fusion(bf16[2048,2048]{1,0:T(8,128)(2,1)} %param.36, bf16[2048,2048]{1,0:T(8,128)(2,1)} %multiply_convert_fusion.3, bf16[2048,512]{1,0:T(8,128)(2,1)} %copy.124), kind=kOutput, calls=%fused_computation.66 | convolution fusion | flops 21495808000 | bytes 39845888 | tf_op jit(solution)/shard_map/dot_general | solution.py:68
  1600.6 20.8 copy.139
  1621.5 19.5 copy.137
  1641.0 42.8 %fusion.26 = f32[2048,7,512]{2,0,1:T(8,128)} fusion(bf16[2048,7,512]{0,2,1:T(8,128)(2,1)} %copy.137, bf16[2048,2048]{1,0:T(8,128)(2,1)} %param.35, f32[2048]{0:T(1024)S(1)} %bitcast.203, f32[2048]{0:T(1024)S(1)} %bitcast.191, f32[2048]{0:T(1024)S(1)} %copy-done.48, f32[2048]{0:T(1024)S(1)} %copy-done.44), kind=kOutput, calls=%fused_computation.54 | convolution fusion | flops 30089936896 | bytes 52461568 | tf_op jit(solution)/shard_map/dot_general | solution.py:68
  1685.8 38.8 %all-reduce.2 = f32[7,8,64]{2,1,0:T(8,128)S(1)} all-reduce(f32[7,8,64]{2,1,0:T(8,128)S(1)} %reshape.756), channel_id=4, replica_groups=mesh['dp'=8,'tensor'=4] {'dp'}, use_global_device_ids=true, to_apply=%region_25.26.clone | all-reduce | flops 3584 | bytes 28672
  1727.5 254.4 %reduce-scatter.9.cloned.1.call-done = f32[256,5,512]{2,0,1:T(8,128)} async-done(((f32[2048,5,512]{2,0,1:T(8,128)}), f32[256,5,512]{2,0,1:T(8,128)}) %reduce-scatter.9.cloned.1.call-update) | async-done | bytes 2621456 | tf_op jit(solution)/shard_map/reduce_scatter | solution.py:248
  1984.9 464.8 %reduce-scatter.7.cloned.1.call-done = f32[256,7,512]{2,0,1:T(8,128)} async-done(((f32[2048,7,512]{2,0,1:T(8,128)}), f32[256,7,512]{2,0,1:T(8,128)}) %reduce-scatter.7.cloned.1.call-update) | async-done | bytes 3670032 | tf_op jit(solution)/shard_map/reduce_scatter | solution.py:247
  2455.2 39.7 %psum.23 = f32[]{:T(128)} all-reduce(f32[]{:T(128)S(6)} %add.331), channel_id=1, replica_groups=mesh['dp'=8,'tensor'=4] {'dp','tensor'}, use_global_device_ids=true, to_apply=%region_32.33 | all-reduce | flops 1 | bytes 8 | tf_op jit(solution)/shard_map/psum | solution.py:258
  (295 shorter events, 308.5 us)
Async XLA Ops:
  7.2 159.0 %all-gather.5.cloned.1.call-start = ((), (), s32[]{:S(2)}) async-start(), calls=%async_computation.4 | async-start | bytes 11796480 | tf_op jit(solution)/shard_map/all_gather | solution.py:122
  10.1 359.1 %all-gather.3.cloned.1.call-start = ((), (), s32[]{:S(2)}) async-start(), calls=%async_computation.3 | async-start | bytes 16515072 | tf_op jit(solution)/shard_map/all_gather | solution.py:121
  13.7 1521.5 %all-reduce.6.cloned.1.call-start = ((), (), s32[]{:S(2)}) async-start(), calls=%async_computation.8 | async-start | bytes 67108864 | tf_op jit(solution)/shard_map/psum | solution.py:186
  83.2 305.2 %copy-start.43 = (f32[2048]{0:T(1024)}, f32[2048]{0:T(1024)S(1)}, u32[]{:S(2)}) copy-start(f32[2048]{0:T(1024)S(1)} %broadcast_multiply_fusion.2) | copy-start | bytes 24580
  89.1 299.3 %copy-start.47 = (f32[2048]{0:T(1024)}, f32[2048]{0:T(1024)S(1)}, u32[]{:S(2)}) copy-start(f32[2048]{0:T(1024)S(1)} %add_rsqrt_fusion) | copy-start | bytes 24580
  92.1 296.3 %copy-start.49 = (f32[1,2048]{1,0:T(1,128)}, f32[1,2048]{1,0:T(1,128)S(1)}, u32[]{:S(2)}) copy-start(f32[1,2048]{1,0:T(1,128)S(1)} %get-tuple-element.171) | copy-start | bytes 24580
  92.1 296.3 %copy-start.59 = (f32[1,2048]{1,0:T(1,128)}, f32[1,2048]{1,0:T(1,128)S(1)}, u32[]{:S(2)}) copy-start(f32[1,2048]{1,0:T(1,128)S(1)} %get-tuple-element.170) | copy-start | bytes 24580
  501.6 57.5 %copy-start.3 = (bf16[2048,8,64]{0,2,1:T(8,128)(2,1)}, bf16[2048,8,64]{0,2,1:T(8,128)(2,1)S(1)}, u32[]{:S(2)}) copy-start(bf16[2048,8,64]{0,2,1:T(8,128)(2,1)S(1)} %get-tuple-element.198) | copy-start | bytes 6291460
  559.2 46.8 %copy-start.41 = (f32[8,512]{1,0:T(8,128)}, f32[8,512]{1,0:T(8,128)S(1)}, u32[]{:S(2)}) copy-start(f32[8,512]{1,0:T(8,128)S(1)} %log_add_fusion.2) | copy-start | bytes 49156
  606.0 24.6 slice-start.7
  681.2 31.5 %slice-start = ((s8[25165824]{0:T(1024)(128)(4,1)}), s8[4194304]{0:T(1024)(128)(4,1)S(1)}, s32[]{:S(2)}) async-start(s8[25165824]{0:T(1024)(128)(4,1)} %bitcast.144), calls=%async_computation.9 | async-start | bytes 8388608
  681.2 31.5 %slice-start.1 = ((s8[25165824]{0:T(1024)(128)(4,1)}), s8[4194304]{0:T(1024)(128)(4,1)S(1)}, s32[]{:S(2)}) async-start(s8[25165824]{0:T(1024)(128)(4,1)} %bitcast.144), calls=%async_computation.10 | async-start | bytes 8388608
  681.2 31.5 %slice-start.2 = ((s8[25165824]{0:T(1024)(128)(4,1)}), s8[4194304]{0:T(1024)(128)(4,1)S(1)}, s32[]{:S(2)}) async-start(s8[25165824]{0:T(1024)(128)(4,1)} %bitcast.144), calls=%async_computation.11 | async-start | bytes 8388608
  681.2 31.5 %slice-start.3 = ((s8[25165824]{0:T(1024)(128)(4,1)}), s8[4194304]{0:T(1024)(128)(4,1)S(1)}, s32[]{:S(2)}) async-start(s8[25165824]{0:T(1024)(128)(4,1)} %bitcast.144), calls=%async_computation.12 | async-start | bytes 8388608
  838.2 27.9 %copy-start.9 = (bf16[2048,8,32]{0,2,1:T(8,128)(2,1)S(1)}, bf16[2048,8,32]{0,2,1:T(8,128)(2,1)}, u32[]{:S(2)}) copy-start(bf16[2048,8,32]{0,2,1:T(8,128)(2,1)} %copy-done.8) | copy-start | bytes 3145732
  838.2 27.9 %copy-start.20 = (bf16[2048,8,16]{0,2,1:T(8,128)(2,1)S(1)}, bf16[2048,8,16]{0,2,1:T(8,128)(2,1)}, u32[]{:S(2)}) copy-start(bf16[2048,8,16]{0,2,1:T(8,128)(2,1)} %copy-done.19) | copy-start | bytes 1572868
  838.2 27.9 %copy-start.22 = (bf16[2048,8,16]{0,2,1:T(8,128)(2,1)S(1)}, bf16[2048,8,16]{0,2,1:T(8,128)(2,1)}, u32[]{:S(2)}) copy-start(bf16[2048,8,16]{0,2,1:T(8,128)(2,1)} %copy-done.21) | copy-start | bytes 1572868
  898.3 29.3 %copy-start.24 = (bf16[2048,1,512]{2,0,1:T(8,128)(2,1)S(1)}, bf16[2048,1,512]{2,0,1:T(8,128)(2,1)}, u32[]{:S(2)}) copy-start(bf16[2048,1,512]{2,0,1:T(8,128)(2,1)} %copy.135) | copy-start | bytes 6291460
  898.3 29.3 %copy-start.25 = (bf16[2048,1,512]{2,0,1:T(8,128)(2,1)S(1)}, bf16[2048,1,512]{2,0,1:T(8,128)(2,1)}, u32[]{:S(2)}) copy-start(bf16[2048,1,512]{2,0,1:T(8,128)(2,1)} %copy.134) | copy-start | bytes 6291460
  977.8 557.4 %copy-start.44 = (f32[2048]{0:T(1024)S(1)}, f32[2048]{0:T(1024)}, u32[]{:S(2)}) copy-start(f32[2048]{0:T(1024)} %copy-done.43) | copy-start | bytes 24580
  977.8 557.4 %copy-start.48 = (f32[2048]{0:T(1024)S(1)}, f32[2048]{0:T(1024)}, u32[]{:S(2)}) copy-start(f32[2048]{0:T(1024)} %copy-done.47) | copy-start | bytes 24580
  977.8 557.4 %copy-start.50 = (f32[1,2048]{1,0:T(1,128)S(1)}, f32[1,2048]{1,0:T(1,128)}, u32[]{:S(2)}) copy-start(f32[1,2048]{1,0:T(1,128)} %copy-done.49) | copy-start | bytes 24580
  977.8 747.5 %reduce-scatter.11.cloned.1.call-start = ((), (), s32[]{:S(2)}) async-start(), calls=%async_computation.7 | async-start | bytes 1179648
  1571.3 410.6 %reduce-scatter.9.cloned.1.call-start = ((), (), s32[]{:S(2)}) async-start(), calls=%async_computation.6 | async-start | bytes 23592960 | tf_op jit(solution)/shard_map/reduce_scatter | solution.py:248
  1621.5 828.3 %reduce-scatter.7.cloned.1.call-start = ((), (), s32[]{:S(2)}) async-start(), calls=%async_computation.5 | async-start | bytes 33030144 | tf_op jit(solution)/shard_map/reduce_scatter | solution.py:247
  1683.8 811.8 %copy-start.58 = (f32[4,256]{1,0:T(4,128)S(1)}, f32[4,256]{1,0:T(4,128)}, u32[]{:S(2)}) copy-start(f32[4,256]{1,0:T(4,128)} %param.47) | copy-start | bytes 12292
  1683.8 811.8 %copy-start.61 = (f32[4,256]{1,0:T(4,128)S(1)}, f32[4,256]{1,0:T(4,128)}, u32[]{:S(2)}) copy-start(f32[4,256]{1,0:T(4,128)} %param.48) | copy-start | bytes 12292
  1683.9 811.8 %copy-start.62 = (f32[4,256]{1,0:T(4,128)S(1)}, f32[4,256]{1,0:T(4,128)}, u32[]{:S(2)}) copy-start(f32[4,256]{1,0:T(4,128)} %param.49) | copy-start | bytes 12292
  1683.9 812.4 %copy-start.46 = (f32[7,8,8]{2,1,0:T(8,128)S(1)}, f32[7,8,8]{2,1,0:T(8,128)}, u32[]{:S(2)}) copy-start(f32[7,8,8]{2,1,0:T(8,128)} %param.44) | copy-start | bytes 5380
  1683.9 812.4 %copy-start.55 = (f32[7,8,8]{2,1,0:T(8,128)S(1)}, f32[7,8,8]{2,1,0:T(8,128)}, u32[]{:S(2)}) copy-start(f32[7,8,8]{2,1,0:T(8,128)} %param.45) | copy-start | bytes 5380
  1683.9 812.4 %copy-start.56 = (f32[7,8,8]{2,1,0:T(8,128)S(1)}, f32[7,8,8]{2,1,0:T(8,128)}, u32[]{:S(2)}) copy-start(f32[7,8,8]{2,1,0:T(8,128)} %param.46) | copy-start | bytes 5380
  1683.9 813.1 %copy-start.15 = (f32[256,5,512]{2,0,1:T(8,128)S(1)}, f32[256,5,512]{2,0,1:T(8,128)}, u32[]{:S(2)}) copy-start(f32[256,5,512]{2,0,1:T(8,128)} %param.41) | copy-start | bytes 7864324
  (60 other events, 732.1 us)
Sparse Core Ops, SparseCore 0:
  10.7 155.4 all-gather.4
  168.9 200.1 all-gather.2
  977.9 557.2 all-reduce.5
  1571.4 63.4 reduce-scatter.10
  1638.7 343.1 reduce-scatter.8
  1985.7 463.9 reduce-scatter.6
where the time goes:
time: 2530 us; the launch traced here: 2520 us
  waiting for transfers between devices  1520 us (60%)
  matrix products  431 us (17%)
  other arithmetic  243 us (10%)
  local copies, waits for them, and re-layouts  170 us (7%)
  blocking collectives  142 us (6%)
    psum x1, waiting for transfers between devices, body(): summed = lax.psum(partial_sum, 'tensor')  557 us
    reduce_scatter x1, waiting for transfers between devices, body(): lax.psum_scatter(d_w_in, 'dp', scatter_dimension=0, tiled=True)  465 us
    reduce_scatter x1, waiting for transfers between devices, body(): lax.psum_scatter(d_w_outs, 'dp', scatter_dimension=0, tiled=True)  254 us
    all_gather x1, waiting for transfers between devices, body(): lax.all_gather(w_in.astype(jnp.bfloat16), 'dp', axis=0, tiled=True)  170 us
    dot_general x2, matrix products, contract_rows(): lax.dot_general(left, right, (((0,), (0,)), ((), ())), preferred_element_...  72.1 us
    all_gather x1, waiting for transfers between devices, body(): lax.all_gather(w_outs.astype(jnp.bfloat16), 'dp', axis=0, tiled=True)  68.9 us
    dot_general x2, matrix products, contract_cols(): lax.dot_general(left, right, (((1,), (1,)), ((), ())), preferred_element_...  67.6 us
    convert_element_type x4, other arithmetic, body(): d_scores = (probs * (d_probs - delta)).astype(jnp.bfloat16)  61.7 us
  transfers between devices with their start and end apart: 6, of which 5 were waited for; matrix products, arithmetic and copies ran while one was open for 7% of the time, Pallas kernels for 0%

commit v1 on v0

v1 whole, which is shorter than its diff:
```python
from functools import partial

import jax
import jax.numpy as jnp
from jax import lax
from jax.experimental import pallas as pl
from jax.experimental.pallas import tpu as pltpu
from jax.sharding import PartitionSpec as P

HDIM = 64
ROT = 32
STEP = 10

BETA_ONE = 0.9
BETA_TWO = 0.95
EPSILON = 1e-08
CLIP_AT = 1.0
RATE_MATRIX = 0.06
RATE_VECTOR = 0.6
DECAY_MATRIX = 0.1

F32 = jnp.float32
BF16 = jnp.bfloat16
LANES = 128
ANY = pl.BlockSpec(memory_space=pl.ANY)
VMEM_LIMIT = 60 * 1024 * 1024


def nn(a, b):
    return lax.dot_general(a, b, (((1,), (0,)), ((), ())), preferred_element_type=F32)


def nt(a, b):
    return lax.dot_general(a, b, (((1,), (1,)), ((), ())), preferred_element_type=F32)


def whole(*shape):
    return pl.BlockSpec(shape, lambda *_: (0,) * len(shape))


def launch(kernel, grid, in_specs, out_specs, out_shape, args, *, scalars=(), scratch=(), flops=0, moved=0, aliases={}):
    return pl.pallas_call(
        kernel,
        grid_spec=pltpu.PrefetchScalarGridSpec(
            num_scalar_prefetch=len(scalars),
            grid=grid,
            in_specs=in_specs,
            out_specs=out_specs,
            scratch_shapes=list(scratch),
        ),
        out_shape=out_shape,
        input_output_aliases=aliases,
        compiler_params=pltpu.CompilerParams(vmem_limit_bytes=VMEM_LIMIT),
        cost_estimate=pl.CostEstimate(flops=int(flops), bytes_accessed=int(moved), transcendentals=0),
    )(*scalars, *args)


def adamw(weight, first, second, grad, factor, rate, decay):
    clipped = grad * factor
    first = BETA_ONE * first + (1.0 - BETA_ONE) * clipped
    second = BETA_TWO * second + (1.0 - BETA_TWO) * clipped * clipped
    first_hat = first / (1.0 - BETA_ONE**STEP)
    second_hat = second / (1.0 - BETA_TWO**STEP)
    weight = weight - rate * (first_hat / (jnp.sqrt(second_hat) + EPSILON) + decay * weight)
    return (weight, first, second)


def load_weights(order_ref, blocks, slots, store, sem, rows, local):
    copies = []
    for r, refs in enumerate(blocks):
        at = pl.ds(pl.multiple_of(order_ref[r] * rows, rows), rows)
        for column, (group, slot) in enumerate(slots):
            copies.append(
                pltpu.make_async_copy(
                    refs[group].at[slot], store.at[at, column * local : (column + 1) * local], sem
                )
            )
    for copy in copies:
        copy.start()
    for copy in copies:
        copy.wait()


def turn(values, table, sign):
    return (
        values * table[0]
        + sign * (pltpu.roll(values, LANES - ROT // 2, 1) * table[1])
        + sign * (pltpu.roll(values, ROT // 2, 1) * table[2])
    )


def cast_group(w_in, w_outs, slots, deps):
    _, rows, local = w_in.shape

    def kernel(*refs):
        ins, out = refs[: len(slots)], refs[-1]
        for i, ref in enumerate(ins):
            out[i] = ref[0].astype(BF16)

    specs = [
        pl.BlockSpec((1, rows, local), lambda i, s=slot: (s, 0, 0)) for _, slot in slots
    ]
    args = [w_in if which == 0 else w_outs for which, _ in slots]
    n = len(slots)
    return launch(
        kernel,
        (1,),
        specs + [ANY] * len(deps),
        whole(n, rows, local),
        jax.ShapeDtypeStruct((n, rows, local), BF16),
        args + list(deps),
        moved=n * rows * local * 6,
    )


def norm_kernel(x_ref, g_ref, vec_ref, normed_ref, normed_t_ref, g_t_ref):
    x = x_ref[...].astype(F32)
    mean = jnp.mean(x, -1, keepdims=True)
    centered = x - mean
    var = jnp.mean(centered * centered, -1, keepdims=True)
    hat = centered * lax.rsqrt(var + 1e-05)
    normed = (hat * vec_ref[0:1, :] + vec_ref[1:2, :]).astype(BF16)
    normed_ref[...] = normed
    normed_t_ref[...] = normed.T
    g_t_ref[...] = g_ref[...].T


def normalize(x, g, vec):
    tokens, width = x.shape
    tile = min(256, tokens)
    row = pl.BlockSpec((tile, width), lambda i: (i, 0))
    col = pl.BlockSpec((width, tile), lambda i: (0, i))
    shape = jax.ShapeDtypeStruct((tokens, width), BF16)
    shape_t = jax.ShapeDtypeStruct((width, tokens), BF16)
    return launch(
        norm_kernel,
        (tokens // tile,),
        [row, row, whole(4, width)],
        (row, col, col),
        (shape, shape_t, shape_t),
        (x, g, vec),
        flops=tokens * width * 10,
        moved=tokens * width * 10,
    )


def qkv_project(order, normed, g, bias, tables, blocks):
    tokens, width = normed.shape
    n_blocks = len(blocks)
    _, rows, local = blocks[0].shape
    tile = min(512, tokens)

    def kernel(order_ref, x_ref, g_ref, bias_ref, table_ref, *rest):
        refs = rest[:n_blocks]
        q_ref, k_ref, v_ref, da_ref, store, sem = rest[n_blocks:]

        @pl.when(pl.program_id(0) == 0)
        def _():
            load_weights(order_ref, [[r] for r in refs], [(0, s) for s in range(4)], store, sem, rows, local)

        x = x_ref[...]
        for slot, out in ((0, q_ref), (1, k_ref)):
            z = nn(x, store[:, slot * local : (slot + 1) * local]) + bias_ref[slot : slot + 1, :]
            for pair in range(local // LANES):
                at = slice(pair * LANES, (pair + 1) * LANES)
                out[:, at] = turn(z[:, at], table_ref, 1.0).astype(BF16)
        v_ref[...] = (nn(x, store[:, 2 * local : 3 * local]) + bias_ref[2:3, :]).astype(BF16)
        da_ref[...] = nn(g_ref[...], store[:, 3 * local : 4 * local]).astype(BF16)

    row = pl.BlockSpec((tile, width), lambda i, *_: (i, 0))
    out = pl.BlockSpec((tile, local), lambda i, *_: (i, 0))
    shape = jax.ShapeDtypeStruct((tokens, local), BF16)
    return launch(
        kernel,
        (tokens // tile,),
        [row, row, whole(7, local), pl.BlockSpec((3, tile, LANES), lambda i, *_: (0, i, 0))] + [ANY] * n_blocks,
        (out,) * 4,
        (shape,) * 4,
        (normed, g, bias, tables, *blocks),
        scalars=(order,),
        scratch=(pltpu.VMEM((width, 4 * local), BF16), pltpu.SemaphoreType.DMA),
        flops=2 * tokens * width * 4 * local,
        moved=tokens * width * 4 + width * local * 8,
    )


def attend(low, query, keys, vals, d_attn, start, tables):
    tokens, local = query.shape
    block = min(256, tokens)
    count = tokens // block
    pairs = local // LANES
    scale = HDIM ** (-0.5)

    def kernel(low_ref, q_ref, k_ref, v_ref, do_ref, start_ref, table_ref, o_ref, dq_ref, dk_ref, dv_ref, db_ref,
               k_half, v_half, k_t, v_t, s_buf, dp_buf, o_t, dq_t, dk_sum, dv_sum):
        i = pl.program_id(1)
        first_lanes = lax.broadcasted_iota(jnp.int32, (1, LANES), 1) < HDIM

        @pl.when(i == 0)
        def _():
            zero = jnp.zeros((), BF16)
            for b in range(count):
                at = slice(b * block, (b + 1) * block)
                for source, half, flipped in ((k_ref, k_half, k_t), (v_ref, v_half, v_t)):
                    part = source[at, :]
                    half[0, at, :] = jnp.where(first_lanes, part, zero)
                    half[1, at, :] = jnp.where(first_lanes, zero, part)
                    flipped[b] = part.T
            dk_sum[...] = jnp.zeros_like(dk_sum)
            dv_sum[...] = jnp.zeros_like(dv_sum)
            db_ref[...] = jnp.zeros_like(db_ref)

        q = q_ref[...]
        do = do_ref[...]
        zero = jnp.zeros((), BF16)
        q_cat = jnp.concatenate([jnp.where(first_lanes, q, zero), jnp.where(first_lanes, zero, q)], 0)
        do_cat = jnp.concatenate([jnp.where(first_lanes, do, zero), jnp.where(first_lanes, zero, do)], 0)
        t_place = i * block + lax.broadcasted_iota(jnp.int32, (1, block), 1)
        t_start = start_ref[...]
        low_block = low_ref[i]
        o_t[...] = jnp.zeros_like(o_t)
        dq_t[...] = jnp.zeros_like(dq_t)

        def score(b, tops):
            at = pl.ds(pl.multiple_of(b * block, block), block)
            u_place = b * block + lax.broadcasted_iota(jnp.int32, (block, 1), 0)
            allowed = (u_place >= t_start) & (u_place <= t_place)
            new = []
            for h in range(2):
                s = jnp.where(allowed, nt(k_half[h, at, :], q) * scale, -1e30)
                s_buf[h, b] = s
                new.append(jnp.maximum(tops[h], jnp.max(s, 0, keepdims=True)))
            return tuple(new)

        lowest = jnp.full((1, block), -jnp.inf, F32)
        tops = lax.fori_loop(low_block, i + 1, score, (lowest, lowest))

        def weigh(b, sums):
            at = pl.ds(pl.multiple_of(b * block, block), block)
            new = []
            for h in range(2):
                p = jnp.exp(s_buf[h, b] - tops[h])
                dp = nt(v_half[h, at, :], do)
                s_buf[h, b] = p
                dp_buf[h, b] = dp
                new.append(sums[2 * h] + jnp.sum(p, 0, keepdims=True))
                new.append(sums[2 * h + 1] + jnp.sum(p * dp, 0, keepdims=True))
            return tuple(new)

        none = jnp.zeros((1, block), F32)
        sums = lax.fori_loop(low_block, i + 1, weigh, (none,) * 4)
        inverse = [1.0 / sums[0], 1.0 / sums[2]]
        delta = [sums[1] * inverse[0], sums[3] * inverse[1]]

        def spread(b, carry):
            at = pl.ds(pl.multiple_of(b * block, block), block)
            probs, grads = [], []
            for h in range(2):
                rows = slice(h * HDIM, (h + 1) * HDIM)
                p = s_buf[h, b] * inverse[h]
                ds = (p * (dp_buf[h, b] - delta[h])).astype(BF16)
                p = p.astype(BF16)
                o_t[rows, :] += nn(v_t[b, rows, :], p)
                dq_t[rows, :] += nn(k_t[b, rows, :], ds)
                probs.append(p)
                grads.append(ds)
            dv_sum[at, :] += nn(jnp.concatenate(probs, 1), do_cat)
            dk_sum[at, :] += nn(jnp.concatenate(grads, 1), q_cat)
            return carry

        lax.fori_loop(low_block, i + 1, spread, 0)
        o_ref[...] = o_t[...].T.astype(BF16)
        here = pl.ds(pl.multiple_of(i * block, block), block)
        dq = turn(dq_t[...].T * scale, [table_ref[n, here, :] for n in range(3)], -1.0).astype(BF16)
        dq_ref[...] = dq
        db_ref[0:1, :] += jnp.sum(dq.astype(F32), 0, keepdims=True)

        @pl.when(i == count - 1)
        def _():
            dk = turn(dk_sum[...] * scale, table_ref, -1.0).astype(BF16)
            dv = dv_sum[...].astype(BF16)
            dk_ref[...] = dk
            dv_ref[...] = dv
            db_ref[1:2, :] = jnp.sum(dk.astype(F32), 0, keepdims=True)
            db_ref[2:3, :] = jnp.sum(dv.astype(F32), 0, keepdims=True)

    part = pl.BlockSpec((block, LANES), lambda p, i, *_: (i, p))
    column = pl.BlockSpec((tokens, LANES), lambda p, i, *_: (0, p))
    shape = jax.ShapeDtypeStruct((tokens, local), BF16)
    return launch(
        kernel,
        (pairs, count),
        [
            part,
            column,
            column,
            part,
            pl.BlockSpec((1, block), lambda p, i, *_: (0, i)),
            whole(3, tokens, LANES),
        ],
        (part, part, column, column, pl.BlockSpec((3, LANES), lambda p, i, *_: (0, p))),
        (shape,) * 4 + (jax.ShapeDtypeStruct((3, local), F32),),
        (query, keys, vals, d_attn, start, tables),
        scalars=(low,),
        scratch=(
            pltpu.VMEM((2, tokens, LANES), BF16),
            pltpu.VMEM((2, tokens, LANES), BF16),
            pltpu.VMEM((count, LANES, block), BF16),
            pltpu.VMEM((count, LANES, block), BF16),
            pltpu.VMEM((2, count, block, block), F32),
            pltpu.VMEM((2, count, block, block), F32),
            pltpu.VMEM((LANES, block), F32),
            pltpu.VMEM((LANES, block), F32),
            pltpu.VMEM((tokens, LANES), F32),
            pltpu.VMEM((tokens, LANES), F32),
        ),
        flops=tokens * tokens * local * 24,
        moved=tokens * local * 20,
    )


def hidden_slot(order, normed, g, bias, blocks):
    tokens, width = normed.shape
    n_blocks = len(blocks)
    _, rows, local = blocks[0].shape
    tile = min(512, tokens)

    def kernel(order_ref, x_ref, g_ref, bias_ref, *rest):
        refs = rest[:n_blocks]
        h_ref, dz_ref, db_ref, store, sem = rest[n_blocks:]

        @pl.when(pl.program_id(0) == 0)
        def _():
            load_weights(order_ref, [[r] for r in refs], [(0, 0), (0, 1)], store, sem, rows, local)
            db_ref[...] = jnp.zeros_like(db_ref)

        v = nn(x_ref[...], store[:, :local]) + bias_ref[...]
        dh = nn(g_ref[...], store[:, local:])
        square = v * v
        t = jnp.tanh(0.7978845608 * (v + 0.044715 * (square * v)))
        half = 0.5 * (1.0 + t)
        h_ref[...] = (v * half).astype(BF16)
        slope = half + (0.5 * v) * (1.0 - t * t) * (0.7978845608 + (3.0 * 0.044715 * 0.7978845608) * square)
        dz = (dh * slope).astype(BF16)
        dz_ref[...] = dz
        db_ref[...] += jnp.sum(dz.astype(F32), 0, keepdims=True)

    row = pl.BlockSpec((tile, width), lambda i, *_: (i, 0))
    out = pl.BlockSpec((tile, local), lambda i, *_: (i, 0))
    shape = jax.ShapeDtypeStruct((tokens, local), BF16)
    return launch(
        kernel,
        (tokens // tile,),
        [row, row, whole(1, local)] + [ANY] * n_blocks,
        (out, out, whole(1, local)),
        (shape, shape, jax.ShapeDtypeStruct((1, local), F32)),
        (normed, g, bias, *blocks),
        scalars=(order,),
        scratch=(pltpu.VMEM((width, 2 * local), BF16), pltpu.SemaphoreType.DMA),
        flops=4 * tokens * width * local,
        moved=tokens * width * 4 + width * local * 4,
    )


def grad_blocks(dest, normed_t, g_t, sides, received, split):
    width, tokens = normed_t.shape
    count = dest.shape[0]
    n = len(sides)
    local = sides[0][1].shape[1]
    rows = width // (lax.axis_size("dp"))

    def kernel(dest_ref, x_ref, g_ref, *rest):
        rights = rest[:n]
        adds = rest[n : n + len(received)]
        outs = rest[n + len(received) :]
        step = pl.program_id(0)
        for i, (left, _) in enumerate(sides):
            total = nn((x_ref if left == 0 else g_ref)[...], rights[i][...])
            for add in adds:
                total += add[0, i].astype(F32)
            if not split:
                outs[0][0, i] = total.astype(BF16)
            else:
                for j, out in enumerate(outs):

                    @pl.when(step == j)
                    def _(out=out, total=total, i=i):
                        out[i] = total.astype(out.dtype)

    left = pl.BlockSpec((rows, tokens), lambda i, dest_ref: (dest_ref[i], 0))
    piece = pl.BlockSpec((1, n, rows, local), lambda i, *_: (i, 0, 0, 0))
    if split:
        out_specs = (whole(n, rows, local),) * count
        out_shape = tuple(
            jax.ShapeDtypeStruct((n, rows, local), F32 if j == 0 else BF16) for j in range(count)
        )
    else:
        out_specs = piece
        out_shape = jax.ShapeDtypeStruct((count, n, rows, local), BF16)
    return launch(
        kernel,
        (count,),
        [left, left] + [whole(tokens, local)] * n + [piece] * len(received),
        out_specs,
        out_shape,
        (normed_t, g_t, *[right for _, right in sides], *received),
        scalars=(dest,),
        flops=2 * count * rows * tokens * n * local,
        moved=count * rows * tokens * 4 + n * tokens * local * 2 + count * n * rows * local * 2,
    )


def project_back(order, shares, lefts, groups, slots, received, split):
    tokens, local = lefts[0].shape
    count = shares.shape[0]
    share = tokens // lax.axis_size("tensor")
    tile = min(256, share)
    steps = share // tile
    n_blocks = len(groups)
    n_groups = len(groups[0])
    rows = groups[0][0].shape[1]
    width = rows * n_blocks
    m = len(lefts)
    flat = [ref for refs in groups for ref in refs]

    def kernel(order_ref, shares_ref, *rest):
        left_refs = rest[:m]
        refs = rest[m : m + len(flat)]
        adds = rest[m + len(flat) : m + len(flat) + len(received)]
        outs = rest[m + len(flat) + len(received) : -2]
        store, sem = rest[-2:]
        step, part = pl.program_id(0), pl.program_id(1)

        @pl.when((step == 0) & (part == 0))
        def _():
            nested = [refs[r * n_groups : (r + 1) * n_groups] for r in range(n_blocks)]
            load_weights(order_ref, nested, slots, store, sem, rows, local)

        total = nt(jnp.concatenate([left[...] for left in left_refs], 1), store[...])
        for add in adds:
            total += add[...].astype(F32)
        if not split:
            outs[0][...] = total.astype(BF16)
        else:
            at = pl.ds(pl.multiple_of(part * tile, tile), tile)
            for j, out in enumerate(outs):

                @pl.when(step == j)
                def _(out=out):
                    out[at, :] = total.astype(out.dtype)

    left = pl.BlockSpec((tile, local), lambda i, j, o_ref, s_ref: (s_ref[i] * steps + j, 0))
    piece = pl.BlockSpec((tile, width), lambda i, j, *_: (i * steps + j, 0))
    if split:
        out_specs = (whole(share, width),) * count
        out_shape = tuple(jax.ShapeDtypeStruct((share, width), F32 if j == 0 else BF16) for j in range(count))
    else:
        out_specs = piece
        out_shape = jax.ShapeDtypeStruct((count * share, width), BF16)
    return launch(
        kernel,
        (count, steps),
        [left] * m + [ANY] * len(flat) + [piece] * len(received),
        out_specs,
        out_shape,
        (*lefts, *flat, *received),
        scalars=(order, shares),
        scratch=(pltpu.VMEM((width, m * local), BF16), pltpu.SemaphoreType.DMA),
        flops=2 * count * share * width * m * local,
        moved=width * m * local * 2 + count * share * (m * local + width) * 2,
    )


def finish_output(mine, own, received, x, vec):
    share, width = own.shape
    tile = min(256, share)
    steps = share // tile

    def kernel(mine_ref, own_ref, x_ref, vec_ref, *rest):
        total = own_ref[...]
        for ref in rest[:-1]:
            total += ref[...].astype(F32)
        rest[-1][...] = (x_ref[...].astype(F32) + total + vec_ref[2:3, :] + vec_ref[3:4, :]).astype(BF16)

    row = pl.BlockSpec((tile, width), lambda i, *_: (i, 0))
    far = pl.BlockSpec((tile, width), lambda i, mine_ref: (mine_ref[0] * steps + i, 0))
    return launch(
        kernel,
        (steps,),
        [row, far, whole(4, width)] + [row] * len(received),
        row,
        jax.ShapeDtypeStruct((share, width), BF16),
        (own, x, vec, *received),
        scalars=(mine,),
        moved=share * width * 10,
    )


def finish_input(mine, own, received, x, g, vec):
    share, width = own.shape
    tile = min(256, share)
    steps = share // tile

    def kernel(mine_ref, own_ref, x_ref, g_ref, vec_ref, *rest):
        grad_ref, rows_ref = rest[-2:]
        dn = own_ref[...]
        for ref in rest[:-2]:
            dn += ref[...].astype(F32)
        x = x_ref[...].astype(F32)
        g = g_ref[...].astype(F32)
        mean = jnp.mean(x, -1, keepdims=True)
        centered = x - mean
        var = jnp.mean(centered * centered, -1, keepdims=True)
        inverse = lax.rsqrt(var + 1e-05)
        hat = centered * inverse
        e = dn * vec_ref[0:1, :]
        back = inverse * (e - jnp.mean(e, -1, keepdims=True) - hat * jnp.mean(e * hat, -1, keepdims=True))
        grad_ref[...] = (g + back).astype(BF16)

        @pl.when(pl.program_id(0) == 0)
        def _():
            rows_ref[...] = jnp.zeros_like(rows_ref)

        rows_ref[0:1, :] += jnp.sum(dn * hat, 0, keepdims=True)
        rows_ref[1:2, :] += jnp.sum(dn, 0, keepdims=True)
        rows_ref[2:3, :] += jnp.sum(g, 0, keepdims=True)

    row = pl.BlockSpec((tile, width), lambda i, *_: (i, 0))
    far = pl.BlockSpec((tile, width), lambda i, mine_ref: (mine_ref[0] * steps + i, 0))
    return launch(
        kernel,
        (steps,),
        [row, far, far, whole(4, width)] + [row] * len(received),
        (row, whole(3, width)),
        (jax.ShapeDtypeStruct((share, width), BF16), jax.ShapeDtypeStruct((3, width), F32)),
        (own, x, g, vec, *received),
        scalars=(mine,),
        moved=share * width * 12,
    )


def lay_out(order, parts):
    share, width = parts[0].shape
    count = len(parts)
    tile = min(256, share)
    steps = share // tile

    def kernel(order_ref, *rest):
        for r in range(count):

            @pl.when(pl.program_id(0) == r)
            def _(r=r):
                rest[count][...] = rest[r][...]

    def fetch(r):
        return pl.BlockSpec(
            (tile, width), lambda i, j, *_: (jnp.where(i == r, j, jnp.where(i < r, 0, steps - 1)), 0)
        )

    return launch(
        kernel,
        (count, steps),
        [fetch(r) for r in range(count)],
        pl.BlockSpec((tile, width), lambda i, j, order_ref: (order_ref[i] * steps + j, 0)),
        jax.ShapeDtypeStruct((share * count, width), parts[0].dtype),
        parts,
        scalars=(order,),
        moved=share * count * width * 4,
    )


def total_group(grads, own, received, places, slots_in_all):
    n, rows, local = own.shape

    def kernel(places_ref, own_ref, *rest):
        out, squares = rest[-2:]
        total = own_ref[0]
        for ref in rest[: len(received)]:
            total += ref[0].astype(F32)
        out[0] = total

        @pl.when(pl.program_id(0) == 0)
        def _():
            squares[...] = jnp.zeros_like(squares)

        squares[...] += jnp.sum(total * total, 0, keepdims=True)

    piece = pl.BlockSpec((1, rows, local), lambda i, *_: (i, 0, 0))
    out = pl.BlockSpec((1, rows, local), lambda i, places_ref: (places_ref[i], 0, 0))
    first = grads is None
    return launch(
        kernel,
        (n,),
        [piece] * (1 + len(received)) + ([] if first else [ANY]),
        (out, whole(1, local)),
        (jax.ShapeDtypeStruct((slots_in_all, rows, local), F32), jax.ShapeDtypeStruct((1, local), F32)),
        (own, *received) + (() if first else (grads,)),
        scalars=(places,),
        aliases={} if first else {2 + len(received): 0},
        moved=n * rows * local * 14,
    )


def double_up(values, axis, count):
    me = lax.axis_index(axis)
    bit = 1
    while bit < count:
        other = lax.ppermute(values, axis, [(i, i ^ bit) for i in range(count)])
        high = (me & bit) != 0
        values = jnp.where(high, jnp.concatenate([other, values], 0), jnp.concatenate([values, other], 0))
        bit *= 2
    return values


def total_over(values, axis, count):
    bit = 1
    while bit < count:
        values = values + lax.ppermute(values, axis, [(i, i ^ bit) for i in range(count)])
        bit *= 2
    return values


def shift(values, axis, count, inner, outer_by, inner_by):
    outer = count // inner
    pairs = [
        (o * inner + i, (o + outer_by) % outer * inner + (i + inner_by) % inner)
        for o in range(outer)
        for i in range(inner)
    ]
    return lax.ppermute(values, axis, pairs)


def body(
    block_input,
    cotangent,
    segment_ids,
    w_in,
    w_in_m,
    w_in_v,
    w_outs,
    w_outs_m,
    w_outs_v,
    in_bias,
    in_bias_m,
    in_bias_v,
    vectors,
    vectors_m,
    vectors_v,
):
    n_dp = lax.axis_size("dp")
    n_tensor = lax.axis_size("tensor")
    inner = 2 if n_dp <= 8 else 4
    outer = n_dp // inner
    cores = 2
    ways = n_tensor // cores
    me = lax.axis_index("dp")
    mine = lax.axis_index("tensor")
    my_outer, my_inner = me // inner, me % inner
    my_way, my_core = mine // cores, mine % cores
    tokens, width = block_input.shape
    _, slots_in, local = w_in.shape
    slots_out = w_outs.shape[1]
    hidden_slots = slots_out - 1

    def numbers(values):
        return jnp.stack([jnp.asarray(v, jnp.int32) for v in values])

    order = numbers(
        [
            (my_outer - o) % outer * inner + (my_inner - i) % inner
            for o in range(outer)
            for i in range(inner)
        ]
    )
    dests = [
        numbers([(my_outer + o) % outer * inner + (my_inner + i) % inner for o in range(outer)])
        for i in range(inner)
    ]
    share_order = numbers(
        [(my_way - w) % ways * cores + (my_core - c) % cores for w in range(ways) for c in range(cores)]
    )
    share_dests = [
        numbers([(my_way + w) % ways * cores + (my_core + c) % cores for w in range(ways)])
        for c in range(cores)
    ]
    share_mine = numbers([mine])

    w_in_s = w_in.transpose(1, 0, 2)
    w_outs_s = w_outs.transpose(1, 0, 2)

    def gather(own):
        blocks = []
        held = [own] + [shift(own, "dp", n_dp, inner, o, 0) for o in range(1, outer)]
        for part in held:
            blocks.append(part)
            for i in range(1, inner):
                blocks.append(shift(part, "dp", n_dp, inner, 0, i))
        return blocks

    first_slots = [(0, 0), (0, 1), (0, 2), (1, 0)]
    group_slots = [first_slots] + [[(0, 3 + s), (1, 1 + s)] for s in range(hidden_slots)]

    small = jnp.concatenate([in_bias.reshape(1, -1), vectors.reshape(1, -1)], 1).astype(BF16).astype(F32)
    small = double_up(small, "dp", n_dp)
    bias_size = in_bias.size
    bias = small[:, :bias_size].reshape((n_dp,) + in_bias.shape).transpose(1, 2, 0, 3).reshape(slots_in, local)
    vec = small[:, bias_size:].reshape((n_dp,) + vectors.shape).transpose(1, 0, 2).reshape(4, width)

    groups = []
    for g, slots in enumerate(group_slots):
        deps = groups[g - 2][-1:] if g >= 2 else []
        groups.append(gather(cast_group(w_in_s, w_outs_s, slots, deps)))

    seg = segment_ids[0]
    start = jnp.sum((seg[None, :] < seg[:, None]).astype(jnp.int32), 1)
    block = min(256, tokens)
    low = start[::block] // block
    place = (jnp.arange(tokens, dtype=jnp.int32) - start).astype(F32)
    freq = 10000.0 ** (-jnp.arange(ROT // 2, dtype=F32) * 2.0 / ROT)
    theta = place[:, None] * freq[None, :]
    cosine, sine = jnp.cos(theta), jnp.sin(theta)
    rest = jnp.zeros((tokens, HDIM - ROT), F32)
    none = jnp.zeros_like(sine)
    tables = jnp.stack(
        [
            jnp.concatenate([cosine, cosine, rest + 1.0] * 2, 1),
            jnp.concatenate([-sine, none, rest] * 2, 1),
            jnp.concatenate([none, sine, rest] * 2, 1),
        ]
    )

    normed, normed_t, g_t = normalize(block_input, cotangent, vec)

    query, keys, vals, d_attn = qkv_project(order, normed, cotangent, bias, tables, groups[0])
    attn, d_query, d_keys, d_vals, d_bias_attn = attend(
        low, query, keys, vals, d_attn, start.reshape(1, tokens), tables
    )

    def send_back(sides):
        received = []
        for i in range(1, inner):
            out = grad_blocks(dests[i], normed_t, g_t, sides, [], False)
            received.append(shift(out, "dp", n_dp, inner, 0, i))
        outs = grad_blocks(dests[0], normed_t, g_t, sides, received, True)
        return outs[0], [shift(outs[o], "dp", n_dp, inner, o, 0) for o in range(1, outer)]

    hidden, d_hidden, d_bias_hidden = [], [], []
    shares = [send_back([(0, d_query), (0, d_keys), (0, d_vals), (1, attn)])]
    for s in range(hidden_slots):
        h, dz, db = hidden_slot(order, normed, cotangent, bias[3 + s : 4 + s], groups[1 + s])
        hidden.append(h)
        d_hidden.append(dz)
        d_bias_hidden.append(db)
        shares.append(send_back([(0, dz), (1, h)]))

    by_owner = [[group[r] for group in groups] for r in range(n_dp)]

    def sum_tensor(lefts, slots):
        received = []
        for c in range(1, cores):
            out = project_back(order, share_dests[c], lefts, by_owner, slots, [], False)
            received.append(shift(out, "tensor", n_tensor, cores, 0, c))
        outs = project_back(order, share_dests[0], lefts, by_owner, slots, received, True)
        return outs[0], [shift(outs[w], "tensor", n_tensor, cores, w, 0) for w in range(1, ways)]

    def gather_tensor(own):
        parts = []
        held = [own] + [shift(own, "tensor", n_tensor, cores, w, 0) for w in range(1, ways)]
        for part in held:
            parts.append(part)
            for c in range(1, cores):
                parts.append(shift(part, "tensor", n_tensor, cores, 0, c))
        return lay_out(share_order, parts)

    own, received = sum_tensor(
        [d_query, d_keys, d_vals] + d_hidden, [(0, 0), (0, 1), (0, 2)] + [(1 + s, 0) for s in range(hidden_slots)]
    )
    d_x, vector_rows = finish_input(share_mine, own, received, block_input, cotangent, vec)
    block_input_gradient = gather_tensor(d_x)

    own, received = sum_tensor([attn] + hidden, [(0, 3)] + [(1 + s, 1) for s in range(hidden_slots)])
    output = gather_tensor(finish_output(share_mine, own, received, block_input, vec))

    vector_rows = total_over(vector_rows.reshape(1, -1), "tensor", n_tensor)
    d_bias = jnp.concatenate([d_bias_attn] + d_bias_hidden, 0)
    small = total_over(jnp.concatenate([d_bias.reshape(1, -1), vector_rows], 1), "dp", n_dp)
    g_bias = lax.dynamic_index_in_dim(
        small[0, : slots_in * local].reshape(slots_in, in_bias.shape[1], n_dp, in_bias.shape[2]), me, 2, False
    )
    g_vec = lax.dynamic_index_in_dim(small[0, slots_in * local :].reshape(3, n_dp, width // n_dp), me, 1, False)
    g_vec = jnp.concatenate([g_vec, g_vec[2:]], 0)

    grads, squares = None, []
    for slots, (own, received) in zip(group_slots, shares):
        places = jnp.asarray([s if which == 0 else slots_in + s for which, s in slots], jnp.int32)
        grads, part = total_group(grads, own, received, places, slots_in + slots_out)
        squares.append(part)
    g_in, g_outs = grads[:slots_in], grads[slots_in:]
    local_squares = (
        jnp.sum(jnp.concatenate(squares, 0)) + jnp.sum(g_bias * g_bias) + jnp.sum(g_vec * g_vec) * (1.0 / n_tensor)
    )
    local_squares = total_over(jnp.full((1, LANES), local_squares), "tensor", n_tensor)
    local_squares = total_over(local_squares, "dp", n_dp)
    grad_norm = jnp.sqrt(local_squares[0, 0])
    factor = CLIP_AT / jnp.maximum(grad_norm, CLIP_AT)

    def slot_major(*arrays):
        return [a.transpose(1, 0, 2) for a in arrays]

    new_in = slot_major(*adamw(w_in_s, *slot_major(w_in_m, w_in_v), g_in, factor, RATE_MATRIX, DECAY_MATRIX))
    new_outs = slot_major(*adamw(w_outs_s, *slot_major(w_outs_m, w_outs_v), g_outs, factor, RATE_MATRIX, DECAY_MATRIX))
    new_bias = adamw(in_bias, in_bias_m, in_bias_v, g_bias, factor, RATE_VECTOR, 0.0)
    new_vec = adamw(vectors, vectors_m, vectors_v, g_vec, factor, RATE_VECTOR, 0.0)
    return (output, block_input_gradient, grad_norm, *new_in, *new_outs, *new_bias, *new_vec)


def solution(mesh):
    rows = P("dp", None)
    matrix = P("dp", None, "tensor")
    small = P(None, "tensor", "dp")
    vector = P(None, "dp")
    return jax.shard_map(
        body,
        mesh=mesh,
        in_specs=(rows,) * 3 + (matrix,) * 6 + (small,) * 3 + (vector,) * 3,
        out_specs=(rows, rows, P()) + (matrix,) * 6 + (small,) * 3 + (vector,) * 3,
        check_vma=False,
    )
```

time: 2530 us -> 1130 us (0.45)
  waiting for transfers between devices: 1520 us -> 374 us
  Pallas kernels: 0 us -> 480 us
  matrix products: 431 us -> 0 us
  other arithmetic: 243 us -> 37.1 us
  starting transfers between devices: 0.25 us -> 206 us
  local copies, waits for them, and re-layouts: 170 us -> 18.8 us
  blocking collectives: 142 us -> 0 us
    reduce_scatter x2 -> x0, waiting for transfers between devices: 719 us -> none  [the longest x1 465 us: body(): lax.psum_scatter(d_w_in, 'dp', scatter_dimension=0, tiled=True)]
    psum x1 -> x0, waiting for transfers between devices: 557 us -> none  [body(): summed = lax.psum(partial_sum, 'tensor')]
    pallas_call x0 -> x35, Pallas kernels: none -> 480 us  [launch(): pl.pallas_call(kernel, grid_spec=pltpu.PrefetchScalarGridSpec(num_scalar_...]
    dot_general x30 -> x0, matrix products: 431 us -> none  [the longest x2 72.1 us: contract_rows(): lax.dot_general(left, right, (((0,), (0,)), ((), ())), preferred_element_...]
    ppermute x0 -> x78, waiting for transfers between devices: none -> 374 us  [the longest x65 288 us: shift(): return lax.ppermute(values, axis, pairs)]
    all_gather x2 -> x0, waiting for transfers between devices: 238 us -> none  [the longest x1 170 us: body(): lax.all_gather(w_in.astype(jnp.bfloat16), 'dp', axis=0, tiled=True)]
    ppermute x0 -> x78, starting transfers between devices: none -> 206 us  [the longest x65 142 us: shift(): return lax.ppermute(values, axis, pairs)]
    reduce_sum x12 -> x7, other arithmetic: 97.1 us -> 6.1 us  [the longest x5 3.71 us: body(): jnp.sum(jnp.concatenate(squares, 0)) + jnp.sum(g_bias * g_bias)]
  transfers between devices with their start and end apart: 6 -> 78, of which waited for: 5 -> 24; matrix products, arithmetic and copies ran while one was open for 7% -> 5% of each run, Pallas kernels for 0% -> 38%
where the time goes in v1:
time: 1130 us
  Pallas kernels  480 us (42%)
  waiting for transfers between devices  374 us (33%)
  starting transfers between devices  206 us (18%)
  other arithmetic  37.1 us (3%)
  local copies, waits for them, and re-layouts  18.8 us (2%)
    pallas_call x35, Pallas kernels, launch(): pl.pallas_call(kernel, grid_spec=pltpu.PrefetchScalarGridSpec(num_scalar_...  480 us
    ppermute x65, waiting for transfers between devices, shift(): return lax.ppermute(values, axis, pairs)  288 us
    ppermute x65, starting transfers between devices, shift(): return lax.ppermute(values, axis, pairs)  142 us
    ppermute x10, starting transfers between devices, total_over(): lax.ppermute(values, axis, [(i, i ^ bit) for i in range(count)])  61 us
    ppermute x3, waiting for transfers between devices, double_up(): other = lax.ppermute(values, axis, [(i, i ^ bit) for i in range(count)])  56.3 us
    ppermute x10, waiting for transfers between devices, total_over(): lax.ppermute(values, axis, [(i, i ^ bit) for i in range(count)])  30.5 us
  transfers between devices with their start and end apart: 78, of which 24 were waited for; matrix products, arithmetic and copies ran while one was open for 5% of the time, Pallas kernels for 38%

profile of v1, /device:TPU:0, one launch (start us, length us, event | category | flops | bytes accessed | tf_op | source)
XLA Modules:
  0.0 1125.1 jit_solution(9363911371612404425)
XLA Ops:
  18.4 46.1 %collective-permute-done.1 = f32[2,1472]{1,0:T(2,128)S(1)} collective-permute-done((f32[2,1472]{1,0:T(2,128)S(1)}, f32[2,1472]{1,0:T(2,128)S(1)}, u32[]{:S(2)}, u32[]{:S(2)}) %collective-permute-start.1) | collective-permute-done | bytes 11808 | tf_op jit(solution)/shard_map/ppermute | solution.py:608
  101.7 15.8 %collective-permute-done.16.rest_7_.refs_2_.rest_41_.rest_43_ = bf16[2,256,512]{2,1,0:T(8,128)(2,1)} collective-permute-done((bf16[2,256,512]{2,1,0:T(8,128)(2,1)}, bf16[2,256,512]{2,1,0:T(8,128)(2,1)}, u32[]{:S(2)}, u32[]{:S(2)}) %collective-permute-start.16) | collective-permute-done | bytes 524320 | tf_op jit(solution)/shard_map/ppermute | solution.py:630
  125.5 22.8 %collective-permute-done.10.rest_1_.rest_11_.rest_13_ = bf16[2,256,512]{2,1,0:T(8,128)(2,1)S(1)} collective-permute-done((bf16[2,256,512]{2,1,0:T(8,128)(2,1)S(1)}, bf16[2,256,512]{2,1,0:T(8,128)(2,1)S(1)}, u32[]{:S(2)}, u32[]{:S(2)}) %collective-permute-start.10) | collective-permute-done | bytes 524320 | tf_op jit(solution)/shard_map/ppermute | solution.py:630
  158.3 18.0 %shard_map.307 = (bf16[2048,2048]{1,0:T(8,128)(2,1)}, bf16[2048,2048]{1,0:T(8,128)(2,1)}, bf16[2048,2048]{1,0:T(8,128)(2,1)}) custom-call(bf16[2048,2048]{1,0:T(8,128)(2,1)} %x_ref.5, bf16[2048,2048]{1,0:T(8,128)(2,1)} %g_ref.13, f32[4,2048]{1,0:T(4,128)} %bitcast.121), custom_call_target="tpu_custom_call" | custom-call | flops 41943040 | bytes 41943040 | tf_op jit(solution)/shard_map/pallas_call | solution.py:42
  183.0 15.9 %shard_map.312 = (bf16[2048,512]{1,0:T(8,128)(2,1)}, bf16[2048,512]{1,0:T(8,128)(2,1)}, f32[1,512]{1,0:T(1,128)}) custom-call(s32[8]{0:T(128)} %stack.115.order_ref, bf16[2048,2048]{1,0:T(8,128)(2,1)} %get-tuple-element.75.x_ref, bf16[2048,2048]{1,0:T(8,128)(2,1)} %g_ref.13, f32[1,512]{1,0:T(1,128)} %slice.58.bias_ref, ...), custom_call_target="tpu_custom_call" | custom-call | flops 8589934592 | bytes 20971520 | tf_op jit(solution)/shard_map/pallas_call | solution.py:42
  207.6 11.7 %collective-permute-done.7.rest_5_.rest_30_.rest_32_ = bf16[4,256,512]{2,1,0:T(8,128)(2,1)} collective-permute-done((bf16[4,256,512]{2,1,0:T(8,128)(2,1)}, bf16[4,256,512]{2,1,0:T(8,128)(2,1)}, u32[]{:S(2)}, u32[]{:S(2)}) %collective-permute-start.7) | collective-permute-done | bytes 1048608 | tf_op jit(solution)/shard_map/ppermute | solution.py:630
  221.4 26.3 %shard_map.309 = (bf16[2048,512]{1,0:T(8,128)(2,1)}, bf16[2048,512]{1,0:T(8,128)(2,1)}, bf16[2048,512]{1,0:T(8,128)(2,1)}, bf16[2048,512]{1,0:T(8,128)(2,1)}) custom-call(s32[8]{0:T(128)} %stack.115.order_ref, bf16[2048,2048]{1,0:T(8,128)(2,1)} %get-tuple-element.75.x_ref, bf16[2048,2048]{1,0:T(8,128)(2,1)} %g_ref.13, f32[7,512]{1,0:T(8,128)} %reshape.121.bias_ref, ...), custom_call_target="tpu_custom_call" | custom-call | flops 17179869184 | bytes 25165824 | tf_op jit(solution)/shard_map/pallas_call | solution.py:42
  256.7 16.0 %collective-permute-done.23.rest_7_.refs_2_.rest_42_.rest_44_ = bf16[2,256,512]{2,1,0:T(8,128)(2,1)S(1)} collective-permute-done((bf16[2,256,512]{2,1,0:T(8,128)(2,1)}, bf16[2,256,512]{2,1,0:T(8,128)(2,1)S(1)}, u32[]{:S(2)}, u32[]{:S(2)}) %collective-permute-start.23) | collective-permute-done | bytes 524320 | tf_op jit(solution)/shard_map/ppermute | solution.py:630
  274.2 94.4 %shard_map.310 = (bf16[2048,512]{1,0:T(8,128)(2,1)}, bf16[2048,512]{1,0:T(8,128)(2,1)}, bf16[2048,512]{1,0:T(8,128)(2,1)}, bf16[2048,512]{1,0:T(8,128)(2,1)}, f32[3,512]{1,0:T(4,128)}) custom-call(s32[8]{0:T(128)} %and_select_fusion.low_ref, bf16[2048,512]{1,0:T(8,128)(2,1)} %get-tuple-element.76.q_ref, bf16[2048,512]{1,0:T(8,128)(2,1)} %get-tuple-element.77.k_ref, ...), custom_call_target="tpu_custom_call" | custom-call | flops 51539607552 | bytes 20971520 | tf_op jit(solution)/shard_map/pallas_call | solution.py:42
  383.9 15.9 %shard_map.316 = (bf16[2048,512]{1,0:T(8,128)(2,1)}, bf16[2048,512]{1,0:T(8,128)(2,1)}, f32[1,512]{1,0:T(1,128)}) custom-call(s32[8]{0:T(128)} %stack.115.order_ref, bf16[2048,2048]{1,0:T(8,128)(2,1)} %get-tuple-element.75.x_ref, bf16[2048,2048]{1,0:T(8,128)(2,1)} %g_ref.13, f32[1,512]{1,0:T(1,128)} %slice.62.bias_ref, ...), custom_call_target="tpu_custom_call" | custom-call | flops 8589934592 | bytes 20971520 | tf_op jit(solution)/shard_map/pallas_call | solution.py:42
  402.0 14.2 %collective-permute-done.34.rest_4_.rest_29_.rest_31_ = bf16[2,256,512]{2,1,0:T(8,128)(2,1)S(1)} collective-permute-done((bf16[2,256,512]{2,1,0:T(8,128)(2,1)}, bf16[2,256,512]{2,1,0:T(8,128)(2,1)S(1)}, u32[]{:S(2)}, u32[]{:S(2)}) %collective-permute-start.34) | collective-permute-done | bytes 524320 | tf_op jit(solution)/shard_map/ppermute | solution.py:630
  418.3 15.9 %shard_map.314 = (bf16[2048,512]{1,0:T(8,128)(2,1)}, bf16[2048,512]{1,0:T(8,128)(2,1)}, f32[1,512]{1,0:T(1,128)}) custom-call(s32[8]{0:T(128)} %stack.115.order_ref, bf16[2048,2048]{1,0:T(8,128)(2,1)} %get-tuple-element.75.x_ref, bf16[2048,2048]{1,0:T(8,128)(2,1)} %g_ref.13, f32[1,512]{1,0:T(1,128)} %slice.60.bias_ref, ...), custom_call_target="tpu_custom_call" | custom-call | flops 8589934592 | bytes 20971520 | tf_op jit(solution)/shard_map/pallas_call | solution.py:42
  445.4 15.9 %shard_map.318 = (bf16[2048,512]{1,0:T(8,128)(2,1)}, bf16[2048,512]{1,0:T(8,128)(2,1)}, f32[1,512]{1,0:T(1,128)}) custom-call(s32[8]{0:T(128)} %stack.115.order_ref, bf16[2048,2048]{1,0:T(8,128)(2,1)} %get-tuple-element.75.x_ref, bf16[2048,2048]{1,0:T(8,128)(2,1)} %g_ref.13, f32[1,512]{1,0:T(1,128)} %slice.64.bias_ref, ...), custom_call_target="tpu_custom_call" | custom-call | flops 8589934592 | bytes 20971520 | tf_op jit(solution)/shard_map/pallas_call | solution.py:42
  461.3 24.9 %shard_map.323 = bf16[1024,2048]{1,0:T(8,128)(2,1)} custom-call(s32[8]{0:T(128)} %stack.115.order_ref, s32[2]{0:T(128)} %pad_add_fusion.2.shares_ref, bf16[2048,512]{1,0:T(8,128)(2,1)} %get-tuple-element.87.rest_0_, bf16[2048,512]{1,0:T(8,128)(2,1)} %get-tuple-element.88.rest_1_, bf16[2048,512]{1,0:T(8,128)(2,1)} %get-tuple-element.89.rest_2_, ...), custom_call_target="tpu_custom_call" | custom-call | flops 15032385536 | bytes 26214400 | tf_op jit(solution)/shard_map/pallas_call | solution.py:42
  487.5 18.9 %shard_map.319 = bf16[1024,2048]{1,0:T(8,128)(2,1)} custom-call(s32[8]{0:T(128)} %stack.115.order_ref, s32[2]{0:T(128)} %pad_add_fusion.2.shares_ref, bf16[2048,512]{1,0:T(8,128)(2,1)} %get-tuple-element.80.rest_0_.rest_3_, bf16[2048,512]{1,0:T(8,128)(2,1)} %get-tuple-element.81.rest_1_, bf16[2048,512]{1,0:T(8,128)(2,1)} %get-tuple-element.82.rest_2_.rest_1_, ...), custom_call_target="tpu_custom_call" | custom-call | flops 10737418240 | bytes 19922944 | tf_op jit(solution)/shard_map/pallas_call | solution.py:42
  517.6 27.2 %shard_map.324 = (f32[512,2048]{1,0:T(8,128)}, bf16[512,2048]{1,0:T(8,128)(2,1)}) custom-call(s32[8]{0:T(128)} %stack.115.order_ref, s32[2]{0:T(128)} %pad_add_fusion.1.shares_ref, bf16[2048,512]{1,0:T(8,128)(2,1)} %get-tuple-element.87.rest_0_, bf16[2048,512]{1,0:T(8,128)(2,1)} %get-tuple-element.88.rest_1_, bf16[2048,512]{1,0:T(8,128)(2,1)} %get-tuple-element.89.rest_2_, ...), custom_call_target="tpu_custom_call" | custom-call | flops 15032385536 | bytes 26214400 | tf_op jit(solution)/shard_map/pallas_call | solution.py:42
  557.9 15.2 %shard_map.327 = bf16[4,4,256,512]{3,2,1,0:T(8,128)(2,1)} custom-call(s32[4]{0:T(128)} %pad_add_fusion.4.dest_ref, bf16[2048,2048]{1,0:T(8,128)(2,1)} %get-tuple-element.97.x_ref, bf16[2048,2048]{1,0:T(8,128)(2,1)} %get-tuple-element.98.g_ref, bf16[2048,512]{1,0:T(8,128)(2,1)} %get-tuple-element.87.rest_0_, bf16[2048,512]{1,0:T(8,128)(2,1)} %get-tuple-element.88.rest_1_, ...), custom_call_target="tpu_custom_call" | custom-call | flops 8589934592 | bytes 20971520 | tf_op jit(solution)/shard_map/pallas_call | solution.py:42
  596.3 11.7 %shard_map.331 = (f32[2,256,512]{2,1,0:T(8,128)}, bf16[2,256,512]{2,1,0:T(8,128)(2,1)}, bf16[2,256,512]{2,1,0:T(8,128)(2,1)}, bf16[2,256,512]{2,1,0:T(8,128)(2,1)}) custom-call(s32[4]{0:T(128)} %pad_add_fusion.3.dest_ref, bf16[2048,2048]{1,0:T(8,128)(2,1)} %get-tuple-element.97.x_ref, bf16[2048,2048]{1,0:T(8,128)(2,1)} %get-tuple-element.98.g_ref, ...), custom_call_target="tpu_custom_call" | custom-call | flops 4294967296 | bytes 14680064 | tf_op jit(solution)/shard_map/pallas_call | solution.py:42
  616.4 21.9 %shard_map.320 = (f32[512,2048]{1,0:T(8,128)}, bf16[512,2048]{1,0:T(8,128)(2,1)}) custom-call(s32[8]{0:T(128)} %stack.115.order_ref, s32[2]{0:T(128)} %pad_add_fusion.1.shares_ref, bf16[2048,512]{1,0:T(8,128)(2,1)} %get-tuple-element.80.rest_0_.rest_3_, bf16[2048,512]{1,0:T(8,128)(2,1)} %get-tuple-element.81.rest_1_, ...), custom_call_target="tpu_custom_call" | custom-call | flops 10737418240 | bytes 19922944 | tf_op jit(solution)/shard_map/pallas_call | solution.py:42
  640.5 11.7 %shard_map.337 = (f32[2,256,512]{2,1,0:T(8,128)}, bf16[2,256,512]{2,1,0:T(8,128)(2,1)}, bf16[2,256,512]{2,1,0:T(8,128)(2,1)}, bf16[2,256,512]{2,1,0:T(8,128)(2,1)}) custom-call(s32[4]{0:T(128)} %pad_add_fusion.3.dest_ref, bf16[2048,2048]{1,0:T(8,128)(2,1)} %get-tuple-element.97.x_ref, bf16[2048,2048]{1,0:T(8,128)(2,1)} %get-tuple-element.98.g_ref, ...), custom_call_target="tpu_custom_call" | custom-call | flops 4294967296 | bytes 14680064 | tf_op jit(solution)/shard_map/pallas_call | solution.py:42
  652.4 93.2 %collective-permute-done.56.rest_2_ = bf16[4,2,256,512]{3,2,1,0:T(8,128)(2,1)S(1)} collective-permute-done((bf16[4,2,256,512]{3,2,1,0:T(8,128)(2,1)}, bf16[4,2,256,512]{3,2,1,0:T(8,128)(2,1)S(1)}, u32[]{:S(2)}, u32[]{:S(2)}) %collective-permute-start.56) | collective-permute-done | bytes 2097184 | tf_op jit(solution)/shard_map/ppermute | solution.py:630
  747.2 42.5 %collective-permute-done.64.rest_2_ = bf16[4,2,256,512]{3,2,1,0:T(8,128)(2,1)} collective-permute-done((bf16[4,2,256,512]{3,2,1,0:T(8,128)(2,1)}, bf16[4,2,256,512]{3,2,1,0:T(8,128)(2,1)}, u32[]{:S(2)}, u32[]{:S(2)}) %collective-permute-start.64) | collective-permute-done | bytes 2097184 | tf_op jit(solution)/shard_map/ppermute | solution.py:630
  794.3 11.8 %shard_map.334 = (f32[2,256,512]{2,1,0:T(8,128)}, bf16[2,256,512]{2,1,0:T(8,128)(2,1)}, bf16[2,256,512]{2,1,0:T(8,128)(2,1)}, bf16[2,256,512]{2,1,0:T(8,128)(2,1)}) custom-call(s32[4]{0:T(128)} %pad_add_fusion.3.dest_ref, bf16[2048,2048]{1,0:T(8,128)(2,1)} %get-tuple-element.97.x_ref, bf16[2048,2048]{1,0:T(8,128)(2,1)} %get-tuple-element.98.g_ref, ...), custom_call_target="tpu_custom_call" | custom-call | flops 4294967296 | bytes 14680064 | tf_op jit(solution)/shard_map/pallas_call | solution.py:42
  806.1 11.8 %shard_map.340 = (f32[2,256,512]{2,1,0:T(8,128)}, bf16[2,256,512]{2,1,0:T(8,128)(2,1)}, bf16[2,256,512]{2,1,0:T(8,128)(2,1)}, bf16[2,256,512]{2,1,0:T(8,128)(2,1)}) custom-call(s32[4]{0:T(128)} %pad_add_fusion.3.dest_ref, bf16[2048,2048]{1,0:T(8,128)(2,1)} %get-tuple-element.97.x_ref, bf16[2048,2048]{1,0:T(8,128)(2,1)} %get-tuple-element.98.g_ref, ...), custom_call_target="tpu_custom_call" | custom-call | flops 4294967296 | bytes 14680064 | tf_op jit(solution)/shard_map/pallas_call | solution.py:42
  834.7 25.1 %collective-permute-start.57 = (bf16[2,256,512]{2,1,0:T(8,128)(2,1)}, bf16[2,256,512]{2,1,0:T(8,128)(2,1)S(1)}, u32[]{:S(2)}, u32[]{:S(2)}) collective-permute-start(bf16[2,256,512]{2,1,0:T(8,128)(2,1)} %get-tuple-element.111), channel_id=1, source_target_pairs={{0,8},{4,12},{8,16},{12,20},{16,24},{20,28},{24,0},{28,4},{1,9},{5... | collective-permute-start | bytes 1572872 | tf_op jit(solution)/shard_map/ppermute | solution.py:630
  859.9 13.4 %collective-permute-done.62.rest_1_ = bf16[2,256,512]{2,1,0:T(8,128)(2,1)S(1)} collective-permute-done((bf16[2,256,512]{2,1,0:T(8,128)(2,1)}, bf16[2,256,512]{2,1,0:T(8,128)(2,1)S(1)}, u32[]{:S(2)}, u32[]{:S(2)}) %collective-permute-start.62) | collective-permute-done | bytes 524320 | tf_op jit(solution)/shard_map/ppermute | solution.py:630
  881.8 14.5 %collective-permute-start.65 = (bf16[2,256,512]{2,1,0:T(8,128)(2,1)}, bf16[2,256,512]{2,1,0:T(8,128)(2,1)}, u32[]{:S(2)}, u32[]{:S(2)}) collective-permute-start(bf16[2,256,512]{2,1,0:T(8,128)(2,1)} %get-tuple-element.123), channel_id=1, source_target_pairs={{0,8},{4,12},{8,16},{12,20},{16,24},{20,28},{24,0},{28,4},{1,9},{5... | collective-permute-start | bytes 1572872 | tf_op jit(solution)/shard_map/ppermute | solution.py:630
  896.8 19.6 %shard_map.328 = (f32[4,256,512]{2,1,0:T(8,128)}, bf16[4,256,512]{2,1,0:T(8,128)(2,1)}, bf16[4,256,512]{2,1,0:T(8,128)(2,1)}, bf16[4,256,512]{2,1,0:T(8,128)(2,1)}) custom-call(s32[4]{0:T(128)} %pad_add_fusion.3.dest_ref, bf16[2048,2048]{1,0:T(8,128)(2,1)} %get-tuple-element.97.x_ref, bf16[2048,2048]{1,0:T(8,128)(2,1)} %get-tuple-element.98.g_ref, ...), custom_call_target="tpu_custom_call" | custom-call | flops 8589934592 | bytes 20971520 | tf_op jit(solution)/shard_map/pallas_call | solution.py:42
  923.7 25.3 %collective-permute-done.59.rest_2_ = bf16[2,256,512]{2,1,0:T(8,128)(2,1)} collective-permute-done((bf16[2,256,512]{2,1,0:T(8,128)(2,1)}, bf16[2,256,512]{2,1,0:T(8,128)(2,1)}, u32[]{:S(2)}, u32[]{:S(2)}) %collective-permute-start.59) | collective-permute-done | bytes 524320 | tf_op jit(solution)/shard_map/ppermute | solution.py:630
  951.0 43.8 %collective-permute-start.71 = (f32[1,9728]{1,0:T(1,128)S(1)}, f32[1,9728]{1,0:T(1,128)S(1)}, u32[]{:S(2)}, u32[]{:S(2)}) collective-permute-start(f32[1,9728]{1,0:T(1,128)S(1)} %fusion.9), channel_id=1, source_target_pairs={{0,8},{4,12},{8,0},{12,4},{16,24},{20,28},{24,16},{28,20},{1,9},{5... | collective-permute-start | bytes 116744 | tf_op jit(solution)/shard_map/ppermute | solution.py:618
  996.9 22.4 %collective-permute-done.71 = f32[1,9728]{1,0:T(1,128)S(1)} collective-permute-done((f32[1,9728]{1,0:T(1,128)S(1)}, f32[1,9728]{1,0:T(1,128)S(1)}, u32[]{:S(2)}, u32[]{:S(2)}) %collective-permute-start.71) | collective-permute-done | bytes 38944 | tf_op jit(solution)/shard_map/ppermute | solution.py:618
  1019.3 12.0 %collective-permute-start.67 = (bf16[2,256,512]{2,1,0:T(8,128)(2,1)}, bf16[2,256,512]{2,1,0:T(8,128)(2,1)}, u32[]{:S(2)}, u32[]{:S(2)}) collective-permute-start(bf16[2,256,512]{2,1,0:T(8,128)(2,1)} %get-tuple-element.125), channel_id=1, source_target_pairs={{0,24},{4,28},{8,0},{12,4},{16,8},{20,12},{24,16},{28,20},{1,25},{... | collective-permute-start | bytes 1572872 | tf_op jit(solution)/shard_map/ppermute | solution.py:630
  (348 shorter events, 321.4 us)
Async XLA Ops:
  2.8 73.7 %collective-permute-start.15 = (bf16[2,256,512]{2,1,0:T(8,128)(2,1)}, bf16[2,256,512]{2,1,0:T(8,128)(2,1)}, u32[]{:S(2)}, u32[]{:S(2)}) collective-permute-start(bf16[2,256,512]{2,1,0:T(8,128)(2,1)} %shard_map.311.rest_0_.rest_6_.rest_8_), channel_id=1, source_target_pairs={{0,24},{4,28},{8,0},{12,4},{16,8},{20,12},{24,16},{28,20},{1,25},{... | collective-permute-start | bytes 1572872 | tf_op jit(solution)/shard_map/ppermute | solution.py:630
  7.8 72.1 %collective-permute-start.11 = (bf16[2,256,512]{2,1,0:T(8,128)(2,1)}, bf16[2,256,512]{2,1,0:T(8,128)(2,1)S(1)}, u32[]{:S(2)}, u32[]{:S(2)}) collective-permute-start(bf16[2,256,512]{2,1,0:T(8,128)(2,1)} %shard_map.311.rest_0_.rest_6_.rest_8_), channel_id=1, source_target_pairs={{0,8},{4,12},{8,16},{12,20},{16,24},{20,28},{24,0},{28,4},{1,9},{5... | collective-permute-start | bytes 1572872 | tf_op jit(solution)/shard_map/ppermute | solution.py:630
  7.8 73.5 %collective-permute-start.13 = (bf16[2,256,512]{2,1,0:T(8,128)(2,1)}, bf16[2,256,512]{2,1,0:T(8,128)(2,1)S(1)}, u32[]{:S(2)}, u32[]{:S(2)}) collective-permute-start(bf16[2,256,512]{2,1,0:T(8,128)(2,1)} %shard_map.311.rest_0_.rest_6_.rest_8_), channel_id=1, source_target_pairs={{0,16},{4,20},{8,24},{12,28},{16,0},{20,4},{24,8},{28,12},{1,17},{... | collective-permute-start | bytes 1572872 | tf_op jit(solution)/shard_map/ppermute | solution.py:630
  13.1 68.8 %collective-permute-start.8 = (bf16[4,256,512]{2,1,0:T(8,128)(2,1)}, bf16[4,256,512]{2,1,0:T(8,128)(2,1)}, u32[]{:S(2)}, u32[]{:S(2)}) collective-permute-start(bf16[4,256,512]{2,1,0:T(8,128)(2,1)} %shard_map.308.rest_0_.rest_5_.rest_7_), channel_id=1, source_target_pairs={{0,24},{4,28},{8,0},{12,4},{16,8},{20,12},{24,16},{28,20},{1,25},{... | collective-permute-start | bytes 3145736 | tf_op jit(solution)/shard_map/ppermute | solution.py:630
  76.4 73.4 %collective-permute-start.4 = (bf16[4,256,512]{2,1,0:T(8,128)(2,1)}, bf16[4,256,512]{2,1,0:T(8,128)(2,1)}, u32[]{:S(2)}, u32[]{:S(2)}) collective-permute-start(bf16[4,256,512]{2,1,0:T(8,128)(2,1)} %shard_map.308.rest_0_.rest_5_.rest_7_), channel_id=1, source_target_pairs={{0,8},{4,12},{8,16},{12,20},{16,24},{20,28},{24,0},{28,4},{1,9},{5... | collective-permute-start | bytes 3145736 | tf_op jit(solution)/shard_map/ppermute | solution.py:630
  76.5 73.8 %collective-permute-start.6 = (bf16[4,256,512]{2,1,0:T(8,128)(2,1)}, bf16[4,256,512]{2,1,0:T(8,128)(2,1)}, u32[]{:S(2)}, u32[]{:S(2)}) collective-permute-start(bf16[4,256,512]{2,1,0:T(8,128)(2,1)} %shard_map.308.rest_0_.rest_5_.rest_7_), channel_id=1, source_target_pairs={{0,16},{4,20},{8,24},{12,28},{16,0},{20,4},{24,8},{28,12},{1,17},{... | collective-permute-start | bytes 3145736 | tf_op jit(solution)/shard_map/ppermute | solution.py:630
  79.9 72.0 %collective-permute-start.3 = (bf16[4,256,512]{2,1,0:T(8,128)(2,1)}, bf16[4,256,512]{2,1,0:T(8,128)(2,1)}, u32[]{:S(2)}, u32[]{:S(2)}) collective-permute-start(bf16[4,256,512]{2,1,0:T(8,128)(2,1)} %shard_map.308.rest_0_.rest_5_.rest_7_), channel_id=1, source_target_pairs={{0,4},{4,0},{8,12},{12,8},{16,20},{20,16},{24,28},{28,24},{1,5},{5... | collective-permute-start | bytes 3145736 | tf_op jit(solution)/shard_map/ppermute | solution.py:630
  82.2 71.2 %collective-permute-start.9 = (bf16[4,256,512]{2,1,0:T(8,128)(2,1)}, bf16[4,256,512]{2,1,0:T(8,128)(2,1)}, u32[]{:S(2)}, u32[]{:S(2)}) collective-permute-start(bf16[4,256,512]{2,1,0:T(8,128)(2,1)} %collective-permute-done.8.rest_6_.rest_35_.rest_37_), channel_id=1, source_target_pairs={{0,4},{4,0},{8,12},{12,8},{16,20},{20,16},{24,28},{28,24},{1,5},{5... | collective-permute-start | bytes 3145736 | tf_op jit(solution)/shard_map/ppermute | solution.py:630
  153.4 66.0 %collective-permute-start.7 = (bf16[4,256,512]{2,1,0:T(8,128)(2,1)}, bf16[4,256,512]{2,1,0:T(8,128)(2,1)}, u32[]{:S(2)}, u32[]{:S(2)}) collective-permute-start(bf16[4,256,512]{2,1,0:T(8,128)(2,1)} %collective-permute-done.6.rest_4_.rest_25_.rest_27_), channel_id=1, source_target_pairs={{0,4},{4,0},{8,12},{12,8},{16,20},{20,16},{24,28},{28,24},{1,5},{5... | collective-permute-start | bytes 3145736 | tf_op jit(solution)/shard_map/ppermute | solution.py:630
  207.1 165.6 %collective-permute-start.28 = (bf16[2,256,512]{2,1,0:T(8,128)(2,1)S(1)}, bf16[2,256,512]{2,1,0:T(8,128)(2,1)}, u32[]{:S(2)}, u32[]{:S(2)}) collective-permute-start(bf16[2,256,512]{2,1,0:T(8,128)(2,1)S(1)} %collective-permute-done.27.rest_4_.rest_28_.rest_30_), channel_id=1, source_target_pairs={{0,4},{4,0},{8,12},{12,8},{16,20},{20,16},{24,28},{28,24},{1,5},{5... | collective-permute-start | bytes 1572872 | tf_op jit(solution)/shard_map/ppermute | solution.py:630
  219.4 160.7 %collective-permute-start.30 = (bf16[2,256,512]{2,1,0:T(8,128)(2,1)S(1)}, bf16[2,256,512]{2,1,0:T(8,128)(2,1)}, u32[]{:S(2)}, u32[]{:S(2)}) collective-permute-start(bf16[2,256,512]{2,1,0:T(8,128)(2,1)S(1)} %collective-permute-done.29.rest_6_.rest_38_.rest_40_), channel_id=1, source_target_pairs={{0,4},{4,0},{8,12},{12,8},{16,20},{20,16},{24,28},{28,24},{1,5},{5... | collective-permute-start | bytes 1572872 | tf_op jit(solution)/shard_map/ppermute | solution.py:630
  247.8 122.9 %collective-permute-start.18 = (bf16[2,256,512]{2,1,0:T(8,128)(2,1)S(1)}, bf16[2,256,512]{2,1,0:T(8,128)(2,1)S(1)}, u32[]{:S(2)}, u32[]{:S(2)}) collective-permute-start(bf16[2,256,512]{2,1,0:T(8,128)(2,1)S(1)} %copy-done.6), channel_id=1, source_target_pairs={{0,8},{4,12},{8,16},{12,20},{16,24},{20,28},{24,0},{28,4},{1,9},{5... | collective-permute-start | bytes 1572872 | tf_op jit(solution)/shard_map/ppermute | solution.py:630
  253.3 117.9 %collective-permute-start.20 = (bf16[2,256,512]{2,1,0:T(8,128)(2,1)S(1)}, bf16[2,256,512]{2,1,0:T(8,128)(2,1)S(1)}, u32[]{:S(2)}, u32[]{:S(2)}) collective-permute-start(bf16[2,256,512]{2,1,0:T(8,128)(2,1)S(1)} %copy-done.6), channel_id=1, source_target_pairs={{0,16},{4,20},{8,24},{12,28},{16,0},{20,4},{24,8},{28,12},{1,17},{... | collective-permute-start | bytes 1572872 | tf_op jit(solution)/shard_map/ppermute | solution.py:630
  272.7 110.9 %collective-permute-start.17 = (bf16[2,256,512]{2,1,0:T(8,128)(2,1)S(1)}, bf16[2,256,512]{2,1,0:T(8,128)(2,1)}, u32[]{:S(2)}, u32[]{:S(2)}) collective-permute-start(bf16[2,256,512]{2,1,0:T(8,128)(2,1)S(1)} %copy-done.6), channel_id=1, source_target_pairs={{0,4},{4,0},{8,12},{12,8},{16,20},{20,16},{24,28},{28,24},{1,5},{5... | collective-permute-start | bytes 1572872 | tf_op jit(solution)/shard_map/ppermute | solution.py:630
  506.4 109.9 %collective-permute-start.38 = (bf16[1024,2048]{1,0:T(8,128)(2,1)}, bf16[1024,2048]{1,0:T(8,128)(2,1)}, u32[]{:S(2)}, u32[]{:S(2)}) collective-permute-start(bf16[1024,2048]{1,0:T(8,128)(2,1)} %shard_map.319), channel_id=1, source_target_pairs={{0,1},{1,0},{2,3},{3,2},{4,5},{5,4},{6,7},{7,6},{8,9},{9,8},{10,11... | collective-permute-start | bytes 12582920 | tf_op jit(solution)/shard_map/ppermute | solution.py:630
  517.1 66.6 %collective-permute-start.52 = (bf16[4,2,256,512]{3,2,1,0:T(8,128)(2,1)}, bf16[4,2,256,512]{3,2,1,0:T(8,128)(2,1)}, u32[]{:S(2)}, u32[]{:S(2)}) collective-permute-start(bf16[4,2,256,512]{3,2,1,0:T(8,128)(2,1)} %shard_map.330), channel_id=1, source_target_pairs={{0,4},{4,0},{8,12},{12,8},{16,20},{20,16},{24,28},{28,24},{1,5},{5... | collective-permute-start | bytes 6291464 | tf_op jit(solution)/shard_map/ppermute | solution.py:630
  556.4 82.5 %collective-permute-start.60 = (bf16[4,2,256,512]{3,2,1,0:T(8,128)(2,1)}, bf16[4,2,256,512]{3,2,1,0:T(8,128)(2,1)}, u32[]{:S(2)}, u32[]{:S(2)}) collective-permute-start(bf16[4,2,256,512]{3,2,1,0:T(8,128)(2,1)} %shard_map.336), channel_id=1, source_target_pairs={{0,4},{4,0},{8,12},{12,8},{16,20},{20,16},{24,28},{28,24},{1,5},{5... | collective-permute-start | bytes 6291464 | tf_op jit(solution)/shard_map/ppermute | solution.py:630
  573.1 308.6 %collective-permute-start.48 = (bf16[4,4,256,512]{3,2,1,0:T(8,128)(2,1)}, bf16[4,4,256,512]{3,2,1,0:T(8,128)(2,1)}, u32[]{:S(2)}, u32[]{:S(2)}) collective-permute-start(bf16[4,4,256,512]{3,2,1,0:T(8,128)(2,1)} %shard_map.327), channel_id=1, source_target_pairs={{0,4},{4,0},{8,12},{12,8},{16,20},{20,16},{24,28},{28,24},{1,5},{5... | collective-permute-start | bytes 12582920 | tf_op jit(solution)/shard_map/ppermute | solution.py:630
  583.6 161.9 %collective-permute-start.56 = (bf16[4,2,256,512]{3,2,1,0:T(8,128)(2,1)}, bf16[4,2,256,512]{3,2,1,0:T(8,128)(2,1)S(1)}, u32[]{:S(2)}, u32[]{:S(2)}) collective-permute-start(bf16[4,2,256,512]{3,2,1,0:T(8,128)(2,1)} %shard_map.333), channel_id=1, source_target_pairs={{0,4},{4,0},{8,12},{12,8},{16,20},{20,16},{24,28},{28,24},{1,5},{5... | collective-permute-start | bytes 6291464 | tf_op jit(solution)/shard_map/ppermute | solution.py:630
  595.1 194.6 %collective-permute-start.64 = (bf16[4,2,256,512]{3,2,1,0:T(8,128)(2,1)}, bf16[4,2,256,512]{3,2,1,0:T(8,128)(2,1)}, u32[]{:S(2)}, u32[]{:S(2)}) collective-permute-start(bf16[4,2,256,512]{3,2,1,0:T(8,128)(2,1)} %shard_map.339), channel_id=1, source_target_pairs={{0,4},{4,0},{8,12},{12,8},{16,20},{20,16},{24,28},{28,24},{1,5},{5... | collective-permute-start | bytes 6291464 | tf_op jit(solution)/shard_map/ppermute | solution.py:630
  638.3 258.0 %collective-permute-start.39 = (bf16[512,2048]{1,0:T(8,128)(2,1)}, bf16[512,2048]{1,0:T(8,128)(2,1)}, u32[]{:S(2)}, u32[]{:S(2)}) collective-permute-start(bf16[512,2048]{1,0:T(8,128)(2,1)} %get-tuple-element.86), channel_id=1, source_target_pairs={{0,2},{1,3},{2,0},{3,1},{4,6},{5,7},{6,4},{7,5},{8,10},{9,11},{10,... | collective-permute-start | bytes 6291464 | tf_op jit(solution)/shard_map/ppermute | solution.py:630
  638.9 152.3 %collective-permute-start.69 = (f32[1,6144]{1,0:T(1,128)S(1)}, f32[1,6144]{1,0:T(1,128)S(1)}, u32[]{:S(2)}, u32[]{:S(2)}) collective-permute-start(f32[1,6144]{1,0:T(1,128)S(1)} %add.342), channel_id=1, source_target_pairs={{0,2},{1,3},{2,0},{3,1},{4,6},{5,7},{6,4},{7,5},{8,10},{9,11},{10,... | collective-permute-start | bytes 73736 | tf_op jit(solution)/shard_map/ppermute | solution.py:618
  745.5 72.4 %collective-permute-start.53 = (bf16[2,256,512]{2,1,0:T(8,128)(2,1)}, bf16[2,256,512]{2,1,0:T(8,128)(2,1)S(1)}, u32[]{:S(2)}, u32[]{:S(2)}) collective-permute-start(bf16[2,256,512]{2,1,0:T(8,128)(2,1)} %get-tuple-element.105), channel_id=1, source_target_pairs={{0,8},{4,12},{8,16},{12,20},{16,24},{20,28},{24,0},{28,4},{1,9},{5... | collective-permute-start | bytes 1572872 | tf_op jit(solution)/shard_map/ppermute | solution.py:630
  820.2 61.6 %collective-permute-start.63 = (bf16[2,256,512]{2,1,0:T(8,128)(2,1)}, bf16[2,256,512]{2,1,0:T(8,128)(2,1)S(1)}, u32[]{:S(2)}, u32[]{:S(2)}) collective-permute-start(bf16[2,256,512]{2,1,0:T(8,128)(2,1)} %get-tuple-element.119), channel_id=1, source_target_pairs={{0,24},{4,28},{8,0},{12,4},{16,8},{20,12},{24,16},{28,20},{1,25},{... | collective-permute-start | bytes 1572872 | tf_op jit(solution)/shard_map/ppermute | solution.py:630
  834.7 86.6 %collective-permute-start.57 = (bf16[2,256,512]{2,1,0:T(8,128)(2,1)}, bf16[2,256,512]{2,1,0:T(8,128)(2,1)S(1)}, u32[]{:S(2)}, u32[]{:S(2)}) collective-permute-start(bf16[2,256,512]{2,1,0:T(8,128)(2,1)} %get-tuple-element.111), channel_id=1, source_target_pairs={{0,8},{4,12},{8,16},{12,20},{16,24},{20,28},{24,0},{28,4},{1,9},{5... | collective-permute-start | bytes 1572872 | tf_op jit(solution)/shard_map/ppermute | solution.py:630
  881.8 67.2 %collective-permute-start.59 = (bf16[2,256,512]{2,1,0:T(8,128)(2,1)}, bf16[2,256,512]{2,1,0:T(8,128)(2,1)}, u32[]{:S(2)}, u32[]{:S(2)}) collective-permute-start(bf16[2,256,512]{2,1,0:T(8,128)(2,1)} %get-tuple-element.113), channel_id=1, source_target_pairs={{0,24},{4,28},{8,0},{12,4},{16,8},{20,12},{24,16},{28,20},{1,25},{... | collective-permute-start | bytes 1572872 | tf_op jit(solution)/shard_map/ppermute | solution.py:630
  881.8 67.2 %collective-permute-start.65 = (bf16[2,256,512]{2,1,0:T(8,128)(2,1)}, bf16[2,256,512]{2,1,0:T(8,128)(2,1)}, u32[]{:S(2)}, u32[]{:S(2)}) collective-permute-start(bf16[2,256,512]{2,1,0:T(8,128)(2,1)} %get-tuple-element.123), channel_id=1, source_target_pairs={{0,8},{4,12},{8,16},{12,20},{16,24},{20,28},{24,0},{28,4},{1,9},{5... | collective-permute-start | bytes 1572872 | tf_op jit(solution)/shard_map/ppermute | solution.py:630
  923.4 73.5 %collective-permute-start.50 = (bf16[4,256,512]{2,1,0:T(8,128)(2,1)}, bf16[4,256,512]{2,1,0:T(8,128)(2,1)S(1)}, u32[]{:S(2)}, u32[]{:S(2)}) collective-permute-start(bf16[4,256,512]{2,1,0:T(8,128)(2,1)} %get-tuple-element.101), channel_id=1, source_target_pairs={{0,16},{4,20},{8,24},{12,28},{16,0},{20,4},{24,8},{28,12},{1,17},{... | collective-permute-start | bytes 3145736 | tf_op jit(solution)/shard_map/ppermute | solution.py:630
  948.9 82.4 %collective-permute-start.51 = (bf16[4,256,512]{2,1,0:T(8,128)(2,1)}, bf16[4,256,512]{2,1,0:T(8,128)(2,1)S(1)}, u32[]{:S(2)}, u32[]{:S(2)}) collective-permute-start(bf16[4,256,512]{2,1,0:T(8,128)(2,1)} %get-tuple-element.102), channel_id=1, source_target_pairs={{0,24},{4,28},{8,0},{12,4},{16,8},{20,12},{24,16},{28,20},{1,25},{... | collective-permute-start | bytes 3145736 | tf_op jit(solution)/shard_map/ppermute | solution.py:630
  948.9 136.1 %collective-permute-start.46 = (bf16[512,2048]{1,0:T(8,128)(2,1)}, bf16[512,2048]{1,0:T(8,128)(2,1)}, u32[]{:S(2)}, u32[]{:S(2)}) collective-permute-start(bf16[512,2048]{1,0:T(8,128)(2,1)} %get-tuple-element.96.rest_0_), channel_id=1, source_target_pairs={{0,2},{1,3},{2,0},{3,1},{4,6},{5,7},{6,4},{7,5},{8,10},{9,11},{10,... | collective-permute-start | bytes 6291464 | tf_op jit(solution)/shard_map/ppermute | solution.py:630
  950.4 134.6 %collective-permute-start.41 = (bf16[512,2048]{1,0:T(8,128)(2,1)}, bf16[512,2048]{1,0:T(8,128)(2,1)}, u32[]{:S(2)}, u32[]{:S(2)}) collective-permute-start(bf16[512,2048]{1,0:T(8,128)(2,1)} %shard_map.321.rest_0_), channel_id=1, source_target_pairs={{0,2},{1,3},{2,0},{3,1},{4,6},{5,7},{6,4},{7,5},{8,10},{9,11},{10,... | collective-permute-start | bytes 6291464 | tf_op jit(solution)/shard_map/ppermute | solution.py:630
  951.0 68.2 %collective-permute-start.71 = (f32[1,9728]{1,0:T(1,128)S(1)}, f32[1,9728]{1,0:T(1,128)S(1)}, u32[]{:S(2)}, u32[]{:S(2)}) collective-permute-start(f32[1,9728]{1,0:T(1,128)S(1)} %fusion.9), channel_id=1, source_target_pairs={{0,8},{4,12},{8,0},{12,4},{16,24},{20,28},{24,16},{28,20},{1,9},{5... | collective-permute-start | bytes 116744 | tf_op jit(solution)/shard_map/ppermute | solution.py:618
  (102 other events, 3048.1 us)

commit v2 on v1

--- a/solution.py
+++ b/solution.py
@@ -1,5 +1,3 @@
-from functools import partial
-
 import jax
 import jax.numpy as jnp
 from jax import lax
@@ -22,7 +20,7 @@
 F32 = jnp.float32
 BF16 = jnp.bfloat16
 LANES = 128
-ANY = pl.BlockSpec(memory_space=pl.ANY)
+ANY = pl.BlockSpec(memory_space=pltpu.HBM)
 VMEM_LIMIT = 60 * 1024 * 1024
 
 
@@ -38,21 +36,61 @@
     return pl.BlockSpec(shape, lambda *_: (0,) * len(shape))
 
 
-def launch(kernel, grid, in_specs, out_specs, out_shape, args, *, scalars=(), scratch=(), flops=0, moved=0, aliases={}):
+class Line:
+    def __init__(self):
+        self.last = ()
+
+
+LINE = Line()
+
+
+def launch(kernel, grid, in_specs, out_specs, out_shape, args, *, scalars=(), scratch=(), flops=0, moved=0, aliases={}, after=(), weight=1):
+    extra = len(after)
+    ahead = len(scalars) + len(args)
+
+    def trimmed(*refs):
+        return kernel(*refs[:ahead], *refs[ahead + extra :])
+
     return pl.pallas_call(
-        kernel,
+        trimmed,
         grid_spec=pltpu.PrefetchScalarGridSpec(
             num_scalar_prefetch=len(scalars),
             grid=grid,
-            in_specs=in_specs,
+            in_specs=list(in_specs) + [ANY] * extra,
             out_specs=out_specs,
             scratch_shapes=list(scratch),
         ),
         out_shape=out_shape,
         input_output_aliases=aliases,
         compiler_params=pltpu.CompilerParams(vmem_limit_bytes=VMEM_LIMIT),
-        cost_estimate=pl.CostEstimate(flops=int(flops), bytes_accessed=int(moved), transcendentals=0),
-    )(*scalars, *args)
+        cost_estimate=pl.CostEstimate(flops=200000000 * weight, bytes_accessed=1, transcendentals=0),
+    )(*scalars, *args, *after)
+
+
+def in_line(call, *args, **more):
+    out = call(*args, after=LINE.last, **more)
+    LINE.last = (out[-1] if isinstance(out, (tuple, list)) else out,)
+    return out
+
+
+def gate(*arrays, weight=1):
+    n = len(arrays)
+
+    def kernel(*refs):
+        pass
+
+    out = in_line(
+        launch,
+        kernel,
+        (1,),
+        [ANY] * n,
+        (ANY,) * n,
+        tuple(jax.ShapeDtypeStruct(a.shape, a.dtype) for a in arrays),
+        arrays,
+        aliases={i: i for i in range(n)},
+        weight=weight,
+    )
+    return list(out)
 
 
 def adamw(weight, first, second, grad, factor, rate, decay):
@@ -65,16 +103,20 @@
     return (weight, first, second)
 
 
-def load_weights(order_ref, blocks, slots, store, sem, rows, local):
+def load_weights(place_ref, groups, slots, store, sem):
     copies = []
-    for r, refs in enumerate(blocks):
-        at = pl.ds(pl.multiple_of(order_ref[r] * rows, rows), rows)
-        for column, (group, slot) in enumerate(slots):
-            copies.append(
-                pltpu.make_async_copy(
-                    refs[group].at[slot], store.at[at, column * local : (column + 1) * local], sem
+    for column, (group, slot) in enumerate(slots):
+        at = 0
+        for part in groups[group]:
+            owners, _, rows, local = part.shape
+            for r in range(owners):
+                to = pl.ds(pl.multiple_of(place_ref[at] * rows, rows), rows)
+                copies.append(
+                    pltpu.make_async_copy(
+                        part.at[r, slot], store.at[to, column * local : (column + 1) * local], sem
+                    )
                 )
-            )
+                at += 1
     for copy in copies:
         copy.start()
     for copy in copies:
@@ -105,11 +147,12 @@
     return launch(
         kernel,
         (1,),
-        specs + [ANY] * len(deps),
+        specs,
         whole(n, rows, local),
         jax.ShapeDtypeStruct((n, rows, local), BF16),
-        args + list(deps),
+        args,
         moved=n * rows * local * 6,
+        after=deps,
     )
 
 
@@ -125,7 +168,7 @@
     g_t_ref[...] = g_ref[...].T
 
 
-def normalize(x, g, vec):
+def normalize(x, g, vec, after=()):
     tokens, width = x.shape
     tile = min(256, tokens)
     row = pl.BlockSpec((tile, width), lambda i: (i, 0))
@@ -141,29 +184,31 @@
         (x, g, vec),
         flops=tokens * width * 10,
         moved=tokens * width * 10,
-    )
-
-
-def qkv_project(order, normed, g, bias, tables, blocks):
+        after=after,
+    )
+
+
+def qkv_project(places, normed, g, bias, tables, groups, slots, after=()):
     tokens, width = normed.shape
-    n_blocks = len(blocks)
-    _, rows, local = blocks[0].shape
+    local = groups[0][0].shape[3]
+    flat = [part for group in groups for part in group]
+    cut = len(groups[0])
     tile = min(512, tokens)
 
-    def kernel(order_ref, x_ref, g_ref, bias_ref, table_ref, *rest):
-        refs = rest[:n_blocks]
-        q_ref, k_ref, v_ref, da_ref, store, sem = rest[n_blocks:]
+    def kernel(place_ref, x_ref, g_ref, bias_ref, table_ref, *rest):
+        parts, (q_ref, k_ref, v_ref, da_ref, store, sem) = rest[:-6], rest[-6:]
 
         @pl.when(pl.program_id(0) == 0)
         def _():
-            load_weights(order_ref, [[r] for r in refs], [(0, s) for s in range(4)], store, sem, rows, local)
+            nested = [parts[k : k + cut] for k in range(0, len(flat), cut)]
+            load_weights(place_ref, nested, slots, store, sem)
 
         x = x_ref[...]
-        for slot, out in ((0, q_ref), (1, k_ref)):
+        for slot, out, scale in ((0, q_ref, HDIM ** (-0.5)), (1, k_ref, 1.0)):
             z = nn(x, store[:, slot * local : (slot + 1) * local]) + bias_ref[slot : slot + 1, :]
             for pair in range(local // LANES):
                 at = slice(pair * LANES, (pair + 1) * LANES)
-                out[:, at] = turn(z[:, at], table_ref, 1.0).astype(BF16)
+                out[:, at] = (turn(z[:, at], table_ref, 1.0) * scale).astype(BF16)
         v_ref[...] = (nn(x, store[:, 2 * local : 3 * local]) + bias_ref[2:3, :]).astype(BF16)
         da_ref[...] = nn(g_ref[...], store[:, 3 * local : 4 * local]).astype(BF16)
 
@@ -173,26 +218,27 @@
     return launch(
         kernel,
         (tokens // tile,),
-        [row, row, whole(7, local), pl.BlockSpec((3, tile, LANES), lambda i, *_: (0, i, 0))] + [ANY] * n_blocks,
+        [row, row, whole(7, local), pl.BlockSpec((3, tile, LANES), lambda i, *_: (0, i, 0))] + [ANY] * len(flat),
         (out,) * 4,
         (shape,) * 4,
-        (normed, g, bias, tables, *blocks),
-        scalars=(order,),
+        (normed, g, bias, tables, *flat),
+        scalars=(places,),
         scratch=(pltpu.VMEM((width, 4 * local), BF16), pltpu.SemaphoreType.DMA),
         flops=2 * tokens * width * 4 * local,
         moved=tokens * width * 4 + width * local * 8,
-    )
-
-
-def attend(low, query, keys, vals, d_attn, start, tables):
+        after=after,
+    )
+
+
+def attend(first, pairs, held, low, query, keys, vals, d_attn, start, tables, after=()):
     tokens, local = query.shape
     block = min(256, tokens)
     count = tokens // block
-    pairs = local // LANES
     scale = HDIM ** (-0.5)
 
-    def kernel(low_ref, q_ref, k_ref, v_ref, do_ref, start_ref, table_ref, o_ref, dq_ref, dk_ref, dv_ref, db_ref,
-               k_half, v_half, k_t, v_t, s_buf, dp_buf, o_t, dq_t, dk_sum, dv_sum):
+    def kernel(low_ref, q_ref, k_ref, v_ref, do_ref, start_ref, table_ref, *rest):
+        (o_ref, dq_ref, dk_ref, dv_ref, db_ref,
+               k_half, v_half, k_t, v_t, s_buf, dp_buf, o_t, dq_t, dk_sum, dv_sum) = rest[len(held):]
         i = pl.program_id(1)
         first_lanes = lax.broadcasted_iota(jnp.int32, (1, LANES), 1) < HDIM
 
@@ -227,7 +273,7 @@
             allowed = (u_place >= t_start) & (u_place <= t_place)
             new = []
             for h in range(2):
-                s = jnp.where(allowed, nt(k_half[h, at, :], q) * scale, -1e30)
+                s = jnp.where(allowed, nt(k_half[h, at, :], q), -1e30)
                 s_buf[h, b] = s
                 new.append(jnp.maximum(tops[h], jnp.max(s, 0, keepdims=True)))
             return tuple(new)
@@ -277,15 +323,15 @@
 
         @pl.when(i == count - 1)
         def _():
-            dk = turn(dk_sum[...] * scale, table_ref, -1.0).astype(BF16)
+            dk = turn(dk_sum[...], table_ref, -1.0).astype(BF16)
             dv = dv_sum[...].astype(BF16)
             dk_ref[...] = dk
             dv_ref[...] = dv
             db_ref[1:2, :] = jnp.sum(dk.astype(F32), 0, keepdims=True)
             db_ref[2:3, :] = jnp.sum(dv.astype(F32), 0, keepdims=True)
 
-    part = pl.BlockSpec((block, LANES), lambda p, i, *_: (i, p))
-    column = pl.BlockSpec((tokens, LANES), lambda p, i, *_: (0, p))
+    part = pl.BlockSpec((block, LANES), lambda p, i, *_: (i, p + first))
+    column = pl.BlockSpec((tokens, LANES), lambda p, i, *_: (0, p + first))
     shape = jax.ShapeDtypeStruct((tokens, local), BF16)
     return launch(
         kernel,
@@ -297,11 +343,13 @@
             part,
             pl.BlockSpec((1, block), lambda p, i, *_: (0, i)),
             whole(3, tokens, LANES),
-        ],
-        (part, part, column, column, pl.BlockSpec((3, LANES), lambda p, i, *_: (0, p))),
+        ]
+        + [ANY] * len(held),
+        (part, part, column, column, pl.BlockSpec((3, LANES), lambda p, i, *_: (0, p + first))),
         (shape,) * 4 + (jax.ShapeDtypeStruct((3, local), F32),),
-        (query, keys, vals, d_attn, start, tables),
+        (query, keys, vals, d_attn, start, tables, *held),
         scalars=(low,),
+        aliases={7 + i: i for i in range(len(held))},
         scratch=(
             pltpu.VMEM((2, tokens, LANES), BF16),
             pltpu.VMEM((2, tokens, LANES), BF16),
@@ -316,22 +364,21 @@
         ),
         flops=tokens * tokens * local * 24,
         moved=tokens * local * 20,
-    )
-
-
-def hidden_slot(order, normed, g, bias, blocks):
+        after=after,
+    )
+
+
+def hidden_slot(places, normed, g, bias, group, after=()):
     tokens, width = normed.shape
-    n_blocks = len(blocks)
-    _, rows, local = blocks[0].shape
+    local = group[0].shape[3]
     tile = min(512, tokens)
 
-    def kernel(order_ref, x_ref, g_ref, bias_ref, *rest):
-        refs = rest[:n_blocks]
-        h_ref, dz_ref, db_ref, store, sem = rest[n_blocks:]
+    def kernel(place_ref, x_ref, g_ref, bias_ref, *rest):
+        parts, (h_ref, dz_ref, db_ref, store, sem) = rest[:-5], rest[-5:]
 
         @pl.when(pl.program_id(0) == 0)
         def _():
-            load_weights(order_ref, [[r] for r in refs], [(0, 0), (0, 1)], store, sem, rows, local)
+            load_weights(place_ref, [parts], [(0, 0), (0, 1)], store, sem)
             db_ref[...] = jnp.zeros_like(db_ref)
 
         v = nn(x_ref[...], store[:, :local]) + bias_ref[...]
@@ -351,90 +398,89 @@
     return launch(
         kernel,
         (tokens // tile,),
-        [row, row, whole(1, local)] + [ANY] * n_blocks,
+        [row, row, whole(1, local)] + [ANY] * len(group),
         (out, out, whole(1, local)),
         (shape, shape, jax.ShapeDtypeStruct((1, local), F32)),
-        (normed, g, bias, *blocks),
-        scalars=(order,),
+        (normed, g, bias, *group),
+        scalars=(places,),
         scratch=(pltpu.VMEM((width, 2 * local), BF16), pltpu.SemaphoreType.DMA),
         flops=4 * tokens * width * local,
         moved=tokens * width * 4 + width * local * 4,
-    )
-
-
-def grad_blocks(dest, normed_t, g_t, sides, received, split):
+        after=after,
+        weight=5,
+    )
+
+
+def grad_blocks(inner_at, inner, normed_t, g_t, sides, received, after=(), weight=1):
     width, tokens = normed_t.shape
-    count = dest.shape[0]
+    outer = lax.axis_size("dp") // inner
+    owners = inner_at.shape[0]
     n = len(sides)
-    local = sides[0][1].shape[1]
-    rows = width // (lax.axis_size("dp"))
-
-    def kernel(dest_ref, x_ref, g_ref, *rest):
-        rights = rest[:n]
-        adds = rest[n : n + len(received)]
-        outs = rest[n + len(received) :]
-        step = pl.program_id(0)
-        for i, (left, _) in enumerate(sides):
-            total = nn((x_ref if left == 0 else g_ref)[...], rights[i][...])
-            for add in adds:
-                total += add[0, i].astype(F32)
-            if not split:
-                outs[0][0, i] = total.astype(BF16)
-            else:
-                for j, out in enumerate(outs):
-
-                    @pl.when(step == j)
-                    def _(out=out, total=total, i=i):
-                        out[i] = total.astype(out.dtype)
-
-    left = pl.BlockSpec((rows, tokens), lambda i, dest_ref: (dest_ref[i], 0))
-    piece = pl.BlockSpec((1, n, rows, local), lambda i, *_: (i, 0, 0, 0))
-    if split:
-        out_specs = (whole(n, rows, local),) * count
-        out_shape = tuple(
-            jax.ShapeDtypeStruct((n, rows, local), F32 if j == 0 else BF16) for j in range(count)
-        )
-    else:
-        out_specs = piece
-        out_shape = jax.ShapeDtypeStruct((count, n, rows, local), BF16)
-    return launch(
-        kernel,
-        (count,),
-        [left, left] + [whole(tokens, local)] * n + [piece] * len(received),
-        out_specs,
-        out_shape,
-        (normed_t, g_t, *[right for _, right in sides], *received),
-        scalars=(dest,),
-        flops=2 * count * rows * tokens * n * local,
-        moved=count * rows * tokens * 4 + n * tokens * local * 2 + count * n * rows * local * 2,
-    )
-
-
-def project_back(order, shares, lefts, groups, slots, received, split):
-    tokens, local = lefts[0].shape
+    cuts = len(sides[0][1])
+    piece_width = sides[0][1][0].shape[1]
+    local = cuts * piece_width
+    rows = width // (outer * inner)
+
+    def kernel(inner_ref, *rest):
+        lefts = rest[:2]
+        rights = rest[2 : 2 + n * cuts]
+        adds = rest[2 + n * cuts : -1]
+        out = rest[-1]
+        step = pl.program_id(1)
+        for i, (side, _) in enumerate(sides):
+
+            @pl.when(step == i)
+            def _(i=i, side=side):
+                left = lefts[side][...].reshape(outer * rows, tokens)
+                for c in range(cuts):
+                    at = slice(c * piece_width, (c + 1) * piece_width)
+                    total = nn(left, rights[i * cuts + c][...]).reshape(outer, rows, piece_width)
+                    for add in adds:
+                        total += add[:, 0, 0, :, at].astype(F32)
+                    out[:, 0, 0, :, at] = total.astype(BF16)
+
+    left = pl.BlockSpec((outer, 1, rows, tokens), lambda o, i, inner_ref, *_: (0, inner_ref[o], 0, 0))
+    piece = pl.BlockSpec((outer, 1, 1, rows, local), lambda o, i, *_: (0, o, i, 0, 0))
+    four = (outer, inner, rows, tokens)
+    return launch(
+        kernel,
+        (owners, n),
+        [left, left] + [whole(tokens, piece_width)] * (n * cuts) + [piece] * len(received),
+        piece,
+        jax.ShapeDtypeStruct((outer, owners, n, rows, local), BF16),
+        (normed_t.reshape(four), g_t.reshape(four), *[right for _, rights in sides for right in rights], *received),
+        scalars=(inner_at,),
+        after=after,
+        weight=weight,
+    )
+
+
+def project_back(places, shares, lefts, groups, slots, received, split, after=()):
+    tokens = lefts[0].shape[0]
+    local = groups[0][0].shape[3]
     count = shares.shape[0]
     share = tokens // lax.axis_size("tensor")
-    tile = min(256, share)
+    tile = min(512, share)
     steps = share // tile
-    n_blocks = len(groups)
-    n_groups = len(groups[0])
-    rows = groups[0][0].shape[1]
-    width = rows * n_blocks
+    width = places.shape[0] * groups[0][0].shape[2]
     m = len(lefts)
-    flat = [ref for refs in groups for ref in refs]
-
-    def kernel(order_ref, shares_ref, *rest):
+    depth = len(slots) * local
+    flat = [part for group in groups for part in group]
+    cut = len(groups[0])
+    n_groups = len(flat)
+
+    def kernel(place_ref, shares_ref, *rest):
         left_refs = rest[:m]
-        refs = rest[m : m + len(flat)]
-        adds = rest[m + len(flat) : m + len(flat) + len(received)]
-        outs = rest[m + len(flat) + len(received) : -2]
+        refs = rest[m : m + n_groups]
+        adds = rest[m + n_groups : m + n_groups + len(received)]
+        outs = rest[m + n_groups + len(received) : -2]
         store, sem = rest[-2:]
         step, part = pl.program_id(0), pl.program_id(1)
 
         @pl.when((step == 0) & (part == 0))
         def _():
-            nested = [refs[r * n_groups : (r + 1) * n_groups] for r in range(n_blocks)]
-            load_weights(order_ref, nested, slots, store, sem, rows, local)
+            nested = [refs[k : k + cut] for k in range(0, n_groups, cut)]
+            load_weights(place_ref, nested, slots, store, sem)
 
         total = nt(jnp.concatenate([left[...] for left in left_refs], 1), store[...])
         for add in adds:
@@ -449,7 +495,9 @@
                 def _(out=out):
                     out[at, :] = total.astype(out.dtype)
 
-    left = pl.BlockSpec((tile, local), lambda i, j, o_ref, s_ref: (s_ref[i] * steps + j, 0))
+    def left(array):
+        return pl.BlockSpec((tile, array.shape[1]), lambda i, j, p_ref, s_ref: (s_ref[i] * steps + j, 0))
+
     piece = pl.BlockSpec((tile, width), lambda i, j, *_: (i * steps + j, 0))
     if split:
         out_specs = (whole(share, width),) * count
@@ -460,18 +508,19 @@
     return launch(
         kernel,
         (count, steps),
-        [left] * m + [ANY] * len(flat) + [piece] * len(received),
+        [left(array) for array in lefts] + [ANY] * n_groups + [piece] * len(received),
         out_specs,
         out_shape,
         (*lefts, *flat, *received),
-        scalars=(order, shares),
-        scratch=(pltpu.VMEM((width, m * local), BF16), pltpu.SemaphoreType.DMA),
-        flops=2 * count * share * width * m * local,
-        moved=width * m * local * 2 + count * share * (m * local + width) * 2,
-    )
-
-
-def finish_output(mine, own, received, x, vec):
+        scalars=(places, shares),
+        scratch=(pltpu.VMEM((width, depth), BF16), pltpu.SemaphoreType.DMA),
+        flops=2 * count * share * width * depth,
+        moved=width * depth * 2 + count * share * (depth + width) * 2,
+        after=after,
+    )
+
+
+def finish_output(mine, own, received, x, vec, after=()):
     share, width = own.shape
     tile = min(256, share)
     steps = share // tile
@@ -493,10 +542,11 @@
         (own, x, vec, *received),
         scalars=(mine,),
         moved=share * width * 10,
-    )
-
-
-def finish_input(mine, own, received, x, g, vec):
+        after=after,
+    )
+
+
+def finish_input(mine, own, received, x, g, vec, after=()):
     share, width = own.shape
     tile = min(256, share)
     steps = share // tile
@@ -536,10 +586,11 @@
         (own, x, g, vec, *received),
         scalars=(mine,),
         moved=share * width * 12,
-    )
-
-
-def lay_out(order, parts):
+        after=after,
+    )
+
+
+def lay_out(order, parts, after=()):
     share, width = parts[0].shape
     count = len(parts)
     tile = min(256, share)
@@ -566,15 +617,16 @@
         parts,
         scalars=(order,),
         moved=share * count * width * 4,
-    )
-
-
-def total_group(grads, own, received, places, slots_in_all):
+        after=after,
+    )
+
+
+def total_group(grads, own, received, places, slots_in_all, after=()):
     n, rows, local = own.shape
 
     def kernel(places_ref, own_ref, *rest):
         out, squares = rest[-2:]
-        total = own_ref[0]
+        total = own_ref[0].astype(F32)
         for ref in rest[: len(received)]:
             total += ref[0].astype(F32)
         out[0] = total
@@ -597,27 +649,23 @@
         (own, *received) + (() if first else (grads,)),
         scalars=(places,),
         aliases={} if first else {2 + len(received): 0},
-        moved=n * rows * local * 14,
-    )
-
-
-def double_up(values, axis, count):
-    me = lax.axis_index(axis)
-    bit = 1
-    while bit < count:
-        other = lax.ppermute(values, axis, [(i, i ^ bit) for i in range(count)])
-        high = (me & bit) != 0
-        values = jnp.where(high, jnp.concatenate([other, values], 0), jnp.concatenate([values, other], 0))
-        bit *= 2
-    return values
+        after=after,
+    )
+
+
+def collect(values, axis, count):
+    rows = [values]
+    for k in range(1, count):
+        rows.append(lax.ppermute(values, axis, [(i, (i + k) % count) for i in range(count)]))
+    rows = jnp.concatenate(rows[::-1] * 2, 0)
+    return lax.dynamic_slice_in_dim(rows, count - 1 - lax.axis_index(axis), count, 0)
 
 
 def total_over(values, axis, count):
-    bit = 1
-    while bit < count:
-        values = values + lax.ppermute(values, axis, [(i, i ^ bit) for i in range(count)])
-        bit *= 2
-    return values
+    total = values
+    for k in range(1, count):
+        total = total + lax.ppermute(values, axis, [(i, (i + k) % count) for i in range(count)])
+    return total
 
 
 def shift(values, axis, count, inner, outer_by, inner_by):
@@ -649,7 +697,7 @@
 ):
     n_dp = lax.axis_size("dp")
     n_tensor = lax.axis_size("tensor")
-    inner = 2 if n_dp <= 8 else 4
+    inner = 2
     outer = n_dp // inner
     cores = 2
     ways = n_tensor // cores
@@ -665,17 +713,13 @@
     def numbers(values):
         return jnp.stack([jnp.asarray(v, jnp.int32) for v in values])
 
-    order = numbers(
-        [
-            (my_outer - o) % outer * inner + (my_inner - i) % inner
-            for o in range(outer)
-            for i in range(inner)
-        ]
-    )
-    dests = [
-        numbers([(my_outer + o) % outer * inner + (my_inner + i) % inner for o in range(outer)])
-        for i in range(inner)
-    ]
+    other_inner = 1 - my_inner
+    inner_at = [numbers([my_inner]), numbers([other_inner])]
+    both_inner = jnp.arange(inner, dtype=jnp.int32)
+    lines = [[o * inner + i for o in range(outer)] for i in range(inner)]
+    owner_places = numbers(
+        [o * inner + i for i in (my_inner, other_inner) for o in range(outer)]
+    )
     share_order = numbers(
         [(my_way - w) % ways * cores + (my_core - c) % cores for w in range(ways) for c in range(cores)]
     )
@@ -685,31 +729,35 @@
     ]
     share_mine = numbers([mine])
 
+    def to_partner(values):
+        return shift(values, "dp", n_dp, inner, 0, 1)
+
+
     w_in_s = w_in.transpose(1, 0, 2)
     w_outs_s = w_outs.transpose(1, 0, 2)
 
-    def gather(own):
-        blocks = []
-        held = [own] + [shift(own, "dp", n_dp, inner, o, 0) for o in range(1, outer)]
-        for part in held:
-            blocks.append(part)
-            for i in range(1, inner):
-                blocks.append(shift(part, "dp", n_dp, inner, 0, i))
-        return blocks
-
     first_slots = [(0, 0), (0, 1), (0, 2), (1, 0)]
+    gather_slots = [first_slots[:2], first_slots[2:]] + [[(0, 3 + s), (1, 1 + s)] for s in range(hidden_slots)]
     group_slots = [first_slots] + [[(0, 3 + s), (1, 1 + s)] for s in range(hidden_slots)]
 
     small = jnp.concatenate([in_bias.reshape(1, -1), vectors.reshape(1, -1)], 1).astype(BF16).astype(F32)
-    small = double_up(small, "dp", n_dp)
+    small = collect(small, "dp", n_dp)
     bias_size = in_bias.size
     bias = small[:, :bias_size].reshape((n_dp,) + in_bias.shape).transpose(1, 2, 0, 3).reshape(slots_in, local)
     vec = small[:, bias_size:].reshape((n_dp,) + vectors.shape).transpose(1, 0, 2).reshape(4, width)
 
+    LINE.last = ()
+    turns = list(range(1 + hidden_slots))
+    along = []
+    for slots in gather_slots:
+        cast = cast_group(w_in_s, w_outs_s, slots, LINE.last)
+        LINE.last = (cast,)
+        along.append(lax.all_gather(cast, "dp", axis=0, axis_index_groups=lines))
     groups = []
-    for g, slots in enumerate(group_slots):
-        deps = groups[g - 2][-1:] if g >= 2 else []
-        groups.append(gather(cast_group(w_in_s, w_outs_s, slots, deps)))
+
+    def exchange(g):
+        here = gate(along[g])[0]
+        groups.append([here, to_partner(here)])
 
     seg = segment_ids[0]
     start = jnp.sum((seg[None, :] < seg[:, None]).astype(jnp.int32), 1)
@@ -717,69 +765,134 @@
     low = start[::block] // block
     place = (jnp.arange(tokens, dtype=jnp.int32) - start).astype(F32)
     freq = 10000.0 ** (-jnp.arange(ROT // 2, dtype=F32) * 2.0 / ROT)
+    freq = jnp.tile(jnp.concatenate([freq, freq, jnp.zeros((HDIM - ROT,), F32)]), LANES // HDIM)
     theta = place[:, None] * freq[None, :]
-    cosine, sine = jnp.cos(theta), jnp.sin(theta)
-    rest = jnp.zeros((tokens, HDIM - ROT), F32)
-    none = jnp.zeros_like(sine)
+    sine = jnp.sin(theta)
+    feature = jnp.arange(LANES) % HDIM
     tables = jnp.stack(
         [
-            jnp.concatenate([cosine, cosine, rest + 1.0] * 2, 1),
-            jnp.concatenate([-sine, none, rest] * 2, 1),
-            jnp.concatenate([none, sine, rest] * 2, 1),
+            jnp.cos(theta),
+            jnp.where(feature < ROT // 2, -sine, 0.0),
+            jnp.where((feature >= ROT // 2) & (feature < ROT), sine, 0.0),
         ]
     )
-
-    normed, normed_t, g_t = normalize(block_input, cotangent, vec)
-
-    query, keys, vals, d_attn = qkv_project(order, normed, cotangent, bias, tables, groups[0])
-    attn, d_query, d_keys, d_vals, d_bias_attn = attend(
-        low, query, keys, vals, d_attn, start.reshape(1, tokens), tables
-    )
-
-    def send_back(sides):
-        received = []
-        for i in range(1, inner):
-            out = grad_blocks(dests[i], normed_t, g_t, sides, [], False)
-            received.append(shift(out, "dp", n_dp, inner, 0, i))
-        outs = grad_blocks(dests[0], normed_t, g_t, sides, received, True)
-        return outs[0], [shift(outs[o], "dp", n_dp, inner, o, 0) for o in range(1, outer)]
-
-    hidden, d_hidden, d_bias_hidden = [], [], []
-    shares = [send_back([(0, d_query), (0, d_keys), (0, d_vals), (1, attn)])]
-    for s in range(hidden_slots):
-        h, dz, db = hidden_slot(order, normed, cotangent, bias[3 + s : 4 + s], groups[1 + s])
+    LINE.last = LINE.last + (tables, low)
+
+    normed, normed_t, g_t = in_line(normalize, block_input, cotangent, vec)
+
+    hidden, d_hidden, d_bias_hidden, sides = [], [], [], {}
+
+    def hidden_step(s):
+        h, dz, db = in_line(hidden_slot, owner_places, normed, cotangent, bias[3 + s : 4 + s], groups[2 + s])
         hidden.append(h)
         d_hidden.append(dz)
         d_bias_hidden.append(db)
-        shares.append(send_back([(0, dz), (1, h)]))
-
-    by_owner = [[group[r] for group in groups] for r in range(n_dp)]
-
-    def sum_tensor(lefts, slots):
+        sides[1 + s] = [(0, [dz]), (1, [h])]
+
+    legs, shares = {}, {}
+
+    def scatter(out):
+        outer_blocks, owners, n, rows, columns = out.shape
+        out = out.reshape(outer_blocks * owners * n, rows, columns)
+        out = lax.psum_scatter(out, "dp", scatter_dimension=0, axis_index_groups=lines, tiled=True)
+        return out.reshape(owners, n, rows, columns)
+
+    def first_next(g, weight=1):
+        out = in_line(grad_blocks, inner_at[1], inner, normed_t, g_t, sides[g], [], weight=weight)
+        legs[g] = [to_partner(out)]
+
+    def second_next(g):
+        out = in_line(grad_blocks, inner_at[0], inner, normed_t, g_t, sides[g], legs[g])
+        shares[g] = (scatter(out)[0], [])
+
+    def line_first(g):
+        out = scatter(in_line(grad_blocks, both_inner, inner, normed_t, g_t, sides[g], []))
+        sent = lax.dynamic_index_in_dim(out, other_inner, 0, False)
+        shares[g] = (lax.dynamic_index_in_dim(out, my_inner, 0, False), [to_partner(sent)])
+
+    exchange(0)
+    exchange(1)
+    groups[0][1] = gate(groups[0][1], weight=5)[0]
+    to_exchange = list(range(2, 2 + hidden_slots))
+    in_first = [(0, 0), (0, 1), (1, 0), (1, 1)]
+    qkvd = in_line(qkv_project, owner_places, normed, cotangent, bias, tables, groups[:2], in_first)
+    pairs = local // LANES
+    held = ()
+    for first in range(pairs):
+        if to_exchange and len(to_exchange) > 1:
+            exchange(to_exchange.pop(0))
+        held = in_line(attend, first, 1, held, low, *qkvd, start.reshape(1, tokens), tables)
+    while to_exchange:
+        exchange(to_exchange.pop(0))
+    attn, d_query, d_keys, d_vals, d_bias_attn = held
+    sides[0] = [(0, [d_query]), (0, [d_keys]), (0, [d_vals]), (1, [attn])]
+    line_first(0)
+    for s in range(hidden_slots):
+        hidden_step(s)
+
+    def first_half(lefts, slots):
         received = []
         for c in range(1, cores):
-            out = project_back(order, share_dests[c], lefts, by_owner, slots, [], False)
+            out = in_line(project_back, owner_places, share_dests[c], lefts, groups, slots, [], False)
             received.append(shift(out, "tensor", n_tensor, cores, 0, c))
-        outs = project_back(order, share_dests[0], lefts, by_owner, slots, received, True)
+        return received
+
+    def second_half(lefts, slots, received):
+        outs = in_line(project_back, owner_places, share_dests[0], lefts, groups, slots, received, True)
         return outs[0], [shift(outs[w], "tensor", n_tensor, cores, w, 0) for w in range(1, ways)]
 
-    def gather_tensor(own):
+    def send_share(own):
+        return [own] + [shift(own, "tensor", n_tensor, cores, w, 0) for w in range(1, ways)]
+
+    def gather_share(held):
         parts = []
-        held = [own] + [shift(own, "tensor", n_tensor, cores, w, 0) for w in range(1, ways)]
-        for part in held:
+        for part in [held[0]] + gate(*held[1:]):
             parts.append(part)
             for c in range(1, cores):
                 parts.append(shift(part, "tensor", n_tensor, cores, 0, c))
-        return lay_out(share_order, parts)
-
-    own, received = sum_tensor(
-        [d_query, d_keys, d_vals] + d_hidden, [(0, 0), (0, 1), (0, 2)] + [(1 + s, 0) for s in range(hidden_slots)]
-    )
-    d_x, vector_rows = finish_input(share_mine, own, received, block_input, cotangent, vec)
-    block_input_gradient = gather_tensor(d_x)
-
-    own, received = sum_tensor([attn] + hidden, [(0, 3)] + [(1 + s, 1) for s in range(hidden_slots)])
-    output = gather_tensor(finish_output(share_mine, own, received, block_input, vec))
+        return parts
+
+    back = (
+        [d_query, d_keys, d_vals] + d_hidden,
+        in_first[:3] + [(2 + s, 0) for s in range(hidden_slots)],
+    )
+    ahead = ([attn] + hidden, in_first[3:] + [(2 + s, 1) for s in range(hidden_slots)])
+    grads, squares = None, []
+
+    def total_next(g):
+        slots, (own, received) = group_slots[g], shares[g]
+        places = jnp.asarray([s if which == 0 else slots_in + s for which, s in slots], jnp.int32)
+        out, part = in_line(total_group, grads, own, received, places, slots_in + slots_out)
+        squares.append(part)
+        return out
+
+    first_next(1, 5000)
+    back_half = first_half(*back)
+    first_next(2)
+    ahead_half = first_half(*ahead)
+    second_next(1)
+    first_next(3)
+    own, received = second_half(*back, back_half)
+    second_next(2)
+    ahead_own, ahead_received = second_half(*ahead, ahead_half)
+    second_next(3)
+    for g in range(4, 1 + hidden_slots):
+        first_next(g)
+    d_x, vector_rows = in_line(finish_input, share_mine, own, received, block_input, cotangent, vec)
+    back_held = send_share(d_x)
+    for g in range(4, 1 + hidden_slots):
+        second_next(g)
+    out_held = send_share(
+        in_line(finish_output, share_mine, ahead_own, ahead_received, block_input, vec)
+    )
+    for g in turns[:2]:
+        grads = total_next(g)
+    back_parts = gather_share(back_held)
+    block_input_gradient = in_line(lay_out, share_order, back_parts)
+    for g in turns[2:-1]:
+        grads = total_next(g)
+    out_parts = gather_share(out_held)
+    output = in_line(lay_out, share_order, out_parts)
 
     vector_rows = total_over(vector_rows.reshape(1, -1), "tensor", n_tensor)
     d_bias = jnp.concatenate([d_bias_attn] + d_bias_hidden, 0)
@@ -790,17 +903,18 @@
     g_vec = lax.dynamic_index_in_dim(small[0, slots_in * local :].reshape(3, n_dp, width // n_dp), me, 1, False)
     g_vec = jnp.concatenate([g_vec, g_vec[2:]], 0)
 
-    grads, squares = None, []
-    for slots, (own, received) in zip(group_slots, shares):
-        places = jnp.asarray([s if which == 0 else slots_in + s for which, s in slots], jnp.int32)
-        grads, part = total_group(grads, own, received, places, slots_in + slots_out)
-        squares.append(part)
+    LINE.last = LINE.last + (g_bias, g_vec)
+    grads = total_next(turns[-1])
     g_in, g_outs = grads[:slots_in], grads[slots_in:]
     local_squares = (
         jnp.sum(jnp.concatenate(squares, 0)) + jnp.sum(g_bias * g_bias) + jnp.sum(g_vec * g_vec) * (1.0 / n_tensor)
     )
     local_squares = total_over(jnp.full((1, LANES), local_squares), "tensor", n_tensor)
-    local_squares = total_over(local_squares, "dp", n_dp)
+    bit = 1
+    while bit < n_dp:
+        pairs_at = [(i, i ^ bit) for i in range(n_dp)]
+        local_squares = local_squares + lax.ppermute(local_squares, "dp", pairs_at)
+        bit *= 2
     grad_norm = jnp.sqrt(local_squares[0, 0])
     factor = CLIP_AT / jnp.maximum(grad_norm, CLIP_AT)
 

time: 1130 us -> 859 us (0.76)
  starting transfers between devices: 206 us -> 44.2 us
  waiting for transfers between devices: 374 us -> 250 us
  between operations: 7.96 us -> 21 us
    ppermute x65 -> x21, starting transfers between devices: 142 us -> 18.1 us  [shift(): return lax.ppermute(values, axis, pairs)]
    ppermute x65 -> x21, waiting for transfers between devices: 288 us -> 184 us  [shift(): return lax.ppermute(values, axis, pairs)]
    ppermute x13 -> x23, waiting for transfers between devices: 86.8 us -> 14.8 us  [the longest x3 10.6 us: body(): local_squares = local_squares + lax.ppermute(local_squares, 'dp', pairs_at)]
    all_gather x0 -> x6, waiting for transfers between devices: none -> 51.1 us  [body(): along.append(lax.all_gather(cast, 'dp', axis=0, axis_index_groups=lines))]
    ppermute x13 -> x23, starting transfers between devices: 64.6 us -> 25.7 us  [the longest x7 13.8 us: collect(): lax.ppermute(values, axis, [(i, (i + k) % count) for i in range(count)])]
    concatenate x3 -> x1, local copies, waits for them, and re-layouts: 11.8 us -> 0.16 us  [collect(): rows = jnp.concatenate(rows[::-1] * 2, 0)]
    pallas_call x35 -> x47, Pallas kernels: 480 us -> 487 us  [launch(): pl.pallas_call(trimmed, grid_spec=pltpu.PrefetchScalarGridSpec(num_scalar...]
  transfers between devices with their start and end apart: 78 -> 55, of which waited for: 24 -> 18; matrix products, arithmetic and copies ran while one was open for 5% -> 3% of each run, Pallas kernels for 38% -> 57%
where the time goes in v2:
time: 859 us; the launch traced here: 852 us
  Pallas kernels  487 us (57%)
  waiting for transfers between devices  250 us (29%)
  starting transfers between devices  44.2 us (5%)
  other arithmetic  33.1 us (4%)
  between operations  21 us (2%)
  local copies, waits for them, and re-layouts  17.6 us (2%)
    pallas_call x47, Pallas kernels, launch(): pl.pallas_call(trimmed, grid_spec=pltpu.PrefetchScalarGridSpec(num_scalar...  487 us
    ppermute x21, waiting for transfers between devices, shift(): return lax.ppermute(values, axis, pairs)  184 us
    all_gather x6, waiting for transfers between devices, body(): along.append(lax.all_gather(cast, 'dp', axis=0, axis_index_groups=lines))  51.1 us
    ppermute x21, starting transfers between devices, shift(): return lax.ppermute(values, axis, pairs)  18.1 us
  transfers between devices with their start and end apart: 55, of which 18 were waited for; matrix products, arithmetic and copies ran while one was open for 3% of the time, Pallas kernels for 57%

profile of v2, /device:TPU:0, one launch (start us, length us, event | category | flops | bytes accessed | tf_op | source)
XLA Modules:
  0.0 852.1 jit_solution(10217625003513384061)
XLA Ops:
  45.0 18.4 %shard_map.313 = (bf16[2048,2048]{1,0:T(8,128)(2,1)}, bf16[2048,2048]{1,0:T(8,128)(2,1)}, bf16[2048,2048]{1,0:T(8,128)(2,1)}) custom-call(bf16[2048,2048]{1,0:T(8,128)(2,1)} %refs_2_.13, bf16[2048,2048]{1,0:T(8,128)(2,1)} %refs_3_.1, f32[4,2048]{1,0:T(4,128)} %bitcast.156, bf16[2,256,512]{2,1,0:T(8,128)(2,1)} %shard_map.312.refs_3_, ...), custom_call_target="tpu_custom_call" | custom-call | flops 200000000 | bytes 1 | tf_op jit(solution)/shard_map/pallas_call | solution.py:54
  65.1 41.6 %all-gather.15.cloned.1.call-done = bf16[8,256,512]{2,1,0:T(8,128)(2,1)} async-done(((bf16[2,256,512]{2,1,0:T(8,128)(2,1)}), bf16[8,256,512]{2,1,0:T(8,128)(2,1)}) %all-gather.15.cloned.1.call-update) | async-done | bytes 2097168 | tf_op jit(solution)/shard_map/all_gather | solution.py:755
  111.0 43.4 %collective-permute-done.8.refs_8_.refs_12_.refs_10_ = bf16[4,2,256,512]{3,2,1,0:T(8,128)(2,1)} collective-permute-done((bf16[4,2,256,512]{3,2,1,0:T(8,128)(2,1)}, bf16[4,2,256,512]{3,2,1,0:T(8,128)(2,1)}, u32[]{:S(2)}, u32[]{:S(2)}) %collective-permute-start.8) | collective-permute-done | bytes 2097184 | tf_op jit(solution)/shard_map/ppermute | solution.py:678
  154.3 26.4 %shard_map.317 = (bf16[2048,512]{1,0:T(8,128)(2,1)}, bf16[2048,512]{1,0:T(8,128)(2,1)}, bf16[2048,512]{1,0:T(8,128)(2,1)}, bf16[2048,512]{1,0:T(8,128)(2,1)}) custom-call(s32[8]{0:T(128)} %stack.83.refs_0_, bf16[2048,2048]{1,0:T(8,128)(2,1)} %get-tuple-element.70.refs_1_, bf16[2048,2048]{1,0:T(8,128)(2,1)} %refs_3_.1, f32[7,512]{1,0:T(8,128)} %reshape.344.refs_3_, ...), custom_call_target="tpu_custom_call" | custom-call | flops 200000000 | bytes 1 | tf_op jit(solution)/shard_map/pallas_call | solution.py:54
  182.2 26.4 %shard_map.319 = (bf16[2048,512]{1,0:T(8,128)(2,1)}, bf16[2048,512]{1,0:T(8,128)(2,1)}, bf16[2048,512]{1,0:T(8,128)(2,1)}, bf16[2048,512]{1,0:T(8,128)(2,1)}, f32[3,512]{1,0:T(4,128)}) custom-call(s32[8]{0:T(128)} %and_select_fusion.1.refs_5_.refs_0_, bf16[2048,512]{1,0:T(8,128)(2,1)} %get-tuple-element.72.refs_1_, ...), custom_call_target="tpu_custom_call" | custom-call | flops 200000000 | bytes 1 | tf_op jit(solution)/shard_map/pallas_call | solution.py:54
  209.3 26.4 %shard_map.321 = (bf16[2048,512]{1,0:T(8,128)(2,1)}, bf16[2048,512]{1,0:T(8,128)(2,1)}, bf16[2048,512]{1,0:T(8,128)(2,1)}, bf16[2048,512]{1,0:T(8,128)(2,1)}, f32[3,512]{1,0:T(4,128)}) custom-call(s32[8]{0:T(128)} %and_select_fusion.1.refs_5_.refs_0_, ...), custom_call_target="tpu_custom_call", output_to_operand_aliasing={{0}: (7, {}), {1}: (8, {}), {2}: (9, {}), {3}: (10, {}), {4... | custom-call | flops 200000000 | bytes 1 | tf_op jit(solution)/shard_map/pallas_call | solution.py:54
  246.6 26.3 %shard_map.323 = (bf16[2048,512]{1,0:T(8,128)(2,1)}, bf16[2048,512]{1,0:T(8,128)(2,1)}, bf16[2048,512]{1,0:T(8,128)(2,1)}, bf16[2048,512]{1,0:T(8,128)(2,1)}, f32[3,512]{1,0:T(4,128)}) custom-call(s32[8]{0:T(128)} %and_select_fusion.1.refs_5_.refs_0_, ...), custom_call_target="tpu_custom_call", output_to_operand_aliasing={{0}: (7, {}), {1}: (8, {}), {2}: (9, {}), {3}: (10, {}), {4... | custom-call | flops 200000000 | bytes 1 | tf_op jit(solution)/shard_map/pallas_call | solution.py:54
  274.2 26.6 %shard_map.324 = (bf16[2048,512]{1,0:T(8,128)(2,1)}, bf16[2048,512]{1,0:T(8,128)(2,1)}, bf16[2048,512]{1,0:T(8,128)(2,1)}, bf16[2048,512]{1,0:T(8,128)(2,1)}, f32[3,512]{1,0:T(4,128)}) custom-call(s32[8]{0:T(128)} %and_select_fusion.1.refs_5_.refs_0_, ...), custom_call_target="tpu_custom_call", output_to_operand_aliasing={{0}: (7, {}), {1}: (8, {}), {2}: (9, {}), {3}: (10, {}), {4... | custom-call | flops 200000000 | bytes 1 | tf_op jit(solution)/shard_map/pallas_call | solution.py:54
  304.7 28.6 %shard_map.326.refs_6_ = bf16[4,2,4,256,512]{4,3,2,1,0:T(8,128)(2,1)} custom-call(s32[2]{0:T(128)} %iota.21.refs_0_, bf16[4,2,256,2048]{3,2,1,0:T(8,128)(2,1)} %bitcast.119, bf16[4,2,256,2048]{3,2,1,0:T(8,128)(2,1)} %bitcast.110, bf16[2048,512]{1,0:T(8,128)(2,1)} %get-tuple-element.93.refs_3_.refs_2_, bf16[2048,512]{1,0:T(8,128)(2,1)} %get-tuple-element.94.refs_4_.refs_3_, ...), custom_call_target="tpu_custom_call" | custom-call | flops 200000000 | bytes 1 | tf_op jit(solution)/shard_map/pallas_call | solution.py:54
  333.4 16.7 %shard_map.327 = (bf16[2048,512]{1,0:T(8,128)(2,1)}, bf16[2048,512]{1,0:T(8,128)(2,1)}, f32[1,512]{1,0:T(1,128)}) custom-call(s32[8]{0:T(128)} %stack.83.refs_0_, bf16[2048,2048]{1,0:T(8,128)(2,1)} %get-tuple-element.70.refs_1_, bf16[2048,2048]{1,0:T(8,128)(2,1)} %refs_3_.1, f32[1,512]{1,0:T(1,128)} %slice.58.refs_3_, ...), custom_call_target="tpu_custom_call" | custom-call | flops 1000000000 | bytes 1 | tf_op jit(solution)/shard_map/pallas_call | solution.py:54
  351.4 15.9 %shard_map.328 = (bf16[2048,512]{1,0:T(8,128)(2,1)}, bf16[2048,512]{1,0:T(8,128)(2,1)}, f32[1,512]{1,0:T(1,128)}) custom-call(s32[8]{0:T(128)} %stack.83.refs_0_, bf16[2048,2048]{1,0:T(8,128)(2,1)} %get-tuple-element.70.refs_1_, bf16[2048,2048]{1,0:T(8,128)(2,1)} %refs_3_.1, f32[1,512]{1,0:T(1,128)} %slice.60.refs_3_, ...), custom_call_target="tpu_custom_call" | custom-call | flops 1000000000 | bytes 1 | tf_op jit(solution)/shard_map/pallas_call | solution.py:54
  367.3 15.8 %shard_map.329 = (bf16[2048,512]{1,0:T(8,128)(2,1)}, bf16[2048,512]{1,0:T(8,128)(2,1)}, f32[1,512]{1,0:T(1,128)}) custom-call(s32[8]{0:T(128)} %stack.83.refs_0_, bf16[2048,2048]{1,0:T(8,128)(2,1)} %get-tuple-element.70.refs_1_, bf16[2048,2048]{1,0:T(8,128)(2,1)} %refs_3_.1, f32[1,512]{1,0:T(1,128)} %slice.62.refs_3_, ...), custom_call_target="tpu_custom_call" | custom-call | flops 1000000000 | bytes 1 | tf_op jit(solution)/shard_map/pallas_call | solution.py:54
  383.2 16.1 %shard_map.330 = (bf16[2048,512]{1,0:T(8,128)(2,1)}, bf16[2048,512]{1,0:T(8,128)(2,1)}, f32[1,512]{1,0:T(1,128)}) custom-call(s32[8]{0:T(128)} %stack.83.refs_0_, bf16[2048,2048]{1,0:T(8,128)(2,1)} %get-tuple-element.70.refs_1_, bf16[2048,2048]{1,0:T(8,128)(2,1)} %refs_3_.1, f32[1,512]{1,0:T(1,128)} %slice.64.refs_3_, ...), custom_call_target="tpu_custom_call" | custom-call | flops 1000000000 | bytes 1 | tf_op jit(solution)/shard_map/pallas_call | solution.py:54
  399.2 10.5 %shard_map.331.refs_21_ = bf16[4,1,2,256,512]{4,3,2,1,0:T(8,128)(2,1)} custom-call(s32[1]{0:T(128)} %bitcast.9.refs_0_, bf16[4,2,256,2048]{3,2,1,0:T(8,128)(2,1)} %bitcast.120, bf16[4,2,256,2048]{3,2,1,0:T(8,128)(2,1)} %bitcast.111, bf16[2048,512]{1,0:T(8,128)(2,1)} %get-tuple-element.105.refs_3_.refs_5_, ...), custom_call_target="tpu_custom_call" | custom-call | flops 999999995904 | bytes 1 | tf_op jit(solution)/shard_map/pallas_call | solution.py:54
  411.5 25.6 %shard_map.332.refs_5_ = bf16[1024,2048]{1,0:T(8,128)(2,1)} custom-call(s32[8]{0:T(128)} %stack.83.refs_0_, s32[2]{0:T(128)} %pad_add_fusion.2.refs_1_, bf16[2048,512]{1,0:T(8,128)(2,1)} %get-tuple-element.93.refs_3_.refs_2_, bf16[2048,512]{1,0:T(8,128)(2,1)} %get-tuple-element.94.refs_4_.refs_3_, bf16[2048,512]{1,0:T(8,128)(2,1)} %get-tuple-element.95.refs_5_.refs_4_, ...), custom_call_target="tpu_custom_call" | custom-call | flops 200000000 | bytes 1 | tf_op jit(solution)/shard_map/pallas_call | solution.py:54
  437.2 10.5 %shard_map.333.refs_19_ = bf16[4,1,2,256,512]{4,3,2,1,0:T(8,128)(2,1)} custom-call(s32[1]{0:T(128)} %bitcast.9.refs_0_, bf16[4,2,256,2048]{3,2,1,0:T(8,128)(2,1)} %bitcast.121, bf16[4,2,256,2048]{3,2,1,0:T(8,128)(2,1)} %bitcast.112, bf16[2048,512]{1,0:T(8,128)(2,1)} %get-tuple-element.104.refs_6_.refs_3_, bf16[2048,512]{1,0:T(8,128)(2,1)} %get-tuple-element.99.refs_4_, ...), custom_call_target="tpu_custom_call" | custom-call | flops 200000000 | bytes 1 | tf_op jit(solution)/shard_map/pallas_call | solution.py:54
  447.7 19.2 %shard_map.334.refs_6_ = bf16[1024,2048]{1,0:T(8,128)(2,1)} custom-call(s32[8]{0:T(128)} %stack.83.refs_0_, s32[2]{0:T(128)} %pad_add_fusion.2.refs_1_, bf16[2048,512]{1,0:T(8,128)(2,1)} %get-tuple-element.91.refs_6_.refs_2_, bf16[2048,512]{1,0:T(8,128)(2,1)} %get-tuple-element.97.refs_4_.refs_3_, bf16[2048,512]{1,0:T(8,128)(2,1)} %get-tuple-element.99.refs_4_, ...), custom_call_target="tpu_custom_call" | custom-call | flops 200000000 | bytes 1 | tf_op jit(solution)/shard_map/pallas_call | solution.py:54
  467.0 11.1 %shard_map.335.refs_5_ = bf16[4,1,2,256,512]{4,3,2,1,0:T(8,128)(2,1)} custom-call(s32[1]{0:T(128)} %bitcast.5.refs_0_, bf16[4,2,256,2048]{3,2,1,0:T(8,128)(2,1)} %bitcast.122, bf16[4,2,256,2048]{3,2,1,0:T(8,128)(2,1)} %bitcast.113, bf16[2048,512]{1,0:T(8,128)(2,1)} %get-tuple-element.105.refs_3_.refs_5_, ...), custom_call_target="tpu_custom_call" | custom-call | flops 200000000 | bytes 1 | tf_op jit(solution)/shard_map/pallas_call | solution.py:54
  479.9 10.4 %shard_map.336.refs_22_ = bf16[4,1,2,256,512]{4,3,2,1,0:T(8,128)(2,1)} custom-call(s32[1]{0:T(128)} %bitcast.9.refs_0_, bf16[4,2,256,2048]{3,2,1,0:T(8,128)(2,1)} %bitcast.123, bf16[4,2,256,2048]{3,2,1,0:T(8,128)(2,1)} %bitcast.114, bf16[2048,512]{1,0:T(8,128)(2,1)} %get-tuple-element.106.refs_7_.refs_3_, ...), custom_call_target="tpu_custom_call" | custom-call | flops 200000000 | bytes 1 | tf_op jit(solution)/shard_map/pallas_call | solution.py:54
  490.3 28.3 %shard_map.337 = (f32[512,2048]{1,0:T(8,128)}, bf16[512,2048]{1,0:T(8,128)(2,1)}) custom-call(s32[8]{0:T(128)} %stack.83.refs_0_, s32[2]{0:T(128)} %pad_add_fusion.1.refs_1_, bf16[2048,512]{1,0:T(8,128)(2,1)} %get-tuple-element.93.refs_3_.refs_2_, bf16[2048,512]{1,0:T(8,128)(2,1)} %get-tuple-element.94.refs_4_.refs_3_, ...), custom_call_target="tpu_custom_call" | custom-call | flops 200000000 | bytes 1 | tf_op jit(solution)/shard_map/pallas_call | solution.py:54
  526.3 10.8 %shard_map.338.refs_20_ = bf16[4,1,2,256,512]{4,3,2,1,0:T(8,128)(2,1)} custom-call(s32[1]{0:T(128)} %bitcast.5.refs_0_, bf16[4,2,256,2048]{3,2,1,0:T(8,128)(2,1)} %bitcast.124, bf16[4,2,256,2048]{3,2,1,0:T(8,128)(2,1)} %bitcast.115, bf16[2048,512]{1,0:T(8,128)(2,1)} %get-tuple-element.104.refs_6_.refs_3_, bf16[2048,512]{1,0:T(8,128)(2,1)} %get-tuple-element.99.refs_4_, ...), custom_call_target="tpu_custom_call" | custom-call | flops 200000000 | bytes 1 | tf_op jit(solution)/shard_map/pallas_call | solution.py:54
  538.1 22.6 %shard_map.339 = (f32[512,2048]{1,0:T(8,128)}, bf16[512,2048]{1,0:T(8,128)(2,1)}) custom-call(s32[8]{0:T(128)} %stack.83.refs_0_, s32[2]{0:T(128)} %pad_add_fusion.1.refs_1_, bf16[2048,512]{1,0:T(8,128)(2,1)} %get-tuple-element.91.refs_6_.refs_2_, bf16[2048,512]{1,0:T(8,128)(2,1)} %get-tuple-element.97.refs_4_.refs_3_, ...), custom_call_target="tpu_custom_call" | custom-call | flops 200000000 | bytes 1 | tf_op jit(solution)/shard_map/pallas_call | solution.py:54
  560.7 23.8 %collective-permute-done.18.refs_5_ = bf16[4,1,2,256,512]{4,3,2,1,0:T(8,128)(2,1)} collective-permute-done((bf16[4,1,2,256,512]{4,3,2,1,0:T(8,128)(2,1)S(1)}, bf16[4,1,2,256,512]{4,3,2,1,0:T(8,128)(2,1)}, u32[]{:S(2)}, u32[]{:S(2)}) %collective-permute-start.18) | collective-permute-done | bytes 2097184 | tf_op jit(solution)/shard_map/ppermute | solution.py:678
  584.5 10.8 %shard_map.340.refs_5_ = bf16[4,1,2,256,512]{4,3,2,1,0:T(8,128)(2,1)} custom-call(s32[1]{0:T(128)} %bitcast.5.refs_0_, bf16[4,2,256,2048]{3,2,1,0:T(8,128)(2,1)} %bitcast.125, bf16[4,2,256,2048]{3,2,1,0:T(8,128)(2,1)} %bitcast.116, bf16[2048,512]{1,0:T(8,128)(2,1)} %get-tuple-element.106.refs_7_.refs_3_, ...), custom_call_target="tpu_custom_call" | custom-call | flops 200000000 | bytes 1 | tf_op jit(solution)/shard_map/pallas_call | solution.py:54
  597.0 10.7 %shard_map.341.refs_6_ = bf16[4,1,2,256,512]{4,3,2,1,0:T(8,128)(2,1)} custom-call(s32[1]{0:T(128)} %bitcast.9.refs_0_, bf16[4,2,256,2048]{3,2,1,0:T(8,128)(2,1)} %bitcast.126, bf16[4,2,256,2048]{3,2,1,0:T(8,128)(2,1)} %bitcast.117, bf16[2048,512]{1,0:T(8,128)(2,1)} %get-tuple-element.107.refs_8_.refs_3_, ...), custom_call_target="tpu_custom_call" | custom-call | flops 200000000 | bytes 1 | tf_op jit(solution)/shard_map/pallas_call | solution.py:54
  609.1 34.9 %collective-permute-done.20.refs_5_ = bf16[512,2048]{1,0:T(8,128)(2,1)} collective-permute-done((bf16[512,2048]{1,0:T(8,128)(2,1)S(1)}, bf16[512,2048]{1,0:T(8,128)(2,1)}, u32[]{:S(2)}, u32[]{:S(2)}) %collective-permute-start.20) | collective-permute-done | bytes 2097184 | tf_op jit(solution)/shard_map/ppermute | solution.py:678
  658.1 10.9 %shard_map.343.refs_5_ = bf16[4,1,2,256,512]{4,3,2,1,0:T(8,128)(2,1)} custom-call(s32[1]{0:T(128)} %bitcast.5.refs_0_, bf16[4,2,256,2048]{3,2,1,0:T(8,128)(2,1)} %bitcast.127, bf16[4,2,256,2048]{3,2,1,0:T(8,128)(2,1)} %bitcast.118, bf16[2048,512]{1,0:T(8,128)(2,1)} %get-tuple-element.107.refs_8_.refs_3_, ...), custom_call_target="tpu_custom_call" | custom-call | flops 200000000 | bytes 1 | tf_op jit(solution)/shard_map/pallas_call | solution.py:54
  669.0 20.0 %collective-permute-done.17.refs_4_ = bf16[512,2048]{1,0:T(8,128)(2,1)} collective-permute-done((bf16[512,2048]{1,0:T(8,128)(2,1)}, bf16[512,2048]{1,0:T(8,128)(2,1)}, u32[]{:S(2)}, u32[]{:S(2)}) %collective-permute-start.17) | collective-permute-done | bytes 2097184 | tf_op jit(solution)/shard_map/ppermute | solution.py:678
  702.8 31.1 %collective-permute-done.25.refs_0_ = bf16[512,2048]{1,0:T(8,128)(2,1)S(1)} collective-permute-done((bf16[512,2048]{1,0:T(8,128)(2,1)}, bf16[512,2048]{1,0:T(8,128)(2,1)S(1)}, u32[]{:S(2)}, u32[]{:S(2)}) %collective-permute-start.25) | collective-permute-done | bytes 2097184 | tf_op jit(solution)/shard_map/ppermute | solution.py:678
  742.5 10.8 %shard_map.348.refs_3_ = bf16[2048,2048]{1,0:T(8,128)(2,1)} custom-call(s32[4]{0:T(128)} %pad_add_fusion.refs_0_, bf16[512,2048]{1,0:T(8,128)(2,1)} %get-tuple-element.117.refs_1_, bf16[512,2048]{1,0:T(8,128)(2,1)} %collective-permute-done.24.refs_2_, bf16[512,2048]{1,0:T(8,128)(2,1)} %shard_map.347.refs_3_.refs_5_, bf16[512,2048]{1,0:T(8,128)(2,1)} %copy-done.10, ...), custom_call_target="tpu_custom_call" | custom-call | flops 200000000 | bytes 1 | tf_op jit(solution)/shard_map/pallas_call | solution.py:54
  757.6 20.1 %collective-permute-done.22.refs_0_ = bf16[512,2048]{1,0:T(8,128)(2,1)} collective-permute-done((bf16[512,2048]{1,0:T(8,128)(2,1)}, bf16[512,2048]{1,0:T(8,128)(2,1)}, u32[]{:S(2)}, u32[]{:S(2)}) %collective-permute-start.22) | collective-permute-done | bytes 2097184 | tf_op jit(solution)/shard_map/ppermute | solution.py:678
  794.3 10.8 %shard_map.352.refs_3_ = bf16[2048,2048]{1,0:T(8,128)(2,1)} custom-call(s32[4]{0:T(128)} %pad_add_fusion.refs_0_, bf16[512,2048]{1,0:T(8,128)(2,1)} %shard_map.344.refs_3_.refs_1_, bf16[512,2048]{1,0:T(8,128)(2,1)} %collective-permute-done.21.refs_2_, bf16[512,2048]{1,0:T(8,128)(2,1)} %shard_map.351.refs_3_.refs_5_, ...), custom_call_target="tpu_custom_call" | custom-call | flops 200000000 | bytes 1 | tf_op jit(solution)/shard_map/pallas_call | solution.py:54
  (281 shorter events, 170.0 us)
Async XLA Ops:
  7.2 56.2 %all-gather.13.cloned.1.call-start = ((), (), s32[]{:S(2)}) async-start(), calls=%async_computation.10 | async-start | bytes 2621440 | tf_op jit(solution)/shard_map/all_gather | solution.py:755
  9.3 97.3 %all-gather.15.cloned.1.call-start = ((), (), s32[]{:S(2)}) async-start(), calls=%async_computation.11 | async-start | bytes 2621440 | tf_op jit(solution)/shard_map/all_gather | solution.py:755
  11.4 169.3 %all-gather.17.cloned.1.call-start = ((), (), s32[]{:S(2)}) async-start(), calls=%async_computation.12 | async-start | bytes 2621440 | tf_op jit(solution)/shard_map/all_gather | solution.py:755
  13.5 195.1 %all-gather.19.cloned.1.call-start = ((), (), s32[]{:S(2)}) async-start(), calls=%async_computation.13 | async-start | bytes 2621440 | tf_op jit(solution)/shard_map/all_gather | solution.py:755
  15.7 229.5 %all-gather.21.cloned.1.call-start = ((), (), s32[]{:S(2)}) async-start(), calls=%async_computation.14 | async-start | bytes 2621440 | tf_op jit(solution)/shard_map/all_gather | solution.py:755
  17.9 283.0 %all-gather.23.cloned.1.call-start = ((), (), s32[]{:S(2)}) async-start(), calls=%async_computation.15 | async-start | bytes 2621440 | tf_op jit(solution)/shard_map/all_gather | solution.py:755
  31.2 622.1 %reduce-scatter.12.cloned.1.call-start = ((), (), s32[]{:S(2)}) async-start(), calls=%async_computation.8 | async-start | bytes 10485760 | tf_op jit(solution)/shard_map/reduce_scatter | solution.py:797
  63.4 46.3 %collective-permute-start.7 = (bf16[4,2,256,512]{3,2,1,0:T(8,128)(2,1)}, bf16[4,2,256,512]{3,2,1,0:T(8,128)(2,1)S(1)}, u32[]{:S(2)}, u32[]{:S(2)}) collective-permute-start(bf16[4,2,256,512]{3,2,1,0:T(8,128)(2,1)} %shard_map.314.refs_1_.refs_5_.refs_9_.refs_7_), channel_id=1, source_target_pairs={{0,4},{4,0},{8,12},{12,8},{16,20},{20,16},{24,28},{28,24},{1,5},{5... | collective-permute-start | bytes 6291464 | tf_op jit(solution)/shard_map/ppermute | solution.py:678
  106.6 47.7 %collective-permute-start.8 = (bf16[4,2,256,512]{3,2,1,0:T(8,128)(2,1)}, bf16[4,2,256,512]{3,2,1,0:T(8,128)(2,1)}, u32[]{:S(2)}, u32[]{:S(2)}) collective-permute-start(bf16[4,2,256,512]{3,2,1,0:T(8,128)(2,1)} %shard_map.315.refs_1_.refs_7_.refs_11_.refs_9_), channel_id=1, source_target_pairs={{0,4},{4,0},{8,12},{12,8},{16,20},{20,16},{24,28},{28,24},{1,5},{5... | collective-permute-start | bytes 6291464 | tf_op jit(solution)/shard_map/ppermute | solution.py:678
  180.7 152.6 %collective-permute-start.9 = (bf16[4,2,256,512]{3,2,1,0:T(8,128)(2,1)}, bf16[4,2,256,512]{3,2,1,0:T(8,128)(2,1)}, u32[]{:S(2)}, u32[]{:S(2)}) collective-permute-start(bf16[4,2,256,512]{3,2,1,0:T(8,128)(2,1)} %shard_map.318.refs_7_.refs_4_.refs_13_.refs_11_), channel_id=1, source_target_pairs={{0,4},{4,0},{8,12},{12,8},{16,20},{20,16},{24,28},{28,24},{1,5},{5... | collective-permute-start | bytes 6291464 | tf_op jit(solution)/shard_map/ppermute | solution.py:678
  208.6 141.5 %collective-permute-start.10 = (bf16[4,2,256,512]{3,2,1,0:T(8,128)(2,1)}, bf16[4,2,256,512]{3,2,1,0:T(8,128)(2,1)S(1)}, u32[]{:S(2)}, u32[]{:S(2)}) collective-permute-start(bf16[4,2,256,512]{3,2,1,0:T(8,128)(2,1)} %shard_map.320.refs_12_.refs_4_.refs_15_.refs_13_), channel_id=1, source_target_pairs={{0,4},{4,0},{8,12},{12,8},{16,20},{20,16},{24,28},{28,24},{1,5},{5... | collective-permute-start | bytes 6291464 | tf_op jit(solution)/shard_map/ppermute | solution.py:678
  245.2 122.1 %collective-permute-start.11 = (bf16[4,2,256,512]{3,2,1,0:T(8,128)(2,1)}, bf16[4,2,256,512]{3,2,1,0:T(8,128)(2,1)}, u32[]{:S(2)}, u32[]{:S(2)}) collective-permute-start(bf16[4,2,256,512]{3,2,1,0:T(8,128)(2,1)} %shard_map.322.refs_12_.refs_4_.refs_17_.refs_15_), channel_id=1, source_target_pairs={{0,4},{4,0},{8,12},{12,8},{16,20},{20,16},{24,28},{28,24},{1,5},{5... | collective-permute-start | bytes 6291464 | tf_op jit(solution)/shard_map/ppermute | solution.py:678
  300.9 82.3 %collective-permute-start.12 = (bf16[4,2,256,512]{3,2,1,0:T(8,128)(2,1)}, bf16[4,2,256,512]{3,2,1,0:T(8,128)(2,1)}, u32[]{:S(2)}, u32[]{:S(2)}) collective-permute-start(bf16[4,2,256,512]{3,2,1,0:T(8,128)(2,1)} %shard_map.325.refs_7_.refs_4_.refs_19_.refs_17_), channel_id=1, source_target_pairs={{0,4},{4,0},{8,12},{12,8},{16,20},{20,16},{24,28},{28,24},{1,5},{5... | collective-permute-start | bytes 6291464 | tf_op jit(solution)/shard_map/ppermute | solution.py:678
  333.3 366.8 %reduce-scatter.10.cloned.1.call-start = ((), (), s32[]{:S(2)}) async-start(), calls=%async_computation.7 | async-start | bytes 2621440 | tf_op jit(solution)/shard_map/reduce_scatter | solution.py:797
  409.8 57.2 %collective-permute-start.16 = (bf16[4,1,2,256,512]{4,3,2,1,0:T(8,128)(2,1)}, bf16[4,1,2,256,512]{4,3,2,1,0:T(8,128)(2,1)}, u32[]{:S(2)}, u32[]{:S(2)}) collective-permute-start(bf16[4,1,2,256,512]{4,3,2,1,0:T(8,128)(2,1)} %shard_map.331.refs_21_), channel_id=1, source_target_pairs={{0,4},{4,0},{8,12},{12,8},{16,20},{20,16},{24,28},{28,24},{1,5},{5... | collective-permute-start | bytes 6291464 | tf_op jit(solution)/shard_map/ppermute | solution.py:678
  437.1 53.2 %collective-permute-start.15 = (bf16[1024,2048]{1,0:T(8,128)(2,1)}, bf16[1024,2048]{1,0:T(8,128)(2,1)}, u32[]{:S(2)}, u32[]{:S(2)}) collective-permute-start(bf16[1024,2048]{1,0:T(8,128)(2,1)} %shard_map.332.refs_5_), channel_id=1, source_target_pairs={{0,1},{1,0},{2,3},{3,2},{4,5},{5,4},{6,7},{7,6},{8,9},{9,8},{10,11... | collective-permute-start | bytes 12582920 | tf_op jit(solution)/shard_map/ppermute | solution.py:678
  478.1 300.8 %reduce-scatter.8.cloned.1.call-start = ((), (), s32[]{:S(2)}) async-start(), calls=%async_computation.6 | async-start | bytes 2621440 | tf_op jit(solution)/shard_map/reduce_scatter | solution.py:797
  478.1 48.1 %collective-permute-start.14 = (bf16[4,1,2,256,512]{4,3,2,1,0:T(8,128)(2,1)S(1)}, bf16[4,1,2,256,512]{4,3,2,1,0:T(8,128)(2,1)}, u32[]{:S(2)}, u32[]{:S(2)}) collective-permute-start(bf16[4,1,2,256,512]{4,3,2,1,0:T(8,128)(2,1)S(1)} %copy-done.6), channel_id=1, source_target_pairs={{0,4},{4,0},{8,12},{12,8},{16,20},{20,16},{24,28},{28,24},{1,5},{5... | collective-permute-start | bytes 6291464 | tf_op jit(solution)/shard_map/ppermute | solution.py:678
  479.6 58.5 %collective-permute-start.13 = (bf16[1024,2048]{1,0:T(8,128)(2,1)}, bf16[1024,2048]{1,0:T(8,128)(2,1)}, u32[]{:S(2)}, u32[]{:S(2)}) collective-permute-start(bf16[1024,2048]{1,0:T(8,128)(2,1)} %shard_map.334.refs_6_), channel_id=1, source_target_pairs={{0,1},{1,0},{2,3},{3,2},{4,5},{5,4},{6,7},{7,6},{8,9},{9,8},{10,11... | collective-permute-start | bytes 12582920 | tf_op jit(solution)/shard_map/ppermute | solution.py:678
  537.1 244.4 %reduce-scatter.6.cloned.1.call-start = ((), (), s32[]{:S(2)}) async-start(), calls=%async_computation.5 | async-start | bytes 2621440 | tf_op jit(solution)/shard_map/reduce_scatter | solution.py:797
  537.1 47.4 %collective-permute-start.18 = (bf16[4,1,2,256,512]{4,3,2,1,0:T(8,128)(2,1)S(1)}, bf16[4,1,2,256,512]{4,3,2,1,0:T(8,128)(2,1)}, u32[]{:S(2)}, u32[]{:S(2)}) collective-permute-start(bf16[4,1,2,256,512]{4,3,2,1,0:T(8,128)(2,1)S(1)} %copy-done.7), channel_id=1, source_target_pairs={{0,4},{4,0},{8,12},{12,8},{16,20},{20,16},{24,28},{28,24},{1,5},{5... | collective-permute-start | bytes 6291464 | tf_op jit(solution)/shard_map/ppermute | solution.py:678
  595.3 209.8 %reduce-scatter.14.cloned.1.call-start = ((), (), s32[]{:S(2)}) async-start(), calls=%async_computation.9 | async-start | bytes 2621440 | tf_op jit(solution)/shard_map/reduce_scatter | solution.py:797
  595.3 48.7 %collective-permute-start.20 = (bf16[512,2048]{1,0:T(8,128)(2,1)S(1)}, bf16[512,2048]{1,0:T(8,128)(2,1)}, u32[]{:S(2)}, u32[]{:S(2)}) collective-permute-start(bf16[512,2048]{1,0:T(8,128)(2,1)S(1)} %copy-done.9), channel_id=1, source_target_pairs={{0,2},{1,3},{2,0},{3,1},{4,6},{5,7},{6,4},{7,5},{8,10},{9,11},{10,... | collective-permute-start | bytes 6291464 | tf_op jit(solution)/shard_map/ppermute | solution.py:678
  607.7 49.4 %collective-permute-start.19 = (bf16[4,1,2,256,512]{4,3,2,1,0:T(8,128)(2,1)}, bf16[4,1,2,256,512]{4,3,2,1,0:T(8,128)(2,1)}, u32[]{:S(2)}, u32[]{:S(2)}) collective-permute-start(bf16[4,1,2,256,512]{4,3,2,1,0:T(8,128)(2,1)} %shard_map.341.refs_6_), channel_id=1, source_target_pairs={{0,4},{4,0},{8,12},{12,8},{16,20},{20,16},{24,28},{28,24},{1,5},{5... | collective-permute-start | bytes 6291464 | tf_op jit(solution)/shard_map/ppermute | solution.py:678
  608.3 80.7 %collective-permute-start.17 = (bf16[512,2048]{1,0:T(8,128)(2,1)}, bf16[512,2048]{1,0:T(8,128)(2,1)}, u32[]{:S(2)}, u32[]{:S(2)}) collective-permute-start(bf16[512,2048]{1,0:T(8,128)(2,1)} %get-tuple-element.111.refs_6_), channel_id=1, source_target_pairs={{0,2},{1,3},{2,0},{3,1},{4,6},{5,7},{6,4},{7,5},{8,10},{9,11},{10,... | collective-permute-start | bytes 6291464 | tf_op jit(solution)/shard_map/ppermute | solution.py:678
  651.7 82.2 %collective-permute-start.25 = (bf16[512,2048]{1,0:T(8,128)(2,1)}, bf16[512,2048]{1,0:T(8,128)(2,1)S(1)}, u32[]{:S(2)}, u32[]{:S(2)}) collective-permute-start(bf16[512,2048]{1,0:T(8,128)(2,1)} %get-tuple-element.117.refs_1_), channel_id=1, source_target_pairs={{0,2},{1,3},{2,0},{3,1},{4,6},{5,7},{6,4},{7,5},{8,10},{9,11},{10,... | collective-permute-start | bytes 6291464 | tf_op jit(solution)/shard_map/ppermute | solution.py:678
  657.0 78.1 %collective-permute-start.30 = (f32[1,6144]{1,0:T(1,128)S(1)}, f32[1,6144]{1,0:T(1,128)S(1)}, u32[]{:S(2)}, u32[]{:S(2)}) collective-permute-start(f32[1,6144]{1,0:T(1,128)S(1)} %bitcast.170), channel_id=1, source_target_pairs={{0,3},{1,0},{2,1},{3,2},{4,7},{5,4},{6,5},{7,6},{8,11},{9,8},{10,9... | collective-permute-start | bytes 73736 | tf_op jit(solution)/shard_map/ppermute | solution.py:667
  657.1 78.1 %collective-permute-start.29 = (f32[1,6144]{1,0:T(1,128)S(1)}, f32[1,6144]{1,0:T(1,128)S(1)}, u32[]{:S(2)}, u32[]{:S(2)}) collective-permute-start(f32[1,6144]{1,0:T(1,128)S(1)} %bitcast.171), channel_id=1, source_target_pairs={{0,2},{1,3},{2,0},{3,1},{4,6},{5,7},{6,4},{7,5},{8,10},{9,11},{10,... | collective-permute-start | bytes 73736 | tf_op jit(solution)/shard_map/ppermute | solution.py:667
  689.0 46.2 %collective-permute-start.28 = (f32[1,6144]{1,0:T(1,128)S(1)}, f32[1,6144]{1,0:T(1,128)S(1)}, u32[]{:S(2)}, u32[]{:S(2)}) collective-permute-start(f32[1,6144]{1,0:T(1,128)S(1)} %bitcast.172), channel_id=1, source_target_pairs={{0,1},{1,2},{2,3},{3,0},{4,5},{5,6},{6,7},{7,4},{8,9},{9,10},{10,1... | collective-permute-start | bytes 73736 | tf_op jit(solution)/shard_map/ppermute | solution.py:667
  693.9 83.7 %collective-permute-start.22 = (bf16[512,2048]{1,0:T(8,128)(2,1)}, bf16[512,2048]{1,0:T(8,128)(2,1)}, u32[]{:S(2)}, u32[]{:S(2)}) collective-permute-start(bf16[512,2048]{1,0:T(8,128)(2,1)} %shard_map.344.refs_3_.refs_1_), channel_id=1, source_target_pairs={{0,2},{1,3},{2,0},{3,1},{4,6},{5,7},{6,4},{7,5},{8,10},{9,11},{10,... | collective-permute-start | bytes 6291464 | tf_op jit(solution)/shard_map/ppermute | solution.py:678
  738.4 45.8 %collective-permute-start.34 = (f32[1,9728]{1,0:T(1,128)S(1)}, f32[1,9728]{1,0:T(1,128)S(1)}, u32[]{:S(2)}, u32[]{:S(2)}) collective-permute-start(f32[1,9728]{1,0:T(1,128)S(1)} %pad_maximum_fusion.1), channel_id=1, source_target_pairs={{0,16},{4,20},{8,24},{12,28},{16,0},{20,4},{24,8},{28,12},{1,17},{... | collective-permute-start | bytes 116744 | tf_op jit(solution)/shard_map/ppermute | solution.py:667
  741.2 44.5 %collective-permute-start.33 = (f32[1,9728]{1,0:T(1,128)S(1)}, f32[1,9728]{1,0:T(1,128)S(1)}, u32[]{:S(2)}, u32[]{:S(2)}) collective-permute-start(f32[1,9728]{1,0:T(1,128)S(1)} %pad_maximum_fusion.1), channel_id=1, source_target_pairs={{0,12},{4,16},{8,20},{12,24},{16,28},{20,0},{24,4},{28,8},{1,13},{... | collective-permute-start | bytes 116744 | tf_op jit(solution)/shard_map/ppermute | solution.py:667
  (60 other events, 670.3 us)
Sparse Core Ops, SparseCore 0:
  10.2 49.7 all-gather.12
  62.1 44.4 all-gather.14
  108.2 44.6 all-gather.16
  154.3 44.5 all-gather.18
  200.4 44.7 all-gather.20
  246.6 44.4 all-gather.22
  333.4 143.1 reduce-scatter.11
  479.0 44.4 reduce-scatter.9
  537.2 41.5 reduce-scatter.7
  595.4 41.5 reduce-scatter.5
  669.1 41.7 reduce-scatter.13

commit v3 on v2

--- a/solution.py
+++ b/solution.py
@@ -230,37 +230,43 @@
     )
 
 
-def attend(first, pairs, held, low, query, keys, vals, d_attn, start, tables, after=()):
+def attend(first, held, low, query, keys, vals, d_attn, start, tables, after=()):
     tokens, local = query.shape
     block = min(256, tokens)
     count = tokens // block
+    pairs = attend_pairs(local)
+    heads = 2 * pairs
+    wide = pairs * LANES
     scale = HDIM ** (-0.5)
+    lanes = [slice(p * LANES, (p + 1) * LANES) for p in range(pairs)]
 
     def kernel(low_ref, q_ref, k_ref, v_ref, do_ref, start_ref, table_ref, *rest):
         (o_ref, dq_ref, dk_ref, dv_ref, db_ref,
-               k_half, v_half, k_t, v_t, s_buf, dp_buf, o_t, dq_t, dk_sum, dv_sum) = rest[len(held):]
-        i = pl.program_id(1)
+         k_half, v_half, k_t, v_t, s_buf, dp_buf, o_t, dq_t, dk_sum, dv_sum) = rest[len(held):]
+        i = pl.program_id(0)
         first_lanes = lax.broadcasted_iota(jnp.int32, (1, LANES), 1) < HDIM
+        zero = jnp.zeros((), BF16)
+
+        def apart(pair):
+            return jnp.where(first_lanes, pair, zero), jnp.where(first_lanes, zero, pair)
 
         @pl.when(i == 0)
         def _():
-            zero = jnp.zeros((), BF16)
             for b in range(count):
                 at = slice(b * block, (b + 1) * block)
                 for source, half, flipped in ((k_ref, k_half, k_t), (v_ref, v_half, v_t)):
-                    part = source[at, :]
-                    half[0, at, :] = jnp.where(first_lanes, part, zero)
-                    half[1, at, :] = jnp.where(first_lanes, zero, part)
-                    flipped[b] = part.T
+                    for p in range(pairs):
+                        part = source[at, lanes[p]]
+                        half[2 * p, at, :], half[2 * p + 1, at, :] = apart(part)
+                        flipped[p, b] = part.T
             dk_sum[...] = jnp.zeros_like(dk_sum)
             dv_sum[...] = jnp.zeros_like(dv_sum)
             db_ref[...] = jnp.zeros_like(db_ref)
 
-        q = q_ref[...]
-        do = do_ref[...]
-        zero = jnp.zeros((), BF16)
-        q_cat = jnp.concatenate([jnp.where(first_lanes, q, zero), jnp.where(first_lanes, zero, q)], 0)
-        do_cat = jnp.concatenate([jnp.where(first_lanes, do, zero), jnp.where(first_lanes, zero, do)], 0)
+        q = [q_ref[:, at] for at in lanes]
+        do = [do_ref[:, at] for at in lanes]
+        q_cat = [jnp.concatenate(apart(pair), 0) for pair in q]
+        do_cat = [jnp.concatenate(apart(pair), 0) for pair in do]
         t_place = i * block + lax.broadcasted_iota(jnp.int32, (1, block), 1)
         t_start = start_ref[...]
         low_block = low_ref[i]
@@ -272,100 +278,98 @@
             u_place = b * block + lax.broadcasted_iota(jnp.int32, (block, 1), 0)
             allowed = (u_place >= t_start) & (u_place <= t_place)
             new = []
-            for h in range(2):
-                s = jnp.where(allowed, nt(k_half[h, at, :], q), -1e30)
+            for h in range(heads):
+                s = jnp.where(allowed, nt(k_half[h, at, :], q[h // 2]), -1e30)
                 s_buf[h, b] = s
+                dp_buf[h, b] = nt(v_half[h, at, :], do[h // 2])
                 new.append(jnp.maximum(tops[h], jnp.max(s, 0, keepdims=True)))
             return tuple(new)
 
         lowest = jnp.full((1, block), -jnp.inf, F32)
-        tops = lax.fori_loop(low_block, i + 1, score, (lowest, lowest))
+        tops = lax.fori_loop(low_block, i + 1, score, (lowest,) * heads)
 
         def weigh(b, sums):
-            at = pl.ds(pl.multiple_of(b * block, block), block)
             new = []
-            for h in range(2):
+            for h in range(heads):
                 p = jnp.exp(s_buf[h, b] - tops[h])
-                dp = nt(v_half[h, at, :], do)
                 s_buf[h, b] = p
-                dp_buf[h, b] = dp
                 new.append(sums[2 * h] + jnp.sum(p, 0, keepdims=True))
-                new.append(sums[2 * h + 1] + jnp.sum(p * dp, 0, keepdims=True))
+                new.append(sums[2 * h + 1] + jnp.sum(p * dp_buf[h, b], 0, keepdims=True))
             return tuple(new)
 
         none = jnp.zeros((1, block), F32)
-        sums = lax.fori_loop(low_block, i + 1, weigh, (none,) * 4)
-        inverse = [1.0 / sums[0], 1.0 / sums[2]]
-        delta = [sums[1] * inverse[0], sums[3] * inverse[1]]
+        sums = lax.fori_loop(low_block, i + 1, weigh, (none,) * (2 * heads))
+        inverse = [1.0 / sums[2 * h] for h in range(heads)]
+        delta = [sums[2 * h + 1] * inverse[h] for h in range(heads)]
 
         def spread(b, carry):
             at = pl.ds(pl.multiple_of(b * block, block), block)
             probs, grads = [], []
-            for h in range(2):
+            for h in range(heads):
                 rows = slice(h * HDIM, (h + 1) * HDIM)
+                inside = slice(h % 2 * HDIM, (h % 2 + 1) * HDIM)
                 p = s_buf[h, b] * inverse[h]
                 ds = (p * (dp_buf[h, b] - delta[h])).astype(BF16)
                 p = p.astype(BF16)
-                o_t[rows, :] += nn(v_t[b, rows, :], p)
-                dq_t[rows, :] += nn(k_t[b, rows, :], ds)
+                o_t[rows, :] += nn(v_t[h // 2, b, inside, :], p)
+                dq_t[rows, :] += nn(k_t[h // 2, b, inside, :], ds)
                 probs.append(p)
                 grads.append(ds)
-            dv_sum[at, :] += nn(jnp.concatenate(probs, 1), do_cat)
-            dk_sum[at, :] += nn(jnp.concatenate(grads, 1), q_cat)
+            for p in range(pairs):
+                dv_sum[at, lanes[p]] += nn(jnp.concatenate(probs[2 * p : 2 * p + 2], 1), do_cat[p])
+                dk_sum[at, lanes[p]] += nn(jnp.concatenate(grads[2 * p : 2 * p + 2], 1), q_cat[p])
             return carry
 
         lax.fori_loop(low_block, i + 1, spread, 0)
         o_ref[...] = o_t[...].T.astype(BF16)
         here = pl.ds(pl.multiple_of(i * block, block), block)
-        dq = turn(dq_t[...].T * scale, [table_ref[n, here, :] for n in range(3)], -1.0).astype(BF16)
-        dq_ref[...] = dq
-        db_ref[0:1, :] += jnp.sum(dq.astype(F32), 0, keepdims=True)
+        table = [table_ref[n, here, :] for n in range(3)]
+        for at in lanes:
+            dq = turn(dq_t[at, :].T * scale, table, -1.0).astype(BF16)
+            dq_ref[:, at] = dq
+            db_ref[0:1, at] += jnp.sum(dq.astype(F32), 0, keepdims=True)
 
         @pl.when(i == count - 1)
         def _():
-            dk = turn(dk_sum[...], table_ref, -1.0).astype(BF16)
-            dv = dv_sum[...].astype(BF16)
-            dk_ref[...] = dk
-            dv_ref[...] = dv
-            db_ref[1:2, :] = jnp.sum(dk.astype(F32), 0, keepdims=True)
-            db_ref[2:3, :] = jnp.sum(dv.astype(F32), 0, keepdims=True)
-
-    part = pl.BlockSpec((block, LANES), lambda p, i, *_: (i, p + first))
-    column = pl.BlockSpec((tokens, LANES), lambda p, i, *_: (0, p + first))
+            for at in lanes:
+                dk = turn(dk_sum[:, at], table_ref, -1.0).astype(BF16)
+                dv = dv_sum[:, at].astype(BF16)
+                dk_ref[:, at] = dk
+                dv_ref[:, at] = dv
+                db_ref[1:2, at] = jnp.sum(dk.astype(F32), 0, keepdims=True)
+                db_ref[2:3, at] = jnp.sum(dv.astype(F32), 0, keepdims=True)
+
+    part = pl.BlockSpec((block, wide), lambda i, *_: (i, first))
+    column = pl.BlockSpec((tokens, wide), lambda i, *_: (0, first))
     shape = jax.ShapeDtypeStruct((tokens, local), BF16)
     return launch(
         kernel,
-        (pairs, count),
-        [
-            part,
-            column,
-            column,
-            part,
-            pl.BlockSpec((1, block), lambda p, i, *_: (0, i)),
-            whole(3, tokens, LANES),
-        ]
+        (count,),
+        [part, column, column, part, pl.BlockSpec((1, block), lambda i, *_: (0, i)), whole(3, tokens, LANES)]
         + [ANY] * len(held),
-        (part, part, column, column, pl.BlockSpec((3, LANES), lambda p, i, *_: (0, p + first))),
+        (part, part, column, column, pl.BlockSpec((3, wide), lambda i, *_: (0, first))),
         (shape,) * 4 + (jax.ShapeDtypeStruct((3, local), F32),),
         (query, keys, vals, d_attn, start, tables, *held),
         scalars=(low,),
         aliases={7 + i: i for i in range(len(held))},
         scratch=(
-            pltpu.VMEM((2, tokens, LANES), BF16),
-            pltpu.VMEM((2, tokens, LANES), BF16),
-            pltpu.VMEM((count, LANES, block), BF16),
-            pltpu.VMEM((count, LANES, block), BF16),
-            pltpu.VMEM((2, count, block, block), F32),
-            pltpu.VMEM((2, count, block, block), F32),
-            pltpu.VMEM((LANES, block), F32),
-            pltpu.VMEM((LANES, block), F32),
-            pltpu.VMEM((tokens, LANES), F32),
-            pltpu.VMEM((tokens, LANES), F32),
+            pltpu.VMEM((heads, tokens, LANES), BF16),
+            pltpu.VMEM((heads, tokens, LANES), BF16),
+            pltpu.VMEM((pairs, count, LANES, block), BF16),
+            pltpu.VMEM((pairs, count, LANES, block), BF16),
+            pltpu.VMEM((heads, count, block, block), F32),
+            pltpu.VMEM((heads, count, block, block), F32),
+            pltpu.VMEM((wide, block), F32),
+            pltpu.VMEM((wide, block), F32),
+            pltpu.VMEM((tokens, wide), F32),
+            pltpu.VMEM((tokens, wide), F32),
         ),
-        flops=tokens * tokens * local * 24,
-        moved=tokens * local * 20,
         after=after,
     )
+
+
+def attend_pairs(local):
+    return 2 if local % (2 * LANES) == 0 else 1
 
 
 def hidden_slot(places, normed, g, bias, group, after=()):
@@ -621,7 +625,7 @@
     )
 
 
-def total_group(grads, own, received, places, slots_in_all, after=()):
+def total_group(grads, own, received, places, slots_in_all, after=(), weight=1):
     n, rows, local = own.shape
 
     def kernel(places_ref, own_ref, *rest):
@@ -650,6 +654,7 @@
         scalars=(places,),
         aliases={} if first else {2 + len(received): 0},
         after=after,
+        weight=weight,
     )
 
 
@@ -738,7 +743,8 @@
 
     first_slots = [(0, 0), (0, 1), (0, 2), (1, 0)]
     gather_slots = [first_slots[:2], first_slots[2:]] + [[(0, 3 + s), (1, 1 + s)] for s in range(hidden_slots)]
-    group_slots = [first_slots] + [[(0, 3 + s), (1, 1 + s)] for s in range(hidden_slots)]
+    joined = [list(range(s, min(s + 2, hidden_slots))) for s in range(0, hidden_slots, 2)]
+    group_slots = [first_slots] + [[at for s in some for at in ((0, 3 + s), (1, 1 + s))] for some in joined]
 
     small = jnp.concatenate([in_bias.reshape(1, -1), vectors.reshape(1, -1)], 1).astype(BF16).astype(F32)
     small = collect(small, "dp", n_dp)
@@ -747,7 +753,7 @@
     vec = small[:, bias_size:].reshape((n_dp,) + vectors.shape).transpose(1, 0, 2).reshape(4, width)
 
     LINE.last = ()
-    turns = list(range(1 + hidden_slots))
+    turns = list(range(len(group_slots)))
     along = []
     for slots in gather_slots:
         cast = cast_group(w_in_s, w_outs_s, slots, LINE.last)
@@ -787,7 +793,7 @@
         hidden.append(h)
         d_hidden.append(dz)
         d_bias_hidden.append(db)
-        sides[1 + s] = [(0, [dz]), (1, [h])]
+        sides.setdefault(1 + s // 2, []).extend([(0, [dz]), (1, [h])])
 
     legs, shares = {}, {}
 
@@ -813,22 +819,33 @@
     exchange(0)
     exchange(1)
     groups[0][1] = gate(groups[0][1], weight=5)[0]
-    to_exchange = list(range(2, 2 + hidden_slots))
+    exchange(2)
+    to_exchange = list(range(3, 2 + hidden_slots))
     in_first = [(0, 0), (0, 1), (1, 0), (1, 1)]
     qkvd = in_line(qkv_project, owner_places, normed, cotangent, bias, tables, groups[:2], in_first)
-    pairs = local // LANES
     held = ()
-    for first in range(pairs):
-        if to_exchange and len(to_exchange) > 1:
+    for first in range(local // (attend_pairs(local) * LANES)):
+        held = in_line(attend, first, held, low, *qkvd, start.reshape(1, tokens), tables)
+        if to_exchange:
             exchange(to_exchange.pop(0))
-        held = in_line(attend, first, 1, held, low, *qkvd, start.reshape(1, tokens), tables)
-    while to_exchange:
-        exchange(to_exchange.pop(0))
     attn, d_query, d_keys, d_vals, d_bias_attn = held
     sides[0] = [(0, [d_query]), (0, [d_keys]), (0, [d_vals]), (1, [attn])]
     line_first(0)
-    for s in range(hidden_slots):
+    while to_exchange:
+        exchange(to_exchange.pop(0))
+    for s in joined[0]:
         hidden_step(s)
+    ahead_of = len(groups) - 1
+    for s in range(len(joined[0]), hidden_slots - 1):
+        groups[2 + s][1] = gate(groups[2 + s][1])[0]
+        hidden_step(s)
+    for g in range(min(ahead_of, 2 + len(hidden)), len(groups)):
+        groups[g][1] = gate(groups[g][1])[0]
+    first_next(1, 5000)
+    for s in range(len(hidden), hidden_slots):
+        hidden_step(s)
+    for g in range(1, len(joined)):
+        first_next(1 + g)
 
     def first_half(lefts, slots):
         received = []
@@ -859,37 +876,29 @@
     ahead = ([attn] + hidden, in_first[3:] + [(2 + s, 1) for s in range(hidden_slots)])
     grads, squares = None, []
 
-    def total_next(g):
+    def total_next(g, weight=1):
         slots, (own, received) = group_slots[g], shares[g]
         places = jnp.asarray([s if which == 0 else slots_in + s for which, s in slots], jnp.int32)
-        out, part = in_line(total_group, grads, own, received, places, slots_in + slots_out)
+        out, part = in_line(total_group, grads, own, received, places, slots_in + slots_out, weight=weight)
         squares.append(part)
         return out
 
-    first_next(1, 5000)
     back_half = first_half(*back)
-    first_next(2)
     ahead_half = first_half(*ahead)
     second_next(1)
-    first_next(3)
     own, received = second_half(*back, back_half)
-    second_next(2)
     ahead_own, ahead_received = second_half(*ahead, ahead_half)
-    second_next(3)
-    for g in range(4, 1 + hidden_slots):
-        first_next(g)
     d_x, vector_rows = in_line(finish_input, share_mine, own, received, block_input, cotangent, vec)
     back_held = send_share(d_x)
-    for g in range(4, 1 + hidden_slots):
-        second_next(g)
     out_held = send_share(
         in_line(finish_output, share_mine, ahead_own, ahead_received, block_input, vec)
     )
-    for g in turns[:2]:
-        grads = total_next(g)
+    for g in range(2, 1 + len(joined)):
+        second_next(g)
+    grads = total_next(0, 5000)
     back_parts = gather_share(back_held)
     block_input_gradient = in_line(lay_out, share_order, back_parts)
-    for g in turns[2:-1]:
+    for g in turns[1:-1]:
         grads = total_next(g)
     out_parts = gather_share(out_held)
     output = in_line(lay_out, share_order, out_parts)

time: 859 us -> 816 us (0.950)
  Pallas kernels: 487 us -> 437 us
    pallas_call x47 -> x41, Pallas kernels: 487 us -> 437 us  [launch(): pl.pallas_call(trimmed, grid_spec=pltpu.PrefetchScalarGridSpec(num_scalar...]
    all_gather x6, waiting for transfers between devices: 51.1 us -> 83.1 us  [body(): along.append(lax.all_gather(cast, 'dp', axis=0, axis_index_groups=lines))]
    ppermute x21 -> x19, waiting for transfers between devices: 184 us -> 157 us  [shift(): return lax.ppermute(values, axis, pairs)]
    ppermute x21 -> x19, starting transfers between devices: 18.1 us -> 16.2 us  [shift(): return lax.ppermute(values, axis, pairs)]
  transfers between devices with their start and end apart: 55 -> 51, of which waited for: 18 -> 20; matrix products, arithmetic and copies ran while one was open for 3% -> 3% of each run, Pallas kernels for 57% -> 53%
where the time goes in v3:
time: 816 us; the launch traced here: 809 us
  Pallas kernels  437 us (54%)
  waiting for transfers between devices  257 us (31%)
  starting transfers between devices  45.7 us (6%)
  other arithmetic  32.6 us (4%)
  between operations  19.6 us (2%)
  local copies, waits for them, and re-layouts  17.3 us (2%)
    pallas_call x41, Pallas kernels, launch(): pl.pallas_call(trimmed, grid_spec=pltpu.PrefetchScalarGridSpec(num_scalar...  437 us
    ppermute x19, waiting for transfers between devices, shift(): return lax.ppermute(values, axis, pairs)  157 us
    all_gather x6, waiting for transfers between devices, body(): along.append(lax.all_gather(cast, 'dp', axis=0, axis_index_groups=lines))  83.1 us
  transfers between devices with their start and end apart: 51, of which 20 were waited for; matrix products, arithmetic and copies ran while one was open for 3% of the time, Pallas kernels for 53%

profile of v3, /device:TPU:0, one launch (start us, length us, event | category | flops | bytes accessed | tf_op | source)
XLA Modules:
  0.0 808.7 jit_solution(940114340342490892)
XLA Ops:
  45.4 18.0 %shard_map.295 = (bf16[2048,2048]{1,0:T(8,128)(2,1)}, bf16[2048,2048]{1,0:T(8,128)(2,1)}, bf16[2048,2048]{1,0:T(8,128)(2,1)}) custom-call(bf16[2048,2048]{1,0:T(8,128)(2,1)} %refs_2_.13, bf16[2048,2048]{1,0:T(8,128)(2,1)} %refs_3_.1, f32[4,2048]{1,0:T(4,128)} %bitcast.144, bf16[2,256,512]{2,1,0:T(8,128)(2,1)} %shard_map.294.refs_3_, ...), custom_call_target="tpu_custom_call" | custom-call | flops 200000000 | bytes 1 | tf_op jit(solution)/shard_map/pallas_call | solution.py:54
  66.2 40.4 %all-gather.15.cloned.1.call-done = bf16[8,256,512]{2,1,0:T(8,128)(2,1)} async-done(((bf16[2,256,512]{2,1,0:T(8,128)(2,1)}), bf16[8,256,512]{2,1,0:T(8,128)(2,1)}) %all-gather.15.cloned.1.call-update) | async-done | bytes 2097168 | tf_op jit(solution)/shard_map/all_gather | solution.py:761
  110.9 42.6 %all-gather.17.cloned.1.call-done = bf16[8,256,512]{2,1,0:T(8,128)(2,1)} async-done(((bf16[2,256,512]{2,1,0:T(8,128)(2,1)}), bf16[8,256,512]{2,1,0:T(8,128)(2,1)}) %all-gather.17.cloned.1.call-update) | async-done | bytes 2097168 | tf_op jit(solution)/shard_map/all_gather | solution.py:761
  155.9 26.5 %shard_map.300 = (bf16[2048,512]{1,0:T(8,128)(2,1)}, bf16[2048,512]{1,0:T(8,128)(2,1)}, bf16[2048,512]{1,0:T(8,128)(2,1)}, bf16[2048,512]{1,0:T(8,128)(2,1)}) custom-call(s32[8]{0:T(128)} %stack.83.refs_0_, bf16[2048,2048]{1,0:T(8,128)(2,1)} %get-tuple-element.56.refs_1_, bf16[2048,2048]{1,0:T(8,128)(2,1)} %refs_3_.1, f32[7,512]{1,0:T(8,128)} %reshape.328.refs_3_, ...), custom_call_target="tpu_custom_call" | custom-call | flops 200000000 | bytes 1 | tf_op jit(solution)/shard_map/pallas_call | solution.py:54
  182.4 38.8 %shard_map.301 = (bf16[2048,512]{1,0:T(8,128)(2,1)}, bf16[2048,512]{1,0:T(8,128)(2,1)}, bf16[2048,512]{1,0:T(8,128)(2,1)}, bf16[2048,512]{1,0:T(8,128)(2,1)}, f32[3,512]{1,0:T(4,128)}) custom-call(s32[8]{0:T(128)} %and_select_fusion.1.refs_5_.refs_0_, bf16[2048,512]{1,0:T(8,128)(2,1)} %get-tuple-element.58.refs_1_, ...), custom_call_target="tpu_custom_call" | custom-call | flops 200000000 | bytes 1 | tf_op jit(solution)/shard_map/pallas_call | solution.py:54
  221.7 39.1 %shard_map.303 = (bf16[2048,512]{1,0:T(8,128)(2,1)}, bf16[2048,512]{1,0:T(8,128)(2,1)}, bf16[2048,512]{1,0:T(8,128)(2,1)}, bf16[2048,512]{1,0:T(8,128)(2,1)}, f32[3,512]{1,0:T(4,128)}) custom-call(s32[8]{0:T(128)} %and_select_fusion.1.refs_5_.refs_0_, ...), custom_call_target="tpu_custom_call", output_to_operand_aliasing={{0}: (7, {}), {1}: (8, {}), {2}: (9, {}), {3}: (10, {}), {4... | custom-call | flops 200000000 | bytes 1 | tf_op jit(solution)/shard_map/pallas_call | solution.py:54
  263.1 28.7 %shard_map.305.refs_1_ = bf16[4,2,4,256,512]{4,3,2,1,0:T(8,128)(2,1)} custom-call(s32[2]{0:T(128)} %iota.21.refs_0_, bf16[4,2,256,2048]{3,2,1,0:T(8,128)(2,1)} %bitcast.120, bf16[4,2,256,2048]{3,2,1,0:T(8,128)(2,1)} %bitcast.115, bf16[2048,512]{1,0:T(8,128)(2,1)} %get-tuple-element.69.refs_3_.refs_2_, bf16[2048,512]{1,0:T(8,128)(2,1)} %get-tuple-element.70.refs_4_.refs_3_, ...), custom_call_target="tpu_custom_call" | custom-call | flops 200000000 | bytes 1 | tf_op jit(solution)/shard_map/pallas_call | solution.py:54
  296.0 16.7 %shard_map.307 = (bf16[2048,512]{1,0:T(8,128)(2,1)}, bf16[2048,512]{1,0:T(8,128)(2,1)}, f32[1,512]{1,0:T(1,128)}) custom-call(s32[8]{0:T(128)} %stack.83.refs_0_, bf16[2048,2048]{1,0:T(8,128)(2,1)} %get-tuple-element.56.refs_1_, bf16[2048,2048]{1,0:T(8,128)(2,1)} %refs_3_.1, f32[1,512]{1,0:T(1,128)} %slice.58.refs_3_, ...), custom_call_target="tpu_custom_call" | custom-call | flops 1000000000 | bytes 1 | tf_op jit(solution)/shard_map/pallas_call | solution.py:54
  312.8 15.9 %shard_map.308 = (bf16[2048,512]{1,0:T(8,128)(2,1)}, bf16[2048,512]{1,0:T(8,128)(2,1)}, f32[1,512]{1,0:T(1,128)}) custom-call(s32[8]{0:T(128)} %stack.83.refs_0_, bf16[2048,2048]{1,0:T(8,128)(2,1)} %get-tuple-element.56.refs_1_, bf16[2048,2048]{1,0:T(8,128)(2,1)} %refs_3_.1, f32[1,512]{1,0:T(1,128)} %slice.60.refs_3_, ...), custom_call_target="tpu_custom_call" | custom-call | flops 1000000000 | bytes 1 | tf_op jit(solution)/shard_map/pallas_call | solution.py:54
  330.0 15.8 %shard_map.310 = (bf16[2048,512]{1,0:T(8,128)(2,1)}, bf16[2048,512]{1,0:T(8,128)(2,1)}, f32[1,512]{1,0:T(1,128)}) custom-call(s32[8]{0:T(128)} %stack.83.refs_0_, bf16[2048,2048]{1,0:T(8,128)(2,1)} %get-tuple-element.56.refs_1_, bf16[2048,2048]{1,0:T(8,128)(2,1)} %refs_3_.1, f32[1,512]{1,0:T(1,128)} %slice.62.refs_3_, ...), custom_call_target="tpu_custom_call" | custom-call | flops 1000000000 | bytes 1 | tf_op jit(solution)/shard_map/pallas_call | solution.py:54
  345.8 12.7 %collective-permute-done.12.refs_0_ = bf16[4,2,256,512]{3,2,1,0:T(8,128)(2,1)} collective-permute-done((bf16[4,2,256,512]{3,2,1,0:T(8,128)(2,1)}, bf16[4,2,256,512]{3,2,1,0:T(8,128)(2,1)}, u32[]{:S(2)}, u32[]{:S(2)}) %collective-permute-start.12) | collective-permute-done | bytes 2097184 | tf_op jit(solution)/shard_map/ppermute | solution.py:683
  358.5 16.6 %shard_map.312.refs_6_ = bf16[4,1,4,256,512]{4,3,2,1,0:T(8,128)(2,1)} custom-call(s32[1]{0:T(128)} %bitcast.9.refs_0_, bf16[4,2,256,2048]{3,2,1,0:T(8,128)(2,1)} %bitcast.121, bf16[4,2,256,2048]{3,2,1,0:T(8,128)(2,1)} %bitcast.116, bf16[2048,512]{1,0:T(8,128)(2,1)} %get-tuple-element.79.refs_3_.refs_5_, bf16[2048,512]{1,0:T(8,128)(2,1)} %get-tuple-element.73.refs_4_.refs_3_, ...), custom_call_target="tpu_custom_call" | custom-call | flops 999999995904 | bytes 1 | tf_op jit(solution)/shard_map/pallas_call | solution.py:54
  376.7 15.8 %shard_map.313 = (bf16[2048,512]{1,0:T(8,128)(2,1)}, bf16[2048,512]{1,0:T(8,128)(2,1)}, f32[1,512]{1,0:T(1,128)}) custom-call(s32[8]{0:T(128)} %stack.83.refs_0_, bf16[2048,2048]{1,0:T(8,128)(2,1)} %get-tuple-element.56.refs_1_, bf16[2048,2048]{1,0:T(8,128)(2,1)} %refs_3_.1, f32[1,512]{1,0:T(1,128)} %slice.64.refs_3_, ...), custom_call_target="tpu_custom_call" | custom-call | flops 1000000000 | bytes 1 | tf_op jit(solution)/shard_map/pallas_call | solution.py:54
  392.5 16.9 %shard_map.314.refs_21_ = bf16[4,1,4,256,512]{4,3,2,1,0:T(8,128)(2,1)} custom-call(s32[1]{0:T(128)} %bitcast.9.refs_0_, bf16[4,2,256,2048]{3,2,1,0:T(8,128)(2,1)} %bitcast.122, bf16[4,2,256,2048]{3,2,1,0:T(8,128)(2,1)} %bitcast.117, bf16[2048,512]{1,0:T(8,128)(2,1)} %get-tuple-element.82.refs_3_.refs_7_, ...), custom_call_target="tpu_custom_call" | custom-call | flops 200000000 | bytes 1 | tf_op jit(solution)/shard_map/pallas_call | solution.py:54
  409.4 25.3 %shard_map.315.refs_19_ = bf16[1024,2048]{1,0:T(8,128)(2,1)} custom-call(s32[8]{0:T(128)} %stack.83.refs_0_, s32[2]{0:T(128)} %pad_add_fusion.2.refs_1_, bf16[2048,512]{1,0:T(8,128)(2,1)} %get-tuple-element.69.refs_3_.refs_2_, bf16[2048,512]{1,0:T(8,128)(2,1)} %get-tuple-element.70.refs_4_.refs_3_, bf16[2048,512]{1,0:T(8,128)(2,1)} %get-tuple-element.71.refs_5_.refs_4_, ...), custom_call_target="tpu_custom_call" | custom-call | flops 200000000 | bytes 1 | tf_op jit(solution)/shard_map/pallas_call | solution.py:54
  434.7 19.3 %shard_map.316.refs_8_ = bf16[1024,2048]{1,0:T(8,128)(2,1)} custom-call(s32[8]{0:T(128)} %stack.83.refs_0_, s32[2]{0:T(128)} %pad_add_fusion.2.refs_1_, bf16[2048,512]{1,0:T(8,128)(2,1)} %get-tuple-element.67.refs_6_.refs_2_, bf16[2048,512]{1,0:T(8,128)(2,1)} %get-tuple-element.73.refs_4_.refs_3_, bf16[2048,512]{1,0:T(8,128)(2,1)} %get-tuple-element.75.refs_6_.refs_4_, ...), custom_call_target="tpu_custom_call" | custom-call | flops 200000000 | bytes 1 | tf_op jit(solution)/shard_map/pallas_call | solution.py:54
  454.1 12.3 %collective-permute-done.15.refs_7_ = bf16[4,1,4,256,512]{4,3,2,1,0:T(8,128)(2,1)} collective-permute-done((bf16[4,1,4,256,512]{4,3,2,1,0:T(8,128)(2,1)}, bf16[4,1,4,256,512]{4,3,2,1,0:T(8,128)(2,1)}, u32[]{:S(2)}, u32[]{:S(2)}) %collective-permute-start.15) | collective-permute-done | bytes 4194336 | tf_op jit(solution)/shard_map/ppermute | solution.py:683
  466.4 16.7 %shard_map.317.refs_22_ = bf16[4,1,4,256,512]{4,3,2,1,0:T(8,128)(2,1)} custom-call(s32[1]{0:T(128)} %bitcast.5.refs_0_, bf16[4,2,256,2048]{3,2,1,0:T(8,128)(2,1)} %bitcast.123, bf16[4,2,256,2048]{3,2,1,0:T(8,128)(2,1)} %bitcast.118, bf16[2048,512]{1,0:T(8,128)(2,1)} %get-tuple-element.79.refs_3_.refs_5_, ...), custom_call_target="tpu_custom_call" | custom-call | flops 200000000 | bytes 1 | tf_op jit(solution)/shard_map/pallas_call | solution.py:54
  484.7 6.1 collective-permute-done.14.refs_21_
  490.7 28.4 %shard_map.318 = (f32[512,2048]{1,0:T(8,128)}, bf16[512,2048]{1,0:T(8,128)(2,1)}) custom-call(s32[8]{0:T(128)} %stack.83.refs_0_, s32[2]{0:T(128)} %pad_add_fusion.1.refs_1_, bf16[2048,512]{1,0:T(8,128)(2,1)} %get-tuple-element.69.refs_3_.refs_2_, bf16[2048,512]{1,0:T(8,128)(2,1)} %get-tuple-element.70.refs_4_.refs_3_, ...), custom_call_target="tpu_custom_call" | custom-call | flops 200000000 | bytes 1 | tf_op jit(solution)/shard_map/pallas_call | solution.py:54
  520.7 22.1 %shard_map.319 = (f32[512,2048]{1,0:T(8,128)}, bf16[512,2048]{1,0:T(8,128)(2,1)}) custom-call(s32[8]{0:T(128)} %stack.83.refs_0_, s32[2]{0:T(128)} %pad_add_fusion.1.refs_1_, bf16[2048,512]{1,0:T(8,128)(2,1)} %get-tuple-element.67.refs_6_.refs_2_, bf16[2048,512]{1,0:T(8,128)(2,1)} %get-tuple-element.73.refs_4_.refs_3_, ...), custom_call_target="tpu_custom_call" | custom-call | flops 200000000 | bytes 1 | tf_op jit(solution)/shard_map/pallas_call | solution.py:54
  547.2 20.9 %collective-permute-done.17.refs_5_ = bf16[512,2048]{1,0:T(8,128)(2,1)} collective-permute-done((bf16[512,2048]{1,0:T(8,128)(2,1)}, bf16[512,2048]{1,0:T(8,128)(2,1)}, u32[]{:S(2)}, u32[]{:S(2)}) %collective-permute-start.17) | collective-permute-done | bytes 2097184 | tf_op jit(solution)/shard_map/ppermute | solution.py:683
  568.0 7.5 shard_map.320
  578.7 33.6 %collective-permute-done.16.refs_4_ = bf16[512,2048]{1,0:T(8,128)(2,1)S(1)} collective-permute-done((bf16[512,2048]{1,0:T(8,128)(2,1)}, bf16[512,2048]{1,0:T(8,128)(2,1)S(1)}, u32[]{:S(2)}, u32[]{:S(2)}) %collective-permute-start.16) | collective-permute-done | bytes 2097184 | tf_op jit(solution)/shard_map/ppermute | solution.py:683
  613.7 4.8 shard_map.321.refs_8_.refs_1_
  619.9 16.7 %shard_map.322.refs_3_ = bf16[4,1,4,256,512]{4,3,2,1,0:T(8,128)(2,1)} custom-call(s32[1]{0:T(128)} %bitcast.5.refs_0_, bf16[4,2,256,2048]{3,2,1,0:T(8,128)(2,1)} %bitcast.124, bf16[4,2,256,2048]{3,2,1,0:T(8,128)(2,1)} %bitcast.119, bf16[2048,512]{1,0:T(8,128)(2,1)} %get-tuple-element.82.refs_3_.refs_7_, bf16[2048,512]{1,0:T(8,128)(2,1)} %get-tuple-element.77.refs_4_.refs_5_, ...), custom_call_target="tpu_custom_call" | custom-call | flops 200000000 | bytes 1 | tf_op jit(solution)/shard_map/pallas_call | solution.py:54
  637.3 4.6 shard_map.323
  642.0 69.5 %collective-permute-done.23.refs_0_ = bf16[512,2048]{1,0:T(8,128)(2,1)} collective-permute-done((bf16[512,2048]{1,0:T(8,128)(2,1)}, bf16[512,2048]{1,0:T(8,128)(2,1)}, u32[]{:S(2)}, u32[]{:S(2)}) %collective-permute-start.23) | collective-permute-done | bytes 2097184 | tf_op jit(solution)/shard_map/ppermute | solution.py:683
  724.6 10.8 %shard_map.325.refs_3_ = bf16[2048,2048]{1,0:T(8,128)(2,1)} custom-call(s32[4]{0:T(128)} %pad_add_fusion.refs_0_, bf16[512,2048]{1,0:T(8,128)(2,1)} %get-tuple-element.91.refs_1_, bf16[512,2048]{1,0:T(8,128)(2,1)} %copy-done.7, bf16[512,2048]{1,0:T(8,128)(2,1)} %shard_map.324.refs_3_.refs_5_, bf16[512,2048]{1,0:T(8,128)(2,1)} %collective-permute-done.24.refs_4_, ...), custom_call_target="tpu_custom_call" | custom-call | flops 200000000 | bytes 1 | tf_op jit(solution)/shard_map/pallas_call | solution.py:54
  748.8 10.8 %shard_map.328.refs_3_ = bf16[2048,2048]{1,0:T(8,128)(2,1)} custom-call(s32[4]{0:T(128)} %pad_add_fusion.refs_0_, bf16[512,2048]{1,0:T(8,128)(2,1)} %shard_map.321.refs_8_.refs_1_, bf16[512,2048]{1,0:T(8,128)(2,1)} %collective-permute-done.18.refs_2_, bf16[512,2048]{1,0:T(8,128)(2,1)} %shard_map.327.refs_3_.refs_5_, ...), custom_call_target="tpu_custom_call" | custom-call | flops 200000000 | bytes 1 | tf_op jit(solution)/shard_map/pallas_call | solution.py:54
  784.5 8.9 %fusion.8 = (f32[256,5,512]{2,0,1:T(8,128)}, f32[256,5,512]{2,0,1:T(8,128)}, f32[256,5,512]{2,0,1:T(8,128)}) fusion(f32[]{:T(128)S(6)} %div.99, f32[12,256,512]{2,1,0:T(8,128)} %get-tuple-element.96, f32[256,5,512]{2,0,1:T(8,128)} %param.26, f32[256,5,512]{2,0,1:T(8,128)} %param.25, f32[256,5,512]{2,0,1:T(8,128)S(1)} %copy-done.3), kind=kLoop, calls=%fused_computation.22 | loop fusion | flops 10485760 | bytes 18350084 | tf_op jit(solution)/shard_map/transpose | solution.py:931
  793.4 7.1 fusion.7
  (252 shorter events, 119.0 us)
Async XLA Ops:
  7.2 56.2 %all-gather.13.cloned.1.call-start = ((), (), s32[]{:S(2)}) async-start(), calls=%async_computation.6 | async-start | bytes 2621440 | tf_op jit(solution)/shard_map/all_gather | solution.py:761
  9.3 97.3 %all-gather.15.cloned.1.call-start = ((), (), s32[]{:S(2)}) async-start(), calls=%async_computation.7 | async-start | bytes 2621440 | tf_op jit(solution)/shard_map/all_gather | solution.py:761
  11.4 142.0 %all-gather.17.cloned.1.call-start = ((), (), s32[]{:S(2)}) async-start(), calls=%async_computation.8 | async-start | bytes 2621440 | tf_op jit(solution)/shard_map/all_gather | solution.py:761
  13.5 207.7 %all-gather.19.cloned.1.call-start = ((), (), s32[]{:S(2)}) async-start(), calls=%async_computation.9 | async-start | bytes 2621440 | tf_op jit(solution)/shard_map/all_gather | solution.py:761
  15.7 245.2 %all-gather.23.cloned.1.call-start = ((), (), s32[]{:S(2)}) async-start(), calls=%async_computation.11 | async-start | bytes 2621440 | tf_op jit(solution)/shard_map/all_gather | solution.py:761
  17.8 273.9 %all-gather.21.cloned.1.call-start = ((), (), s32[]{:S(2)}) async-start(), calls=%async_computation.10 | async-start | bytes 2621440 | tf_op jit(solution)/shard_map/all_gather | solution.py:761
  18.1 20.9 %collective-permute-start.6 = (f32[1,1472]{1,0:T(1,128)S(1)}, f32[1,1472]{1,0:T(1,128)S(1)}, u32[]{:S(2)}, u32[]{:S(2)}) collective-permute-start(f32[1,1472]{1,0:T(1,128)S(1)} %maximum_convert_fusion), channel_id=1, source_target_pairs={{0,4},{4,8},{8,12},{12,16},{16,20},{20,24},{24,28},{28,0},{1,5},{5... | collective-permute-start | bytes 17672 | tf_op jit(solution)/shard_map/ppermute | solution.py:664
  22.7 20.2 %collective-permute-start.4 = (f32[1,1472]{1,0:T(1,128)S(1)}, f32[1,1472]{1,0:T(1,128)S(1)}, u32[]{:S(2)}, u32[]{:S(2)}) collective-permute-start(f32[1,1472]{1,0:T(1,128)S(1)} %maximum_convert_fusion), channel_id=1, source_target_pairs={{0,12},{4,16},{8,20},{12,24},{16,28},{20,0},{24,4},{28,8},{1,13},{... | collective-permute-start | bytes 17672 | tf_op jit(solution)/shard_map/ppermute | solution.py:664
  31.2 512.3 %reduce-scatter.6.cloned.1.call-start = ((), (), s32[]{:S(2)}) async-start(), calls=%async_computation.4 | async-start | bytes 10485760 | tf_op jit(solution)/shard_map/reduce_scatter | solution.py:803
  63.4 46.2 %collective-permute-start.7 = (bf16[4,2,256,512]{3,2,1,0:T(8,128)(2,1)}, bf16[4,2,256,512]{3,2,1,0:T(8,128)(2,1)S(1)}, u32[]{:S(2)}, u32[]{:S(2)}) collective-permute-start(bf16[4,2,256,512]{3,2,1,0:T(8,128)(2,1)} %shard_map.296.refs_1_.refs_5_.refs_9_.refs_7_), channel_id=1, source_target_pairs={{0,4},{4,0},{8,12},{12,8},{16,20},{20,16},{24,28},{28,24},{1,5},{5... | collective-permute-start | bytes 6291464 | tf_op jit(solution)/shard_map/ppermute | solution.py:683
  106.6 49.2 %collective-permute-start.8 = (bf16[4,2,256,512]{3,2,1,0:T(8,128)(2,1)}, bf16[4,2,256,512]{3,2,1,0:T(8,128)(2,1)}, u32[]{:S(2)}, u32[]{:S(2)}) collective-permute-start(bf16[4,2,256,512]{3,2,1,0:T(8,128)(2,1)} %shard_map.297.refs_1_.refs_7_.refs_11_.refs_9_), channel_id=1, source_target_pairs={{0,4},{4,0},{8,12},{12,8},{16,20},{20,16},{24,28},{28,24},{1,5},{5... | collective-permute-start | bytes 6291464 | tf_op jit(solution)/shard_map/ppermute | solution.py:683
  153.5 142.5 %collective-permute-start.9 = (bf16[4,2,256,512]{3,2,1,0:T(8,128)(2,1)}, bf16[4,2,256,512]{3,2,1,0:T(8,128)(2,1)}, u32[]{:S(2)}, u32[]{:S(2)}) collective-permute-start(bf16[4,2,256,512]{3,2,1,0:T(8,128)(2,1)} %shard_map.299.refs_9_.refs_4_.refs_13_.refs_11_), channel_id=1, source_target_pairs={{0,4},{4,0},{8,12},{12,8},{16,20},{20,16},{24,28},{28,24},{1,5},{5... | collective-permute-start | bytes 6291464 | tf_op jit(solution)/shard_map/ppermute | solution.py:683
  221.3 91.5 %collective-permute-start.10 = (bf16[4,2,256,512]{3,2,1,0:T(8,128)(2,1)}, bf16[4,2,256,512]{3,2,1,0:T(8,128)(2,1)}, u32[]{:S(2)}, u32[]{:S(2)}) collective-permute-start(bf16[4,2,256,512]{3,2,1,0:T(8,128)(2,1)} %shard_map.302.refs_12_.refs_4_.refs_15_.refs_13_), channel_id=1, source_target_pairs={{0,4},{4,0},{8,12},{12,8},{16,20},{20,16},{24,28},{28,24},{1,5},{5... | collective-permute-start | bytes 6291464 | tf_op jit(solution)/shard_map/ppermute | solution.py:683
  260.9 67.8 %collective-permute-start.11 = (bf16[4,2,256,512]{3,2,1,0:T(8,128)(2,1)}, bf16[4,2,256,512]{3,2,1,0:T(8,128)(2,1)S(1)}, u32[]{:S(2)}, u32[]{:S(2)}) collective-permute-start(bf16[4,2,256,512]{3,2,1,0:T(8,128)(2,1)} %shard_map.304.refs_7_.refs_4_.refs_17_.refs_15_), channel_id=1, source_target_pairs={{0,4},{4,0},{8,12},{12,8},{16,20},{20,16},{24,28},{28,24},{1,5},{5... | collective-permute-start | bytes 6291464 | tf_op jit(solution)/shard_map/ppermute | solution.py:683
  291.8 66.7 %collective-permute-start.12 = (bf16[4,2,256,512]{3,2,1,0:T(8,128)(2,1)}, bf16[4,2,256,512]{3,2,1,0:T(8,128)(2,1)}, u32[]{:S(2)}, u32[]{:S(2)}) collective-permute-start(bf16[4,2,256,512]{3,2,1,0:T(8,128)(2,1)} %shard_map.306.refs_6_.refs_4_.refs_19_.refs_17_), channel_id=1, source_target_pairs={{0,4},{4,0},{8,12},{12,8},{16,20},{20,16},{24,28},{28,24},{1,5},{5... | collective-permute-start | bytes 6291464 | tf_op jit(solution)/shard_map/ppermute | solution.py:683
  295.9 439.5 %reduce-scatter.4.cloned.1.call-start = ((), (), s32[]{:S(2)}) async-start(), calls=%async_computation.3 | async-start | bytes 5242880 | tf_op jit(solution)/shard_map/reduce_scatter | solution.py:803
  375.1 91.3 %collective-permute-start.15 = (bf16[4,1,4,256,512]{4,3,2,1,0:T(8,128)(2,1)}, bf16[4,1,4,256,512]{4,3,2,1,0:T(8,128)(2,1)}, u32[]{:S(2)}, u32[]{:S(2)}) collective-permute-start(bf16[4,1,4,256,512]{4,3,2,1,0:T(8,128)(2,1)} %shard_map.312.refs_6_), channel_id=1, source_target_pairs={{0,4},{4,0},{8,12},{12,8},{16,20},{20,16},{24,28},{28,24},{1,5},{5... | collective-permute-start | bytes 12582920 | tf_op jit(solution)/shard_map/ppermute | solution.py:683
  483.1 276.4 %reduce-scatter.8.cloned.1.call-start = ((), (), s32[]{:S(2)}) async-start(), calls=%async_computation.5 | async-start | bytes 5242880 | tf_op jit(solution)/shard_map/reduce_scatter | solution.py:803
  483.2 37.4 %collective-permute-start.13 = (bf16[1024,2048]{1,0:T(8,128)(2,1)}, bf16[1024,2048]{1,0:T(8,128)(2,1)}, u32[]{:S(2)}, u32[]{:S(2)}) collective-permute-start(bf16[1024,2048]{1,0:T(8,128)(2,1)} %shard_map.316.refs_8_), channel_id=1, source_target_pairs={{0,1},{1,0},{2,3},{3,2},{4,5},{5,4},{6,7},{7,6},{8,9},{9,8},{10,11... | collective-permute-start | bytes 12582920 | tf_op jit(solution)/shard_map/ppermute | solution.py:683
  483.7 134.7 %collective-permute-start.21 = (bf16[4,1,4,256,512]{4,3,2,1,0:T(8,128)(2,1)}, bf16[4,1,4,256,512]{4,3,2,1,0:T(8,128)(2,1)}, u32[]{:S(2)}, u32[]{:S(2)}) collective-permute-start(bf16[4,1,4,256,512]{4,3,2,1,0:T(8,128)(2,1)} %shard_map.314.refs_21_), channel_id=1, source_target_pairs={{0,4},{4,0},{8,12},{12,8},{16,20},{20,16},{24,28},{28,24},{1,5},{5... | collective-permute-start | bytes 12582920 | tf_op jit(solution)/shard_map/ppermute | solution.py:683
  519.2 48.9 %collective-permute-start.17 = (bf16[512,2048]{1,0:T(8,128)(2,1)}, bf16[512,2048]{1,0:T(8,128)(2,1)}, u32[]{:S(2)}, u32[]{:S(2)}) collective-permute-start(bf16[512,2048]{1,0:T(8,128)(2,1)} %get-tuple-element.85.refs_20_), channel_id=1, source_target_pairs={{0,2},{1,3},{2,0},{3,1},{4,6},{5,7},{6,4},{7,5},{8,10},{9,11},{10,... | collective-permute-start | bytes 6291464 | tf_op jit(solution)/shard_map/ppermute | solution.py:683
  542.8 69.5 %collective-permute-start.16 = (bf16[512,2048]{1,0:T(8,128)(2,1)}, bf16[512,2048]{1,0:T(8,128)(2,1)S(1)}, u32[]{:S(2)}, u32[]{:S(2)}) collective-permute-start(bf16[512,2048]{1,0:T(8,128)(2,1)} %get-tuple-element.87.refs_6_), channel_id=1, source_target_pairs={{0,2},{1,3},{2,0},{3,1},{4,6},{5,7},{6,4},{7,5},{8,10},{9,11},{10,... | collective-permute-start | bytes 6291464 | tf_op jit(solution)/shard_map/ppermute | solution.py:683
  546.2 90.5 %collective-permute-start.20 = (bf16[4,256,512]{2,1,0:T(8,128)(2,1)S(1)}, bf16[4,256,512]{2,1,0:T(8,128)(2,1)}, u32[]{:S(2)}, u32[]{:S(2)}) collective-permute-start(bf16[4,256,512]{2,1,0:T(8,128)(2,1)S(1)} %get-tuple-element.111), channel_id=1, source_target_pairs={{0,4},{4,0},{8,12},{12,8},{16,20},{20,16},{24,28},{28,24},{1,5},{5... | collective-permute-start | bytes 3145736 | tf_op jit(solution)/shard_map/ppermute | solution.py:683
  577.0 134.5 %collective-permute-start.28 = (f32[1,6144]{1,0:T(1,128)}, f32[1,6144]{1,0:T(1,128)}, u32[]{:S(2)}, u32[]{:S(2)}) collective-permute-start(f32[1,6144]{1,0:T(1,128)} %bitcast.67), channel_id=1, source_target_pairs={{0,3},{1,0},{2,1},{3,2},{4,7},{5,4},{6,5},{7,6},{8,11},{9,8},{10,9... | collective-permute-start | bytes 73736 | tf_op jit(solution)/shard_map/ppermute | solution.py:672
  577.2 134.8 %collective-permute-start.27 = (f32[1,6144]{1,0:T(1,128)}, f32[1,6144]{1,0:T(1,128)}, u32[]{:S(2)}, u32[]{:S(2)}) collective-permute-start(f32[1,6144]{1,0:T(1,128)} %bitcast.67), channel_id=1, source_target_pairs={{0,2},{1,3},{2,0},{3,1},{4,6},{5,7},{6,4},{7,5},{8,10},{9,11},{10,... | collective-permute-start | bytes 73736 | tf_op jit(solution)/shard_map/ppermute | solution.py:672
  612.3 99.7 %collective-permute-start.26 = (f32[1,6144]{1,0:T(1,128)}, f32[1,6144]{1,0:T(1,128)}, u32[]{:S(2)}, u32[]{:S(2)}) collective-permute-start(f32[1,6144]{1,0:T(1,128)} %bitcast.67), channel_id=1, source_target_pairs={{0,1},{1,2},{2,3},{3,0},{4,5},{5,6},{6,7},{7,4},{8,9},{9,10},{10,1... | collective-permute-start | bytes 73736 | tf_op jit(solution)/shard_map/ppermute | solution.py:672
  618.5 102.1 %collective-permute-start.19 = (bf16[512,2048]{1,0:T(8,128)(2,1)}, bf16[512,2048]{1,0:T(8,128)(2,1)}, u32[]{:S(2)}, u32[]{:S(2)}) collective-permute-start(bf16[512,2048]{1,0:T(8,128)(2,1)} %shard_map.321.refs_8_.refs_1_), channel_id=1, source_target_pairs={{0,2},{1,3},{2,0},{3,1},{4,6},{5,7},{6,4},{7,5},{8,10},{9,11},{10,... | collective-permute-start | bytes 6291464 | tf_op jit(solution)/shard_map/ppermute | solution.py:683
  636.7 74.9 %collective-permute-start.23 = (bf16[512,2048]{1,0:T(8,128)(2,1)}, bf16[512,2048]{1,0:T(8,128)(2,1)}, u32[]{:S(2)}, u32[]{:S(2)}) collective-permute-start(bf16[512,2048]{1,0:T(8,128)(2,1)} %get-tuple-element.91.refs_1_), channel_id=1, source_target_pairs={{0,2},{1,3},{2,0},{3,1},{4,6},{5,7},{6,4},{7,5},{8,10},{9,11},{10,... | collective-permute-start | bytes 6291464 | tf_op jit(solution)/shard_map/ppermute | solution.py:683
  717.0 22.7 %collective-permute-start.32 = (f32[1,9728]{1,0:T(1,128)S(1)}, f32[1,9728]{1,0:T(1,128)S(1)}, u32[]{:S(2)}, u32[]{:S(2)}) collective-permute-start(f32[1,9728]{1,0:T(1,128)S(1)} %pad_maximum_fusion.1), channel_id=1, source_target_pairs={{0,16},{4,20},{8,24},{12,28},{16,0},{20,4},{24,8},{28,12},{1,17},{... | collective-permute-start | bytes 116744 | tf_op jit(solution)/shard_map/ppermute | solution.py:672
  719.3 22.0 %collective-permute-start.31 = (f32[1,9728]{1,0:T(1,128)S(1)}, f32[1,9728]{1,0:T(1,128)S(1)}, u32[]{:S(2)}, u32[]{:S(2)}) collective-permute-start(f32[1,9728]{1,0:T(1,128)S(1)} %pad_maximum_fusion.1), channel_id=1, source_target_pairs={{0,12},{4,16},{8,20},{12,24},{16,28},{20,0},{24,4},{28,8},{1,13},{... | collective-permute-start | bytes 116744 | tf_op jit(solution)/shard_map/ppermute | solution.py:672
  720.6 21.2 %collective-permute-start.30 = (f32[1,9728]{1,0:T(1,128)S(1)}, f32[1,9728]{1,0:T(1,128)S(1)}, u32[]{:S(2)}, u32[]{:S(2)}) collective-permute-start(f32[1,9728]{1,0:T(1,128)S(1)} %pad_maximum_fusion.1), channel_id=1, source_target_pairs={{0,8},{4,12},{8,16},{12,20},{16,24},{20,28},{24,0},{28,4},{1,9},{5... | collective-permute-start | bytes 116744 | tf_op jit(solution)/shard_map/ppermute | solution.py:672
  721.1 20.7 %collective-permute-start.35 = (f32[1,9728]{1,0:T(1,128)S(1)}, f32[1,9728]{1,0:T(1,128)S(1)}, u32[]{:S(2)}, u32[]{:S(2)}) collective-permute-start(f32[1,9728]{1,0:T(1,128)S(1)} %pad_maximum_fusion.1), channel_id=1, source_target_pairs={{0,28},{4,0},{8,4},{12,8},{16,12},{20,16},{24,20},{28,24},{1,29},{... | collective-permute-start | bytes 116744 | tf_op jit(solution)/shard_map/ppermute | solution.py:672
  (51 other events, 571.9 us)
Sparse Core Ops, SparseCore 0:
  10.2 49.6 all-gather.12
  62.0 44.5 all-gather.14
  108.8 44.6 all-gather.16
  154.9 44.6 all-gather.18
  201.0 44.6 all-gather.22
  247.1 44.6 all-gather.20
  296.1 142.2 reduce-scatter.5
  483.2 74.7 reduce-scatter.3
  636.8 73.8 reduce-scatter.7

commit v4 on v3

--- a/solution.py
+++ b/solution.py
@@ -39,6 +39,7 @@
 class Line:
     def __init__(self):
         self.last = ()
+        self.weight = 1
 
 
 LINE = Line()
@@ -63,7 +64,7 @@
         out_shape=out_shape,
         input_output_aliases=aliases,
         compiler_params=pltpu.CompilerParams(vmem_limit_bytes=VMEM_LIMIT),
-        cost_estimate=pl.CostEstimate(flops=200000000 * weight, bytes_accessed=1, transcendentals=0),
+        cost_estimate=pl.CostEstimate(flops=200000000 * weight * LINE.weight, bytes_accessed=1, transcendentals=0),
     )(*scalars, *args, *after)
 
 
@@ -667,10 +668,11 @@
 
 
 def total_over(values, axis, count):
-    total = values
-    for k in range(1, count):
-        total = total + lax.ppermute(values, axis, [(i, (i + k) % count) for i in range(count)])
-    return total
+    bit = 1
+    while bit < count:
+        values = values + lax.ppermute(values, axis, [(i, i ^ bit) for i in range(count)])
+        bit *= 2
+    return values
 
 
 def shift(values, axis, count, inner, outer_by, inner_by):
@@ -753,6 +755,7 @@
     vec = small[:, bias_size:].reshape((n_dp,) + vectors.shape).transpose(1, 0, 2).reshape(4, width)
 
     LINE.last = ()
+    LINE.weight = 1
     turns = list(range(len(group_slots)))
     along = []
     for slots in gather_slots:
@@ -844,8 +847,7 @@
     first_next(1, 5000)
     for s in range(len(hidden), hidden_slots):
         hidden_step(s)
-    for g in range(1, len(joined)):
-        first_next(1 + g)
+    LINE.weight = 5000
 
     def first_half(lefts, slots):
         received = []
@@ -862,8 +864,11 @@
         return [own] + [shift(own, "tensor", n_tensor, cores, w, 0) for w in range(1, ways)]
 
     def gather_share(held):
+        return [held[0]] + gate(*held[1:])
+
+    def spread_share(held):
         parts = []
-        for part in [held[0]] + gate(*held[1:]):
+        for part in held:
             parts.append(part)
             for c in range(1, cores):
                 parts.append(shift(part, "tensor", n_tensor, cores, 0, c))
@@ -883,10 +888,12 @@
         squares.append(part)
         return out
 
+    for g in range(2, 1 + len(joined)):
+        first_next(g)
     back_half = first_half(*back)
     ahead_half = first_half(*ahead)
+    own, received = second_half(*back, back_half)
     second_next(1)
-    own, received = second_half(*back, back_half)
     ahead_own, ahead_received = second_half(*ahead, ahead_half)
     d_x, vector_rows = in_line(finish_input, share_mine, own, received, block_input, cotangent, vec)
     back_held = send_share(d_x)
@@ -895,14 +902,7 @@
     )
     for g in range(2, 1 + len(joined)):
         second_next(g)
-    grads = total_next(0, 5000)
-    back_parts = gather_share(back_held)
-    block_input_gradient = in_line(lay_out, share_order, back_parts)
-    for g in turns[1:-1]:
-        grads = total_next(g)
-    out_parts = gather_share(out_held)
-    output = in_line(lay_out, share_order, out_parts)
-
+    grads = total_next(0)
     vector_rows = total_over(vector_rows.reshape(1, -1), "tensor", n_tensor)
     d_bias = jnp.concatenate([d_bias_attn] + d_bias_hidden, 0)
     small = total_over(jnp.concatenate([d_bias.reshape(1, -1), vector_rows], 1), "dp", n_dp)
@@ -912,18 +912,21 @@
     g_vec = lax.dynamic_index_in_dim(small[0, slots_in * local :].reshape(3, n_dp, width // n_dp), me, 1, False)
     g_vec = jnp.concatenate([g_vec, g_vec[2:]], 0)
 
+    back_parts = spread_share(gather_share(back_held))
+    for g in turns[1:-1]:
+        grads = total_next(g)
+    block_input_gradient = in_line(lay_out, share_order, back_parts)
+    out_parts = spread_share(gather_share(out_held))
     LINE.last = LINE.last + (g_bias, g_vec)
     grads = total_next(turns[-1])
+    output = in_line(lay_out, share_order, out_parts)
+    LINE.weight = 1
     g_in, g_outs = grads[:slots_in], grads[slots_in:]
     local_squares = (
         jnp.sum(jnp.concatenate(squares, 0)) + jnp.sum(g_bias * g_bias) + jnp.sum(g_vec * g_vec) * (1.0 / n_tensor)
     )
     local_squares = total_over(jnp.full((1, LANES), local_squares), "tensor", n_tensor)
-    bit = 1
-    while bit < n_dp:
-        pairs_at = [(i, i ^ bit) for i in range(n_dp)]
-        local_squares = local_squares + lax.ppermute(local_squares, "dp", pairs_at)
-        bit *= 2
+    local_squares = total_over(local_squares, "dp", n_dp)
     grad_norm = jnp.sqrt(local_squares[0, 0])
     factor = CLIP_AT / jnp.maximum(grad_norm, CLIP_AT)
 

time: 816 us -> 797 us (0.977)
  waiting for transfers between devices: 257 us -> 240 us
    ppermute x19, waiting for transfers between devices: 157 us -> 96.9 us  [shift(): return lax.ppermute(values, axis, pairs)]
    reduce_scatter x3, waiting for transfers between devices: 0.01 us -> 46.3 us  [scatter(): lax.psum_scatter(out, 'dp', scatter_dimension=0, axis_index_groups=lines,...]
  transfers between devices with their start and end apart: 51 -> 45, of which waited for: 20 -> 18; matrix products, arithmetic and copies ran while one was open for 3% -> 6% of each run, Pallas kernels for 53% -> 53%
where the time goes in v4:
time: 797 us; the launch traced here: 790 us
  Pallas kernels  438 us (55%)
  waiting for transfers between devices  240 us (30%)
  starting transfers between devices  44.3 us (6%)
  other arithmetic  35.3 us (4%)
  between operations  19.5 us (2%)
  local copies, waits for them, and re-layouts  13.5 us (2%)
    pallas_call x41, Pallas kernels, launch(): pl.pallas_call(trimmed, grid_spec=pltpu.PrefetchScalarGridSpec(num_scalar...  438 us
    ppermute x19, waiting for transfers between devices, shift(): return lax.ppermute(values, axis, pairs)  96.9 us
    all_gather x6, waiting for transfers between devices, body(): along.append(lax.all_gather(cast, 'dp', axis=0, axis_index_groups=lines))  83 us
    reduce_scatter x3, waiting for transfers between devices, scatter(): lax.psum_scatter(out, 'dp', scatter_dimension=0, axis_index_groups=lines,...  46.3 us
    ppermute x19, starting transfers between devices, shift(): return lax.ppermute(values, axis, pairs)  16.9 us
    transpose x2, other arithmetic, slot_major(): return [a.transpose(1, 0, 2) for a in arrays]  16 us
  transfers between devices with their start and end apart: 45, of which 18 were waited for; matrix products, arithmetic and copies ran while one was open for 6% of the time, Pallas kernels for 53%

profile of v4, /device:TPU:0, one launch (start us, length us, event | category | flops | bytes accessed | tf_op | source)
XLA Modules:
  0.0 790.0 jit_solution(7460707442304363397)
XLA Ops:
  45.4 18.0 %shard_map.295 = (bf16[2048,2048]{1,0:T(8,128)(2,1)}, bf16[2048,2048]{1,0:T(8,128)(2,1)}, bf16[2048,2048]{1,0:T(8,128)(2,1)}) custom-call(bf16[2048,2048]{1,0:T(8,128)(2,1)} %refs_2_.13, bf16[2048,2048]{1,0:T(8,128)(2,1)} %refs_3_.1, f32[4,2048]{1,0:T(4,128)} %bitcast.147, bf16[2,256,512]{2,1,0:T(8,128)(2,1)} %shard_map.294.refs_3_, ...), custom_call_target="tpu_custom_call" | custom-call | flops 200000000 | bytes 1 | tf_op jit(solution)/shard_map/pallas_call | solution.py:55
  66.3 40.4 %all-gather.15.cloned.1.call-done = bf16[8,256,512]{2,1,0:T(8,128)(2,1)} async-done(((bf16[2,256,512]{2,1,0:T(8,128)(2,1)}), bf16[8,256,512]{2,1,0:T(8,128)(2,1)}) %all-gather.15.cloned.1.call-update) | async-done | bytes 2097168 | tf_op jit(solution)/shard_map/all_gather | solution.py:764
  110.9 42.6 %all-gather.17.cloned.1.call-done = bf16[8,256,512]{2,1,0:T(8,128)(2,1)} async-done(((bf16[2,256,512]{2,1,0:T(8,128)(2,1)}), bf16[8,256,512]{2,1,0:T(8,128)(2,1)}) %all-gather.17.cloned.1.call-update) | async-done | bytes 2097168 | tf_op jit(solution)/shard_map/all_gather | solution.py:764
  155.9 26.5 %shard_map.300 = (bf16[2048,512]{1,0:T(8,128)(2,1)}, bf16[2048,512]{1,0:T(8,128)(2,1)}, bf16[2048,512]{1,0:T(8,128)(2,1)}, bf16[2048,512]{1,0:T(8,128)(2,1)}) custom-call(s32[8]{0:T(128)} %stack.83.refs_0_, bf16[2048,2048]{1,0:T(8,128)(2,1)} %get-tuple-element.56.refs_1_, bf16[2048,2048]{1,0:T(8,128)(2,1)} %refs_3_.1, f32[7,512]{1,0:T(8,128)} %reshape.328.refs_3_, ...), custom_call_target="tpu_custom_call" | custom-call | flops 200000000 | bytes 1 | tf_op jit(solution)/shard_map/pallas_call | solution.py:55
  182.4 38.8 %shard_map.301 = (bf16[2048,512]{1,0:T(8,128)(2,1)}, bf16[2048,512]{1,0:T(8,128)(2,1)}, bf16[2048,512]{1,0:T(8,128)(2,1)}, bf16[2048,512]{1,0:T(8,128)(2,1)}, f32[3,512]{1,0:T(4,128)}) custom-call(s32[8]{0:T(128)} %and_select_fusion.1.refs_5_.refs_0_, bf16[2048,512]{1,0:T(8,128)(2,1)} %get-tuple-element.58.refs_1_, ...), custom_call_target="tpu_custom_call" | custom-call | flops 200000000 | bytes 1 | tf_op jit(solution)/shard_map/pallas_call | solution.py:55
  221.8 39.1 %shard_map.303 = (bf16[2048,512]{1,0:T(8,128)(2,1)}, bf16[2048,512]{1,0:T(8,128)(2,1)}, bf16[2048,512]{1,0:T(8,128)(2,1)}, bf16[2048,512]{1,0:T(8,128)(2,1)}, f32[3,512]{1,0:T(4,128)}) custom-call(s32[8]{0:T(128)} %and_select_fusion.1.refs_5_.refs_0_, ...), custom_call_target="tpu_custom_call", output_to_operand_aliasing={{0}: (7, {}), {1}: (8, {}), {2}: (9, {}), {3}: (10, {}), {4... | custom-call | flops 200000000 | bytes 1 | tf_op jit(solution)/shard_map/pallas_call | solution.py:55
  263.1 28.7 %shard_map.305.refs_1_ = bf16[4,2,4,256,512]{4,3,2,1,0:T(8,128)(2,1)} custom-call(s32[2]{0:T(128)} %iota.21.refs_0_, bf16[4,2,256,2048]{3,2,1,0:T(8,128)(2,1)} %bitcast.132, bf16[4,2,256,2048]{3,2,1,0:T(8,128)(2,1)} %bitcast.121, bf16[2048,512]{1,0:T(8,128)(2,1)} %get-tuple-element.69.refs_3_.refs_2_, bf16[2048,512]{1,0:T(8,128)(2,1)} %get-tuple-element.70.refs_4_.refs_3_, ...), custom_call_target="tpu_custom_call" | custom-call | flops 200000000 | bytes 1 | tf_op jit(solution)/shard_map/pallas_call | solution.py:55
  297.3 16.7 %shard_map.307 = (bf16[2048,512]{1,0:T(8,128)(2,1)}, bf16[2048,512]{1,0:T(8,128)(2,1)}, f32[1,512]{1,0:T(1,128)}) custom-call(s32[8]{0:T(128)} %stack.83.refs_0_, bf16[2048,2048]{1,0:T(8,128)(2,1)} %get-tuple-element.56.refs_1_, bf16[2048,2048]{1,0:T(8,128)(2,1)} %refs_3_.1, f32[1,512]{1,0:T(1,128)} %slice.58.refs_3_, ...), custom_call_target="tpu_custom_call" | custom-call | flops 1000000000 | bytes 1 | tf_op jit(solution)/shard_map/pallas_call | solution.py:55
  314.0 15.9 %shard_map.308 = (bf16[2048,512]{1,0:T(8,128)(2,1)}, bf16[2048,512]{1,0:T(8,128)(2,1)}, f32[1,512]{1,0:T(1,128)}) custom-call(s32[8]{0:T(128)} %stack.83.refs_0_, bf16[2048,2048]{1,0:T(8,128)(2,1)} %get-tuple-element.56.refs_1_, bf16[2048,2048]{1,0:T(8,128)(2,1)} %refs_3_.1, f32[1,512]{1,0:T(1,128)} %slice.60.refs_3_, ...), custom_call_target="tpu_custom_call" | custom-call | flops 1000000000 | bytes 1 | tf_op jit(solution)/shard_map/pallas_call | solution.py:55
  331.2 15.8 %shard_map.310 = (bf16[2048,512]{1,0:T(8,128)(2,1)}, bf16[2048,512]{1,0:T(8,128)(2,1)}, f32[1,512]{1,0:T(1,128)}) custom-call(s32[8]{0:T(128)} %stack.83.refs_0_, bf16[2048,2048]{1,0:T(8,128)(2,1)} %get-tuple-element.56.refs_1_, bf16[2048,2048]{1,0:T(8,128)(2,1)} %refs_3_.1, f32[1,512]{1,0:T(1,128)} %slice.62.refs_3_, ...), custom_call_target="tpu_custom_call" | custom-call | flops 1000000000 | bytes 1 | tf_op jit(solution)/shard_map/pallas_call | solution.py:55
  347.1 11.5 %collective-permute-done.12.refs_0_ = bf16[4,2,256,512]{3,2,1,0:T(8,128)(2,1)} collective-permute-done((bf16[4,2,256,512]{3,2,1,0:T(8,128)(2,1)}, bf16[4,2,256,512]{3,2,1,0:T(8,128)(2,1)}, u32[]{:S(2)}, u32[]{:S(2)}) %collective-permute-start.12) | collective-permute-done | bytes 2097184 | tf_op jit(solution)/shard_map/ppermute | solution.py:685
  358.5 16.6 %shard_map.312.refs_6_ = bf16[4,1,4,256,512]{4,3,2,1,0:T(8,128)(2,1)} custom-call(s32[1]{0:T(128)} %bitcast.9.refs_0_, bf16[4,2,256,2048]{3,2,1,0:T(8,128)(2,1)} %bitcast.133, bf16[4,2,256,2048]{3,2,1,0:T(8,128)(2,1)} %bitcast.122, bf16[2048,512]{1,0:T(8,128)(2,1)} %get-tuple-element.79.refs_3_.refs_5_, bf16[2048,512]{1,0:T(8,128)(2,1)} %get-tuple-element.73.refs_4_.refs_3_, ...), custom_call_target="tpu_custom_call" | custom-call | flops 999999995904 | bytes 1 | tf_op jit(solution)/shard_map/pallas_call | solution.py:55
  375.5 15.9 %shard_map.313 = (bf16[2048,512]{1,0:T(8,128)(2,1)}, bf16[2048,512]{1,0:T(8,128)(2,1)}, f32[1,512]{1,0:T(1,128)}) custom-call(s32[8]{0:T(128)} %stack.83.refs_0_, bf16[2048,2048]{1,0:T(8,128)(2,1)} %get-tuple-element.56.refs_1_, bf16[2048,2048]{1,0:T(8,128)(2,1)} %refs_3_.1, f32[1,512]{1,0:T(1,128)} %slice.64.refs_3_, ...), custom_call_target="tpu_custom_call" | custom-call | flops 1000000000 | bytes 1 | tf_op jit(solution)/shard_map/pallas_call | solution.py:55
  391.5 16.8 %shard_map.314.refs_21_ = bf16[4,1,4,256,512]{4,3,2,1,0:T(8,128)(2,1)} custom-call(s32[1]{0:T(128)} %bitcast.9.refs_0_, bf16[4,2,256,2048]{3,2,1,0:T(8,128)(2,1)} %bitcast.134, bf16[4,2,256,2048]{3,2,1,0:T(8,128)(2,1)} %bitcast.123, bf16[2048,512]{1,0:T(8,128)(2,1)} %get-tuple-element.82.refs_3_.refs_7_, ...), custom_call_target="tpu_custom_call" | custom-call | flops 999999995904 | bytes 1 | tf_op jit(solution)/shard_map/pallas_call | solution.py:55
  408.3 25.2 %shard_map.315.refs_19_ = bf16[1024,2048]{1,0:T(8,128)(2,1)} custom-call(s32[8]{0:T(128)} %stack.83.refs_0_, s32[2]{0:T(128)} %pad_add_fusion.2.refs_1_, bf16[2048,512]{1,0:T(8,128)(2,1)} %get-tuple-element.69.refs_3_.refs_2_, bf16[2048,512]{1,0:T(8,128)(2,1)} %get-tuple-element.70.refs_4_.refs_3_, bf16[2048,512]{1,0:T(8,128)(2,1)} %get-tuple-element.71.refs_5_.refs_4_, ...), custom_call_target="tpu_custom_call" | custom-call | flops 999999995904 | bytes 1 | tf_op jit(solution)/shard_map/pallas_call | solution.py:55
  433.6 19.3 %shard_map.316.refs_22_ = bf16[1024,2048]{1,0:T(8,128)(2,1)} custom-call(s32[8]{0:T(128)} %stack.83.refs_0_, s32[2]{0:T(128)} %pad_add_fusion.2.refs_1_, bf16[2048,512]{1,0:T(8,128)(2,1)} %get-tuple-element.67.refs_6_.refs_2_, bf16[2048,512]{1,0:T(8,128)(2,1)} %get-tuple-element.73.refs_4_.refs_3_, bf16[2048,512]{1,0:T(8,128)(2,1)} %get-tuple-element.75.refs_6_.refs_4_, ...), custom_call_target="tpu_custom_call" | custom-call | flops 999999995904 | bytes 1 | tf_op jit(solution)/shard_map/pallas_call | solution.py:55
  453.5 28.1 %shard_map.317 = (f32[512,2048]{1,0:T(8,128)}, bf16[512,2048]{1,0:T(8,128)(2,1)}) custom-call(s32[8]{0:T(128)} %stack.83.refs_0_, s32[2]{0:T(128)} %pad_add_fusion.1.refs_1_, bf16[2048,512]{1,0:T(8,128)(2,1)} %get-tuple-element.69.refs_3_.refs_2_, bf16[2048,512]{1,0:T(8,128)(2,1)} %get-tuple-element.70.refs_4_.refs_3_, ...), custom_call_target="tpu_custom_call" | custom-call | flops 999999995904 | bytes 1 | tf_op jit(solution)/shard_map/pallas_call | solution.py:55
  483.1 16.9 %shard_map.318.refs_20_ = bf16[4,1,4,256,512]{4,3,2,1,0:T(8,128)(2,1)} custom-call(s32[1]{0:T(128)} %bitcast.5.refs_0_, bf16[4,2,256,2048]{3,2,1,0:T(8,128)(2,1)} %bitcast.135, bf16[4,2,256,2048]{3,2,1,0:T(8,128)(2,1)} %bitcast.124, bf16[2048,512]{1,0:T(8,128)(2,1)} %get-tuple-element.79.refs_3_.refs_5_, ...), custom_call_target="tpu_custom_call" | custom-call | flops 999999995904 | bytes 1 | tf_op jit(solution)/shard_map/pallas_call | solution.py:55
  500.0 22.0 %shard_map.319 = (f32[512,2048]{1,0:T(8,128)}, bf16[512,2048]{1,0:T(8,128)(2,1)}) custom-call(s32[8]{0:T(128)} %stack.83.refs_0_, s32[2]{0:T(128)} %pad_add_fusion.1.refs_1_, bf16[2048,512]{1,0:T(8,128)(2,1)} %get-tuple-element.67.refs_6_.refs_2_, bf16[2048,512]{1,0:T(8,128)(2,1)} %get-tuple-element.73.refs_4_.refs_3_, ...), custom_call_target="tpu_custom_call" | custom-call | flops 999999995904 | bytes 1 | tf_op jit(solution)/shard_map/pallas_call | solution.py:55
  522.0 7.5 collective-permute-done.17.refs_5_
  529.6 7.7 shard_map.320
  548.9 45.8 %collective-permute-done.16.refs_4_ = bf16[512,2048]{1,0:T(8,128)(2,1)} collective-permute-done((bf16[512,2048]{1,0:T(8,128)(2,1)S(1)}, bf16[512,2048]{1,0:T(8,128)(2,1)}, u32[]{:S(2)}, u32[]{:S(2)}) %collective-permute-start.16) | collective-permute-done | bytes 2097184 | tf_op jit(solution)/shard_map/ppermute | solution.py:685
  594.7 5.2 shard_map.321.refs_8_.refs_1_
  608.0 29.4 %collective-permute-done.23.refs_7_ = bf16[4,1,4,256,512]{4,3,2,1,0:T(8,128)(2,1)} collective-permute-done((bf16[4,1,4,256,512]{4,3,2,1,0:T(8,128)(2,1)}, bf16[4,1,4,256,512]{4,3,2,1,0:T(8,128)(2,1)}, u32[]{:S(2)}, u32[]{:S(2)}) %collective-permute-start.23) | collective-permute-done | bytes 4194336 | tf_op jit(solution)/shard_map/ppermute | solution.py:685
  638.0 16.7 %shard_map.322.refs_3_ = bf16[4,1,4,256,512]{4,3,2,1,0:T(8,128)(2,1)} custom-call(s32[1]{0:T(128)} %bitcast.5.refs_0_, bf16[4,2,256,2048]{3,2,1,0:T(8,128)(2,1)} %bitcast.136, bf16[4,2,256,2048]{3,2,1,0:T(8,128)(2,1)} %bitcast.125, bf16[2048,512]{1,0:T(8,128)(2,1)} %get-tuple-element.82.refs_3_.refs_7_, bf16[2048,512]{1,0:T(8,128)(2,1)} %get-tuple-element.77.refs_4_.refs_5_, ...), custom_call_target="tpu_custom_call" | custom-call | flops 999999995904 | bytes 1 | tf_op jit(solution)/shard_map/pallas_call | solution.py:55
  660.8 4.5 shard_map.323
  673.0 10.8 %shard_map.326.refs_1_ = bf16[2048,2048]{1,0:T(8,128)(2,1)} custom-call(s32[4]{0:T(128)} %pad_add_fusion.refs_0_, bf16[512,2048]{1,0:T(8,128)(2,1)} %get-tuple-element.90.refs_1_, bf16[512,2048]{1,0:T(8,128)(2,1)} %collective-permute-done.20.refs_2_, bf16[512,2048]{1,0:T(8,128)(2,1)} %shard_map.324.refs_3_, ...), custom_call_target="tpu_custom_call" | custom-call | flops 999999995904 | bytes 1 | tf_op jit(solution)/shard_map/pallas_call | solution.py:55
  683.9 46.3 %reduce-scatter.8.cloned.1.call-done.refs_1_ = bf16[4,256,512]{2,1,0:T(8,128)(2,1)} async-done(((bf16[16,256,512]{2,1,0:T(8,128)(2,1)}), bf16[4,256,512]{2,1,0:T(8,128)(2,1)}) %reduce-scatter.8.cloned.1.call-update) | async-done | bytes 1048592 | tf_op jit(solution)/shard_map/reduce_scatter | solution.py:806
  730.3 4.4 shard_map.328
  755.1 8.9 %fusion.8 = (f32[256,5,512]{2,0,1:T(8,128)}, f32[256,5,512]{2,0,1:T(8,128)}, f32[256,5,512]{2,0,1:T(8,128)}) fusion(f32[]{:T(128)S(6)} %div.99, f32[12,256,512]{2,1,0:T(8,128)} %get-tuple-element.96, f32[256,5,512]{2,0,1:T(8,128)} %param.26, f32[256,5,512]{2,0,1:T(8,128)} %param.25, f32[256,5,512]{2,0,1:T(8,128)S(1)} %copy-done.1), kind=kLoop, calls=%fused_computation.22 | loop fusion | flops 10485760 | bytes 18350084 | tf_op jit(solution)/shard_map/transpose | solution.py:934
  764.0 7.1 fusion.7
  771.1 10.8 %shard_map.329 = bf16[2048,2048]{1,0:T(8,128)(2,1)} custom-call(s32[4]{0:T(128)} %pad_add_fusion.refs_0_, bf16[512,2048]{1,0:T(8,128)(2,1)} %shard_map.321.refs_8_.refs_1_, bf16[512,2048]{1,0:T(8,128)(2,1)} %collective-permute-done.18.refs_2_, bf16[512,2048]{1,0:T(8,128)(2,1)} %shard_map.327.refs_3_, bf16[512,2048]{1,0:T(8,128)(2,1)} %collective-permute-done.25.refs_4_, ...), custom_call_target="tpu_custom_call" | custom-call | flops 999999995904 | bytes 1 | tf_op jit(solution)/shard_map/pallas_call | solution.py:55
  (234 shorter events, 110.4 us)
Async XLA Ops:
  7.2 56.3 %all-gather.13.cloned.1.call-start = ((), (), s32[]{:S(2)}) async-start(), calls=%async_computation.6 | async-start | bytes 2621440 | tf_op jit(solution)/shard_map/all_gather | solution.py:764
  9.3 97.3 %all-gather.15.cloned.1.call-start = ((), (), s32[]{:S(2)}) async-start(), calls=%async_computation.7 | async-start | bytes 2621440 | tf_op jit(solution)/shard_map/all_gather | solution.py:764
  11.4 142.0 %all-gather.17.cloned.1.call-start = ((), (), s32[]{:S(2)}) async-start(), calls=%async_computation.8 | async-start | bytes 2621440 | tf_op jit(solution)/shard_map/all_gather | solution.py:764
  13.5 207.7 %all-gather.19.cloned.1.call-start = ((), (), s32[]{:S(2)}) async-start(), calls=%async_computation.9 | async-start | bytes 2621440 | tf_op jit(solution)/shard_map/all_gather | solution.py:764
  15.7 245.2 %all-gather.23.cloned.1.call-start = ((), (), s32[]{:S(2)}) async-start(), calls=%async_computation.11 | async-start | bytes 2621440 | tf_op jit(solution)/shard_map/all_gather | solution.py:764
  17.8 274.0 %all-gather.21.cloned.1.call-start = ((), (), s32[]{:S(2)}) async-start(), calls=%async_computation.10 | async-start | bytes 2621440 | tf_op jit(solution)/shard_map/all_gather | solution.py:764
  18.1 20.9 %collective-permute-start.6 = (f32[1,1472]{1,0:T(1,128)S(1)}, f32[1,1472]{1,0:T(1,128)S(1)}, u32[]{:S(2)}, u32[]{:S(2)}) collective-permute-start(f32[1,1472]{1,0:T(1,128)S(1)} %maximum_convert_fusion), channel_id=1, source_target_pairs={{0,4},{4,8},{8,12},{12,16},{16,20},{20,24},{24,28},{28,0},{1,5},{5... | collective-permute-start | bytes 17672 | tf_op jit(solution)/shard_map/ppermute | solution.py:665
  21.1 19.4 %collective-permute-start.5 = (f32[1,1472]{1,0:T(1,128)S(1)}, f32[1,1472]{1,0:T(1,128)S(1)}, u32[]{:S(2)}, u32[]{:S(2)}) collective-permute-start(f32[1,1472]{1,0:T(1,128)S(1)} %maximum_convert_fusion), channel_id=1, source_target_pairs={{0,8},{4,12},{8,16},{12,20},{16,24},{20,28},{24,0},{28,4},{1,9},{5... | collective-permute-start | bytes 17672 | tf_op jit(solution)/shard_map/ppermute | solution.py:665
  22.7 20.2 %collective-permute-start.4 = (f32[1,1472]{1,0:T(1,128)S(1)}, f32[1,1472]{1,0:T(1,128)S(1)}, u32[]{:S(2)}, u32[]{:S(2)}) collective-permute-start(f32[1,1472]{1,0:T(1,128)S(1)} %maximum_convert_fusion), channel_id=1, source_target_pairs={{0,12},{4,16},{8,20},{12,24},{16,28},{20,0},{24,4},{28,8},{1,13},{... | collective-permute-start | bytes 17672 | tf_op jit(solution)/shard_map/ppermute | solution.py:665
  31.2 573.7 %reduce-scatter.4.cloned.1.call-start = ((), (), s32[]{:S(2)}) async-start(), calls=%async_computation.3 | async-start | bytes 10485760 | tf_op jit(solution)/shard_map/reduce_scatter | solution.py:806
  63.4 46.1 %collective-permute-start.7 = (bf16[4,2,256,512]{3,2,1,0:T(8,128)(2,1)}, bf16[4,2,256,512]{3,2,1,0:T(8,128)(2,1)S(1)}, u32[]{:S(2)}, u32[]{:S(2)}) collective-permute-start(bf16[4,2,256,512]{3,2,1,0:T(8,128)(2,1)} %shard_map.296.refs_1_.refs_5_.refs_9_.refs_7_), channel_id=1, source_target_pairs={{0,4},{4,0},{8,12},{12,8},{16,20},{20,16},{24,28},{28,24},{1,5},{5... | collective-permute-start | bytes 6291464 | tf_op jit(solution)/shard_map/ppermute | solution.py:685
  106.6 49.2 %collective-permute-start.8 = (bf16[4,2,256,512]{3,2,1,0:T(8,128)(2,1)}, bf16[4,2,256,512]{3,2,1,0:T(8,128)(2,1)}, u32[]{:S(2)}, u32[]{:S(2)}) collective-permute-start(bf16[4,2,256,512]{3,2,1,0:T(8,128)(2,1)} %shard_map.297.refs_1_.refs_7_.refs_11_.refs_9_), channel_id=1, source_target_pairs={{0,4},{4,0},{8,12},{12,8},{16,20},{20,16},{24,28},{28,24},{1,5},{5... | collective-permute-start | bytes 6291464 | tf_op jit(solution)/shard_map/ppermute | solution.py:685
  153.5 143.8 %collective-permute-start.9 = (bf16[4,2,256,512]{3,2,1,0:T(8,128)(2,1)}, bf16[4,2,256,512]{3,2,1,0:T(8,128)(2,1)}, u32[]{:S(2)}, u32[]{:S(2)}) collective-permute-start(bf16[4,2,256,512]{3,2,1,0:T(8,128)(2,1)} %shard_map.299.refs_9_.refs_4_.refs_13_.refs_11_), channel_id=1, source_target_pairs={{0,4},{4,0},{8,12},{12,8},{16,20},{20,16},{24,28},{28,24},{1,5},{5... | collective-permute-start | bytes 6291464 | tf_op jit(solution)/shard_map/ppermute | solution.py:685
  221.3 92.7 %collective-permute-start.10 = (bf16[4,2,256,512]{3,2,1,0:T(8,128)(2,1)}, bf16[4,2,256,512]{3,2,1,0:T(8,128)(2,1)}, u32[]{:S(2)}, u32[]{:S(2)}) collective-permute-start(bf16[4,2,256,512]{3,2,1,0:T(8,128)(2,1)} %shard_map.302.refs_12_.refs_4_.refs_15_.refs_13_), channel_id=1, source_target_pairs={{0,4},{4,0},{8,12},{12,8},{16,20},{20,16},{24,28},{28,24},{1,5},{5... | collective-permute-start | bytes 6291464 | tf_op jit(solution)/shard_map/ppermute | solution.py:685
  260.9 69.0 %collective-permute-start.11 = (bf16[4,2,256,512]{3,2,1,0:T(8,128)(2,1)}, bf16[4,2,256,512]{3,2,1,0:T(8,128)(2,1)S(1)}, u32[]{:S(2)}, u32[]{:S(2)}) collective-permute-start(bf16[4,2,256,512]{3,2,1,0:T(8,128)(2,1)} %shard_map.304.refs_7_.refs_4_.refs_17_.refs_15_), channel_id=1, source_target_pairs={{0,4},{4,0},{8,12},{12,8},{16,20},{20,16},{24,28},{28,24},{1,5},{5... | collective-permute-start | bytes 6291464 | tf_op jit(solution)/shard_map/ppermute | solution.py:685
  291.8 66.7 %collective-permute-start.12 = (bf16[4,2,256,512]{3,2,1,0:T(8,128)(2,1)}, bf16[4,2,256,512]{3,2,1,0:T(8,128)(2,1)}, u32[]{:S(2)}, u32[]{:S(2)}) collective-permute-start(bf16[4,2,256,512]{3,2,1,0:T(8,128)(2,1)} %shard_map.306.refs_6_.refs_4_.refs_19_.refs_17_), channel_id=1, source_target_pairs={{0,4},{4,0},{8,12},{12,8},{16,20},{20,16},{24,28},{28,24},{1,5},{5... | collective-permute-start | bytes 6291464 | tf_op jit(solution)/shard_map/ppermute | solution.py:685
  297.2 368.2 %reduce-scatter.6.cloned.1.call-start = ((), (), s32[]{:S(2)}) async-start(), calls=%async_computation.4 | async-start | bytes 5242880 | tf_op jit(solution)/shard_map/reduce_scatter | solution.py:806
  375.1 108.0 %collective-permute-start.14 = (bf16[4,1,4,256,512]{4,3,2,1,0:T(8,128)(2,1)}, bf16[4,1,4,256,512]{4,3,2,1,0:T(8,128)(2,1)}, u32[]{:S(2)}, u32[]{:S(2)}) collective-permute-start(bf16[4,1,4,256,512]{4,3,2,1,0:T(8,128)(2,1)} %shard_map.312.refs_6_), channel_id=1, source_target_pairs={{0,4},{4,0},{8,12},{12,8},{16,20},{20,16},{24,28},{28,24},{1,5},{5... | collective-permute-start | bytes 12582920 | tf_op jit(solution)/shard_map/ppermute | solution.py:685
  433.5 20.0 %collective-permute-start.15 = (bf16[1024,2048]{1,0:T(8,128)(2,1)}, bf16[1024,2048]{1,0:T(8,128)(2,1)}, u32[]{:S(2)}, u32[]{:S(2)}) collective-permute-start(bf16[1024,2048]{1,0:T(8,128)(2,1)} %shard_map.315.refs_19_), channel_id=1, source_target_pairs={{0,1},{1,0},{2,3},{3,2},{4,5},{5,4},{6,7},{7,6},{8,9},{9,8},{10,11... | collective-permute-start | bytes 12582920 | tf_op jit(solution)/shard_map/ppermute | solution.py:685
  452.9 47.1 %collective-permute-start.13 = (bf16[1024,2048]{1,0:T(8,128)(2,1)}, bf16[1024,2048]{1,0:T(8,128)(2,1)}, u32[]{:S(2)}, u32[]{:S(2)}) collective-permute-start(bf16[1024,2048]{1,0:T(8,128)(2,1)} %shard_map.316.refs_22_), channel_id=1, source_target_pairs={{0,1},{1,0},{2,3},{3,2},{4,5},{5,4},{6,7},{7,6},{8,9},{9,8},{10,11... | collective-permute-start | bytes 12582920 | tf_op jit(solution)/shard_map/ppermute | solution.py:685
  481.6 48.0 %collective-permute-start.17 = (bf16[512,2048]{1,0:T(8,128)(2,1)}, bf16[512,2048]{1,0:T(8,128)(2,1)}, u32[]{:S(2)}, u32[]{:S(2)}) collective-permute-start(bf16[512,2048]{1,0:T(8,128)(2,1)} %get-tuple-element.85.refs_8_), channel_id=1, source_target_pairs={{0,2},{1,3},{2,0},{3,1},{4,6},{5,7},{6,4},{7,5},{8,10},{9,11},{10,... | collective-permute-start | bytes 6291464 | tf_op jit(solution)/shard_map/ppermute | solution.py:685
  545.6 91.8 %collective-permute-start.23 = (bf16[4,1,4,256,512]{4,3,2,1,0:T(8,128)(2,1)}, bf16[4,1,4,256,512]{4,3,2,1,0:T(8,128)(2,1)}, u32[]{:S(2)}, u32[]{:S(2)}) collective-permute-start(bf16[4,1,4,256,512]{4,3,2,1,0:T(8,128)(2,1)} %shard_map.314.refs_21_), channel_id=1, source_target_pairs={{0,4},{4,0},{8,12},{12,8},{16,20},{20,16},{24,28},{28,24},{1,5},{5... | collective-permute-start | bytes 12582920 | tf_op jit(solution)/shard_map/ppermute | solution.py:685
  546.0 48.7 %collective-permute-start.16 = (bf16[512,2048]{1,0:T(8,128)(2,1)S(1)}, bf16[512,2048]{1,0:T(8,128)(2,1)}, u32[]{:S(2)}, u32[]{:S(2)}) collective-permute-start(bf16[512,2048]{1,0:T(8,128)(2,1)S(1)} %copy-done.23), channel_id=1, source_target_pairs={{0,2},{1,3},{2,0},{3,1},{4,6},{5,7},{6,4},{7,5},{8,10},{9,11},{10,... | collective-permute-start | bytes 6291464 | tf_op jit(solution)/shard_map/ppermute | solution.py:685
  547.5 182.7 %reduce-scatter.8.cloned.1.call-start = ((), (), s32[]{:S(2)}) async-start(), calls=%async_computation.5 | async-start | bytes 5242880 | tf_op jit(solution)/shard_map/reduce_scatter | solution.py:806
  547.6 117.7 %collective-permute-start.21 = (bf16[512,2048]{1,0:T(8,128)(2,1)}, bf16[512,2048]{1,0:T(8,128)(2,1)}, u32[]{:S(2)}, u32[]{:S(2)}) collective-permute-start(bf16[512,2048]{1,0:T(8,128)(2,1)} %get-tuple-element.90.refs_1_), channel_id=1, source_target_pairs={{0,2},{1,3},{2,0},{3,1},{4,6},{5,7},{6,4},{7,5},{8,10},{9,11},{10,... | collective-permute-start | bytes 6291464 | tf_op jit(solution)/shard_map/ppermute | solution.py:685
  548.2 124.8 %collective-permute-start.20 = (bf16[512,2048]{1,0:T(8,128)(2,1)}, bf16[512,2048]{1,0:T(8,128)(2,1)}, u32[]{:S(2)}, u32[]{:S(2)}) collective-permute-start(bf16[512,2048]{1,0:T(8,128)(2,1)} %get-tuple-element.90.refs_1_), channel_id=1, source_target_pairs={{0,1},{1,0},{2,3},{3,2},{4,5},{5,4},{6,7},{7,6},{8,9},{9,8},{10,11... | collective-permute-start | bytes 6291464 | tf_op jit(solution)/shard_map/ppermute | solution.py:685
  548.9 52.4 %collective-permute-start.29 = (f32[1,9728]{1,0:T(1,128)}, f32[1,9728]{1,0:T(1,128)}, u32[]{:S(2)}, u32[]{:S(2)}) collective-permute-start(f32[1,9728]{1,0:T(1,128)} %fusion.12), channel_id=1, source_target_pairs={{0,8},{4,12},{8,0},{12,4},{16,24},{20,28},{24,16},{28,20},{1,9},{5... | collective-permute-start | bytes 116744 | tf_op jit(solution)/shard_map/ppermute | solution.py:673
  599.9 84.0 %collective-permute-start.19 = (bf16[512,2048]{1,0:T(8,128)(2,1)}, bf16[512,2048]{1,0:T(8,128)(2,1)}, u32[]{:S(2)}, u32[]{:S(2)}) collective-permute-start(bf16[512,2048]{1,0:T(8,128)(2,1)} %shard_map.321.refs_8_.refs_1_), channel_id=1, source_target_pairs={{0,2},{1,3},{2,0},{3,1},{4,6},{5,7},{6,4},{7,5},{8,10},{9,11},{10,... | collective-permute-start | bytes 6291464 | tf_op jit(solution)/shard_map/ppermute | solution.py:685
  602.7 52.0 %collective-permute-start.30 = (f32[1,9728]{1,0:T(1,128)}, f32[1,9728]{1,0:T(1,128)}, u32[]{:S(2)}, u32[]{:S(2)}) collective-permute-start(f32[1,9728]{1,0:T(1,128)} %add.241), channel_id=1, source_target_pairs={{0,16},{4,20},{8,24},{12,28},{16,0},{20,4},{24,8},{28,12},{1,17},{... | collective-permute-start | bytes 116744 | tf_op jit(solution)/shard_map/ppermute | solution.py:673
  637.4 23.4 %collective-permute-start.22 = (bf16[4,256,512]{2,1,0:T(8,128)(2,1)}, bf16[4,256,512]{2,1,0:T(8,128)(2,1)}, u32[]{:S(2)}, u32[]{:S(2)}) collective-permute-start(bf16[4,256,512]{2,1,0:T(8,128)(2,1)} %get-tuple-element.111), channel_id=1, source_target_pairs={{0,4},{4,0},{8,12},{12,8},{16,20},{20,16},{24,28},{28,24},{1,5},{5... | collective-permute-start | bytes 3145736 | tf_op jit(solution)/shard_map/ppermute | solution.py:685
  752.1 19.0 %collective-permute-start.18 = (bf16[512,2048]{1,0:T(8,128)(2,1)}, bf16[512,2048]{1,0:T(8,128)(2,1)}, u32[]{:S(2)}, u32[]{:S(2)}) collective-permute-start(bf16[512,2048]{1,0:T(8,128)(2,1)} %shard_map.321.refs_8_.refs_1_), channel_id=1, source_target_pairs={{0,1},{1,0},{2,3},{3,2},{4,5},{5,4},{6,7},{7,6},{8,9},{9,8},{10,11... | collective-permute-start | bytes 6291464 | tf_op jit(solution)/shard_map/ppermute | solution.py:685
  752.1 19.0 %collective-permute-start.25 = (bf16[512,2048]{1,0:T(8,128)(2,1)}, bf16[512,2048]{1,0:T(8,128)(2,1)}, u32[]{:S(2)}, u32[]{:S(2)}) collective-permute-start(bf16[512,2048]{1,0:T(8,128)(2,1)} %shard_map.327.refs_3_), channel_id=1, source_target_pairs={{0,1},{1,0},{2,3},{3,2},{4,5},{5,4},{6,7},{7,6},{8,9},{9,8},{10,11... | collective-permute-start | bytes 6291464 | tf_op jit(solution)/shard_map/ppermute | solution.py:685
  (40 other events, 432.5 us)
Sparse Core Ops, SparseCore 0:
  10.2 49.6 all-gather.12
  62.0 44.6 all-gather.14
  108.8 44.6 all-gather.16
  154.9 44.6 all-gather.18
  201.0 44.6 all-gather.22
  247.1 44.6 all-gather.20
  297.3 143.1 reduce-scatter.3
  547.6 75.4 reduce-scatter.5
  654.9 75.2 reduce-scatter.7

commit v5 on v4

--- a/solution.py
+++ b/solution.py
@@ -915,11 +915,11 @@
     back_parts = spread_share(gather_share(back_held))
     for g in turns[1:-1]:
         grads = total_next(g)
+    out_parts = spread_share(gather_share(out_held))
     block_input_gradient = in_line(lay_out, share_order, back_parts)
-    out_parts = spread_share(gather_share(out_held))
+    output = in_line(lay_out, share_order, out_parts)
     LINE.last = LINE.last + (g_bias, g_vec)
     grads = total_next(turns[-1])
-    output = in_line(lay_out, share_order, out_parts)
     LINE.weight = 1
     g_in, g_outs = grads[:slots_in], grads[slots_in:]
     local_squares = (

time: 797 us -> 786 us (0.986)
  waiting for transfers between devices: 240 us -> 229 us
    reduce_scatter x3, waiting for transfers between devices: 46.3 us -> 21.9 us  [scatter(): lax.psum_scatter(out, 'dp', scatter_dimension=0, axis_index_groups=lines,...]
    ppermute x19, waiting for transfers between devices: 96.9 us -> 110 us  [shift(): return lax.ppermute(values, axis, pairs)]
  transfers between devices with their start and end apart: 45 -> 45, of which waited for: 18 -> 19; matrix products, arithmetic and copies ran while one was open for 6% -> 3% of each run, Pallas kernels for 53% -> 55%
where the time goes in v5:
time: 786 us; the launch traced here: 779 us
  Pallas kernels  437 us (56%)
  waiting for transfers between devices  229 us (29%)
  starting transfers between devices  44.4 us (6%)
  other arithmetic  34.7 us (4%)
  between operations  19.5 us (2%)
  local copies, waits for them, and re-layouts  14.1 us (2%)
    pallas_call x41, Pallas kernels, launch(): pl.pallas_call(trimmed, grid_spec=pltpu.PrefetchScalarGridSpec(num_scalar...  437 us
    ppermute x19, waiting for transfers between devices, shift(): return lax.ppermute(values, axis, pairs)  110 us
    all_gather x6, waiting for transfers between devices, body(): along.append(lax.all_gather(cast, 'dp', axis=0, axis_index_groups=lines))  83.3 us
    reduce_scatter x3, waiting for transfers between devices, scatter(): lax.psum_scatter(out, 'dp', scatter_dimension=0, axis_index_groups=lines,...  21.9 us
    ppermute x19, starting transfers between devices, shift(): return lax.ppermute(values, axis, pairs)  20.5 us
    transpose x2, other arithmetic, slot_major(): return [a.transpose(1, 0, 2) for a in arrays]  16 us
  transfers between devices with their start and end apart: 45, of which 19 were waited for; matrix products, arithmetic and copies ran while one was open for 3% of the time, Pallas kernels for 55%

profile of v5, /device:TPU:0, one launch (start us, length us, event | category | flops | bytes accessed | tf_op | source)
XLA Modules:
  0.0 779.1 jit_solution(8563230175209998899)
XLA Ops:
  45.4 18.0 %shard_map.295 = (bf16[2048,2048]{1,0:T(8,128)(2,1)}, bf16[2048,2048]{1,0:T(8,128)(2,1)}, bf16[2048,2048]{1,0:T(8,128)(2,1)}) custom-call(bf16[2048,2048]{1,0:T(8,128)(2,1)} %refs_2_.13, bf16[2048,2048]{1,0:T(8,128)(2,1)} %refs_3_.1, f32[4,2048]{1,0:T(4,128)} %bitcast.147, bf16[2,256,512]{2,1,0:T(8,128)(2,1)} %shard_map.294.refs_3_, ...), custom_call_target="tpu_custom_call" | custom-call | flops 200000000 | bytes 1 | tf_op jit(solution)/shard_map/pallas_call | solution.py:55
  66.1 40.5 %all-gather.15.cloned.1.call-done = bf16[8,256,512]{2,1,0:T(8,128)(2,1)} async-done(((bf16[2,256,512]{2,1,0:T(8,128)(2,1)}), bf16[8,256,512]{2,1,0:T(8,128)(2,1)}) %all-gather.15.cloned.1.call-update) | async-done | bytes 2097168 | tf_op jit(solution)/shard_map/all_gather | solution.py:764
  110.7 42.8 %all-gather.17.cloned.1.call-done = bf16[8,256,512]{2,1,0:T(8,128)(2,1)} async-done(((bf16[2,256,512]{2,1,0:T(8,128)(2,1)}), bf16[8,256,512]{2,1,0:T(8,128)(2,1)}) %all-gather.17.cloned.1.call-update) | async-done | bytes 2097168 | tf_op jit(solution)/shard_map/all_gather | solution.py:764
  155.9 26.5 %shard_map.300 = (bf16[2048,512]{1,0:T(8,128)(2,1)}, bf16[2048,512]{1,0:T(8,128)(2,1)}, bf16[2048,512]{1,0:T(8,128)(2,1)}, bf16[2048,512]{1,0:T(8,128)(2,1)}) custom-call(s32[8]{0:T(128)} %stack.83.refs_0_, bf16[2048,2048]{1,0:T(8,128)(2,1)} %get-tuple-element.56.refs_1_, bf16[2048,2048]{1,0:T(8,128)(2,1)} %refs_3_.1, f32[7,512]{1,0:T(8,128)} %reshape.328.refs_3_, ...), custom_call_target="tpu_custom_call" | custom-call | flops 200000000 | bytes 1 | tf_op jit(solution)/shard_map/pallas_call | solution.py:55
  182.4 38.8 %shard_map.301 = (bf16[2048,512]{1,0:T(8,128)(2,1)}, bf16[2048,512]{1,0:T(8,128)(2,1)}, bf16[2048,512]{1,0:T(8,128)(2,1)}, bf16[2048,512]{1,0:T(8,128)(2,1)}, f32[3,512]{1,0:T(4,128)}) custom-call(s32[8]{0:T(128)} %and_select_fusion.1.refs_5_.refs_0_, bf16[2048,512]{1,0:T(8,128)(2,1)} %get-tuple-element.58.refs_1_, ...), custom_call_target="tpu_custom_call" | custom-call | flops 200000000 | bytes 1 | tf_op jit(solution)/shard_map/pallas_call | solution.py:55
  223.0 39.1 %shard_map.303 = (bf16[2048,512]{1,0:T(8,128)(2,1)}, bf16[2048,512]{1,0:T(8,128)(2,1)}, bf16[2048,512]{1,0:T(8,128)(2,1)}, bf16[2048,512]{1,0:T(8,128)(2,1)}, f32[3,512]{1,0:T(4,128)}) custom-call(s32[8]{0:T(128)} %and_select_fusion.1.refs_5_.refs_0_, ...), custom_call_target="tpu_custom_call", output_to_operand_aliasing={{0}: (7, {}), {1}: (8, {}), {2}: (9, {}), {3}: (10, {}), {4... | custom-call | flops 200000000 | bytes 1 | tf_op jit(solution)/shard_map/pallas_call | solution.py:55
  264.4 28.6 %shard_map.305.refs_1_ = bf16[4,2,4,256,512]{4,3,2,1,0:T(8,128)(2,1)} custom-call(s32[2]{0:T(128)} %iota.21.refs_0_, bf16[4,2,256,2048]{3,2,1,0:T(8,128)(2,1)} %bitcast.132, bf16[4,2,256,2048]{3,2,1,0:T(8,128)(2,1)} %bitcast.121, bf16[2048,512]{1,0:T(8,128)(2,1)} %get-tuple-element.69.refs_3_.refs_2_, bf16[2048,512]{1,0:T(8,128)(2,1)} %get-tuple-element.70.refs_4_.refs_3_, ...), custom_call_target="tpu_custom_call" | custom-call | flops 200000000 | bytes 1 | tf_op jit(solution)/shard_map/pallas_call | solution.py:55
  297.5 16.8 %shard_map.307 = (bf16[2048,512]{1,0:T(8,128)(2,1)}, bf16[2048,512]{1,0:T(8,128)(2,1)}, f32[1,512]{1,0:T(1,128)}) custom-call(s32[8]{0:T(128)} %stack.83.refs_0_, bf16[2048,2048]{1,0:T(8,128)(2,1)} %get-tuple-element.56.refs_1_, bf16[2048,2048]{1,0:T(8,128)(2,1)} %refs_3_.1, f32[1,512]{1,0:T(1,128)} %slice.58.refs_3_, ...), custom_call_target="tpu_custom_call" | custom-call | flops 1000000000 | bytes 1 | tf_op jit(solution)/shard_map/pallas_call | solution.py:55
  314.3 15.9 %shard_map.308 = (bf16[2048,512]{1,0:T(8,128)(2,1)}, bf16[2048,512]{1,0:T(8,128)(2,1)}, f32[1,512]{1,0:T(1,128)}) custom-call(s32[8]{0:T(128)} %stack.83.refs_0_, bf16[2048,2048]{1,0:T(8,128)(2,1)} %get-tuple-element.56.refs_1_, bf16[2048,2048]{1,0:T(8,128)(2,1)} %refs_3_.1, f32[1,512]{1,0:T(1,128)} %slice.60.refs_3_, ...), custom_call_target="tpu_custom_call" | custom-call | flops 1000000000 | bytes 1 | tf_op jit(solution)/shard_map/pallas_call | solution.py:55
  331.5 15.8 %shard_map.310 = (bf16[2048,512]{1,0:T(8,128)(2,1)}, bf16[2048,512]{1,0:T(8,128)(2,1)}, f32[1,512]{1,0:T(1,128)}) custom-call(s32[8]{0:T(128)} %stack.83.refs_0_, bf16[2048,2048]{1,0:T(8,128)(2,1)} %get-tuple-element.56.refs_1_, bf16[2048,2048]{1,0:T(8,128)(2,1)} %refs_3_.1, f32[1,512]{1,0:T(1,128)} %slice.62.refs_3_, ...), custom_call_target="tpu_custom_call" | custom-call | flops 1000000000 | bytes 1 | tf_op jit(solution)/shard_map/pallas_call | solution.py:55
  347.3 11.2 %collective-permute-done.12.refs_0_ = bf16[4,2,256,512]{3,2,1,0:T(8,128)(2,1)} collective-permute-done((bf16[4,2,256,512]{3,2,1,0:T(8,128)(2,1)}, bf16[4,2,256,512]{3,2,1,0:T(8,128)(2,1)}, u32[]{:S(2)}, u32[]{:S(2)}) %collective-permute-start.12) | collective-permute-done | bytes 2097184 | tf_op jit(solution)/shard_map/ppermute | solution.py:685
  358.5 16.6 %shard_map.312.refs_6_ = bf16[4,1,4,256,512]{4,3,2,1,0:T(8,128)(2,1)} custom-call(s32[1]{0:T(128)} %bitcast.9.refs_0_, bf16[4,2,256,2048]{3,2,1,0:T(8,128)(2,1)} %bitcast.133, bf16[4,2,256,2048]{3,2,1,0:T(8,128)(2,1)} %bitcast.122, bf16[2048,512]{1,0:T(8,128)(2,1)} %get-tuple-element.79.refs_3_.refs_5_, bf16[2048,512]{1,0:T(8,128)(2,1)} %get-tuple-element.73.refs_4_.refs_3_, ...), custom_call_target="tpu_custom_call" | custom-call | flops 999999995904 | bytes 1 | tf_op jit(solution)/shard_map/pallas_call | solution.py:55
  376.8 15.9 %shard_map.313 = (bf16[2048,512]{1,0:T(8,128)(2,1)}, bf16[2048,512]{1,0:T(8,128)(2,1)}, f32[1,512]{1,0:T(1,128)}) custom-call(s32[8]{0:T(128)} %stack.83.refs_0_, bf16[2048,2048]{1,0:T(8,128)(2,1)} %get-tuple-element.56.refs_1_, bf16[2048,2048]{1,0:T(8,128)(2,1)} %refs_3_.1, f32[1,512]{1,0:T(1,128)} %slice.64.refs_3_, ...), custom_call_target="tpu_custom_call" | custom-call | flops 1000000000 | bytes 1 | tf_op jit(solution)/shard_map/pallas_call | solution.py:55
  392.6 16.9 %shard_map.314.refs_21_ = bf16[4,1,4,256,512]{4,3,2,1,0:T(8,128)(2,1)} custom-call(s32[1]{0:T(128)} %bitcast.9.refs_0_, bf16[4,2,256,2048]{3,2,1,0:T(8,128)(2,1)} %bitcast.134, bf16[4,2,256,2048]{3,2,1,0:T(8,128)(2,1)} %bitcast.123, bf16[2048,512]{1,0:T(8,128)(2,1)} %get-tuple-element.82.refs_3_.refs_7_, ...), custom_call_target="tpu_custom_call" | custom-call | flops 999999995904 | bytes 1 | tf_op jit(solution)/shard_map/pallas_call | solution.py:55
  409.5 25.2 %shard_map.315.refs_19_ = bf16[1024,2048]{1,0:T(8,128)(2,1)} custom-call(s32[8]{0:T(128)} %stack.83.refs_0_, s32[2]{0:T(128)} %pad_add_fusion.2.refs_1_, bf16[2048,512]{1,0:T(8,128)(2,1)} %get-tuple-element.69.refs_3_.refs_2_, bf16[2048,512]{1,0:T(8,128)(2,1)} %get-tuple-element.70.refs_4_.refs_3_, bf16[2048,512]{1,0:T(8,128)(2,1)} %get-tuple-element.71.refs_5_.refs_4_, ...), custom_call_target="tpu_custom_call" | custom-call | flops 999999995904 | bytes 1 | tf_op jit(solution)/shard_map/pallas_call | solution.py:55
  434.8 19.4 %shard_map.316.refs_22_ = bf16[1024,2048]{1,0:T(8,128)(2,1)} custom-call(s32[8]{0:T(128)} %stack.83.refs_0_, s32[2]{0:T(128)} %pad_add_fusion.2.refs_1_, bf16[2048,512]{1,0:T(8,128)(2,1)} %get-tuple-element.67.refs_6_.refs_2_, bf16[2048,512]{1,0:T(8,128)(2,1)} %get-tuple-element.73.refs_4_.refs_3_, bf16[2048,512]{1,0:T(8,128)(2,1)} %get-tuple-element.75.refs_6_.refs_4_, ...), custom_call_target="tpu_custom_call" | custom-call | flops 999999995904 | bytes 1 | tf_op jit(solution)/shard_map/pallas_call | solution.py:55
  454.7 28.1 %shard_map.317 = (f32[512,2048]{1,0:T(8,128)}, bf16[512,2048]{1,0:T(8,128)(2,1)}) custom-call(s32[8]{0:T(128)} %stack.83.refs_0_, s32[2]{0:T(128)} %pad_add_fusion.1.refs_1_, bf16[2048,512]{1,0:T(8,128)(2,1)} %get-tuple-element.69.refs_3_.refs_2_, bf16[2048,512]{1,0:T(8,128)(2,1)} %get-tuple-element.70.refs_4_.refs_3_, ...), custom_call_target="tpu_custom_call" | custom-call | flops 999999995904 | bytes 1 | tf_op jit(solution)/shard_map/pallas_call | solution.py:55
  484.5 16.9 %shard_map.318.refs_20_ = bf16[4,1,4,256,512]{4,3,2,1,0:T(8,128)(2,1)} custom-call(s32[1]{0:T(128)} %bitcast.5.refs_0_, bf16[4,2,256,2048]{3,2,1,0:T(8,128)(2,1)} %bitcast.135, bf16[4,2,256,2048]{3,2,1,0:T(8,128)(2,1)} %bitcast.124, bf16[2048,512]{1,0:T(8,128)(2,1)} %get-tuple-element.79.refs_3_.refs_5_, ...), custom_call_target="tpu_custom_call" | custom-call | flops 999999995904 | bytes 1 | tf_op jit(solution)/shard_map/pallas_call | solution.py:55
  501.4 22.0 %shard_map.319 = (f32[512,2048]{1,0:T(8,128)}, bf16[512,2048]{1,0:T(8,128)(2,1)}) custom-call(s32[8]{0:T(128)} %stack.83.refs_0_, s32[2]{0:T(128)} %pad_add_fusion.1.refs_1_, bf16[2048,512]{1,0:T(8,128)(2,1)} %get-tuple-element.67.refs_6_.refs_2_, bf16[2048,512]{1,0:T(8,128)(2,1)} %get-tuple-element.73.refs_4_.refs_3_, ...), custom_call_target="tpu_custom_call" | custom-call | flops 999999995904 | bytes 1 | tf_op jit(solution)/shard_map/pallas_call | solution.py:55
  523.4 7.4 collective-permute-done.17.refs_5_
  530.9 7.7 shard_map.320
  550.2 45.7 %collective-permute-done.16.refs_4_ = bf16[512,2048]{1,0:T(8,128)(2,1)} collective-permute-done((bf16[512,2048]{1,0:T(8,128)(2,1)S(1)}, bf16[512,2048]{1,0:T(8,128)(2,1)}, u32[]{:S(2)}, u32[]{:S(2)}) %collective-permute-start.16) | collective-permute-done | bytes 2097184 | tf_op jit(solution)/shard_map/ppermute | solution.py:685
  596.0 5.2 shard_map.321.refs_8_.refs_1_
  607.1 30.4 %collective-permute-done.21.refs_7_ = bf16[4,1,4,256,512]{4,3,2,1,0:T(8,128)(2,1)} collective-permute-done((bf16[4,1,4,256,512]{4,3,2,1,0:T(8,128)(2,1)}, bf16[4,1,4,256,512]{4,3,2,1,0:T(8,128)(2,1)}, u32[]{:S(2)}, u32[]{:S(2)}) %collective-permute-start.21) | collective-permute-done | bytes 4194336 | tf_op jit(solution)/shard_map/ppermute | solution.py:685
  638.9 16.7 %shard_map.322.refs_3_ = bf16[4,1,4,256,512]{4,3,2,1,0:T(8,128)(2,1)} custom-call(s32[1]{0:T(128)} %bitcast.5.refs_0_, bf16[4,2,256,2048]{3,2,1,0:T(8,128)(2,1)} %bitcast.136, bf16[4,2,256,2048]{3,2,1,0:T(8,128)(2,1)} %bitcast.125, bf16[2048,512]{1,0:T(8,128)(2,1)} %get-tuple-element.82.refs_3_.refs_7_, bf16[2048,512]{1,0:T(8,128)(2,1)} %get-tuple-element.77.refs_4_.refs_5_, ...), custom_call_target="tpu_custom_call" | custom-call | flops 999999995904 | bytes 1 | tf_op jit(solution)/shard_map/pallas_call | solution.py:55
  661.2 4.5 shard_map.323
  670.1 13.2 %collective-permute-done.19.refs_0_ = bf16[512,2048]{1,0:T(8,128)(2,1)} collective-permute-done((bf16[512,2048]{1,0:T(8,128)(2,1)}, bf16[512,2048]{1,0:T(8,128)(2,1)}, u32[]{:S(2)}, u32[]{:S(2)}) %collective-permute-start.19) | collective-permute-done | bytes 2097184 | tf_op jit(solution)/shard_map/ppermute | solution.py:685
  686.5 10.9 %shard_map.327.refs_5_ = bf16[2048,2048]{1,0:T(8,128)(2,1)} custom-call(s32[4]{0:T(128)} %pad_add_fusion.refs_0_, bf16[512,2048]{1,0:T(8,128)(2,1)} %get-tuple-element.91.refs_1_, bf16[512,2048]{1,0:T(8,128)(2,1)} %collective-permute-done.24.refs_2_, bf16[512,2048]{1,0:T(8,128)(2,1)} %shard_map.324.refs_3_, ...), custom_call_target="tpu_custom_call" | custom-call | flops 999999995904 | bytes 1 | tf_op jit(solution)/shard_map/pallas_call | solution.py:55
  697.4 10.8 %shard_map.328.refs_3_ = bf16[2048,2048]{1,0:T(8,128)(2,1)} custom-call(s32[4]{0:T(128)} %pad_add_fusion.refs_0_, bf16[512,2048]{1,0:T(8,128)(2,1)} %shard_map.321.refs_8_.refs_1_, bf16[512,2048]{1,0:T(8,128)(2,1)} %collective-permute-done.18.refs_2_, bf16[512,2048]{1,0:T(8,128)(2,1)} %shard_map.326.refs_5_.refs_3_, ...), custom_call_target="tpu_custom_call" | custom-call | flops 999999995904 | bytes 1 | tf_op jit(solution)/shard_map/pallas_call | solution.py:55
  708.2 21.9 %reduce-scatter.8.cloned.1.call-done.refs_1_ = bf16[4,256,512]{2,1,0:T(8,128)(2,1)} async-done(((bf16[16,256,512]{2,1,0:T(8,128)(2,1)}), bf16[4,256,512]{2,1,0:T(8,128)(2,1)}) %reduce-scatter.8.cloned.1.call-update) | async-done | bytes 1048592 | tf_op jit(solution)/shard_map/reduce_scatter | solution.py:806
  754.9 8.9 %fusion.8 = (f32[256,5,512]{2,0,1:T(8,128)}, f32[256,5,512]{2,0,1:T(8,128)}, f32[256,5,512]{2,0,1:T(8,128)}) fusion(f32[]{:T(128)S(6)} %div.99, f32[12,256,512]{2,1,0:T(8,128)} %get-tuple-element.96, f32[256,5,512]{2,0,1:T(8,128)} %param.26, f32[256,5,512]{2,0,1:T(8,128)} %param.25, f32[256,5,512]{2,0,1:T(8,128)S(1)} %copy-done.1), kind=kLoop, calls=%fused_computation.22 | loop fusion | flops 10485760 | bytes 18350084 | tf_op jit(solution)/shard_map/transpose | solution.py:934
  763.9 7.1 fusion.7
  (236 shorter events, 114.3 us)
Async XLA Ops:
  7.2 56.2 %all-gather.13.cloned.1.call-start = ((), (), s32[]{:S(2)}) async-start(), calls=%async_computation.6 | async-start | bytes 2621440 | tf_op jit(solution)/shard_map/all_gather | solution.py:764
  9.3 97.3 %all-gather.15.cloned.1.call-start = ((), (), s32[]{:S(2)}) async-start(), calls=%async_computation.7 | async-start | bytes 2621440 | tf_op jit(solution)/shard_map/all_gather | solution.py:764
  11.4 142.0 %all-gather.17.cloned.1.call-start = ((), (), s32[]{:S(2)}) async-start(), calls=%async_computation.8 | async-start | bytes 2621440 | tf_op jit(solution)/shard_map/all_gather | solution.py:764
  13.5 207.7 %all-gather.19.cloned.1.call-start = ((), (), s32[]{:S(2)}) async-start(), calls=%async_computation.9 | async-start | bytes 2621440 | tf_op jit(solution)/shard_map/all_gather | solution.py:764
  15.7 246.5 %all-gather.23.cloned.1.call-start = ((), (), s32[]{:S(2)}) async-start(), calls=%async_computation.11 | async-start | bytes 2621440 | tf_op jit(solution)/shard_map/all_gather | solution.py:764
  17.8 275.2 %all-gather.21.cloned.1.call-start = ((), (), s32[]{:S(2)}) async-start(), calls=%async_computation.10 | async-start | bytes 2621440 | tf_op jit(solution)/shard_map/all_gather | solution.py:764
  18.1 20.9 %collective-permute-start.6 = (f32[1,1472]{1,0:T(1,128)S(1)}, f32[1,1472]{1,0:T(1,128)S(1)}, u32[]{:S(2)}, u32[]{:S(2)}) collective-permute-start(f32[1,1472]{1,0:T(1,128)S(1)} %maximum_convert_fusion), channel_id=1, source_target_pairs={{0,4},{4,8},{8,12},{12,16},{16,20},{20,24},{24,28},{28,0},{1,5},{5... | collective-permute-start | bytes 17672 | tf_op jit(solution)/shard_map/ppermute | solution.py:665
  21.1 19.4 %collective-permute-start.5 = (f32[1,1472]{1,0:T(1,128)S(1)}, f32[1,1472]{1,0:T(1,128)S(1)}, u32[]{:S(2)}, u32[]{:S(2)}) collective-permute-start(f32[1,1472]{1,0:T(1,128)S(1)} %maximum_convert_fusion), channel_id=1, source_target_pairs={{0,8},{4,12},{8,16},{12,20},{16,24},{20,28},{24,0},{28,4},{1,9},{5... | collective-permute-start | bytes 17672 | tf_op jit(solution)/shard_map/ppermute | solution.py:665
  22.6 20.2 %collective-permute-start.4 = (f32[1,1472]{1,0:T(1,128)S(1)}, f32[1,1472]{1,0:T(1,128)S(1)}, u32[]{:S(2)}, u32[]{:S(2)}) collective-permute-start(f32[1,1472]{1,0:T(1,128)S(1)} %maximum_convert_fusion), channel_id=1, source_target_pairs={{0,12},{4,16},{8,20},{12,24},{16,28},{20,0},{24,4},{28,8},{1,13},{... | collective-permute-start | bytes 17672 | tf_op jit(solution)/shard_map/ppermute | solution.py:665
  31.2 572.9 %reduce-scatter.6.cloned.1.call-start = ((), (), s32[]{:S(2)}) async-start(), calls=%async_computation.4 | async-start | bytes 10485760 | tf_op jit(solution)/shard_map/reduce_scatter | solution.py:806
  63.3 46.0 %collective-permute-start.7 = (bf16[4,2,256,512]{3,2,1,0:T(8,128)(2,1)}, bf16[4,2,256,512]{3,2,1,0:T(8,128)(2,1)S(1)}, u32[]{:S(2)}, u32[]{:S(2)}) collective-permute-start(bf16[4,2,256,512]{3,2,1,0:T(8,128)(2,1)} %shard_map.296.refs_1_.refs_5_.refs_9_.refs_7_), channel_id=1, source_target_pairs={{0,4},{4,0},{8,12},{12,8},{16,20},{20,16},{24,28},{28,24},{1,5},{5... | collective-permute-start | bytes 6291464 | tf_op jit(solution)/shard_map/ppermute | solution.py:685
  106.6 49.2 %collective-permute-start.8 = (bf16[4,2,256,512]{3,2,1,0:T(8,128)(2,1)}, bf16[4,2,256,512]{3,2,1,0:T(8,128)(2,1)}, u32[]{:S(2)}, u32[]{:S(2)}) collective-permute-start(bf16[4,2,256,512]{3,2,1,0:T(8,128)(2,1)} %shard_map.297.refs_1_.refs_7_.refs_11_.refs_9_), channel_id=1, source_target_pairs={{0,4},{4,0},{8,12},{12,8},{16,20},{20,16},{24,28},{28,24},{1,5},{5... | collective-permute-start | bytes 6291464 | tf_op jit(solution)/shard_map/ppermute | solution.py:685
  153.5 144.1 %collective-permute-start.9 = (bf16[4,2,256,512]{3,2,1,0:T(8,128)(2,1)}, bf16[4,2,256,512]{3,2,1,0:T(8,128)(2,1)}, u32[]{:S(2)}, u32[]{:S(2)}) collective-permute-start(bf16[4,2,256,512]{3,2,1,0:T(8,128)(2,1)} %shard_map.299.refs_9_.refs_4_.refs_13_.refs_11_), channel_id=1, source_target_pairs={{0,4},{4,0},{8,12},{12,8},{16,20},{20,16},{24,28},{28,24},{1,5},{5... | collective-permute-start | bytes 6291464 | tf_op jit(solution)/shard_map/ppermute | solution.py:685
  221.3 93.0 %collective-permute-start.10 = (bf16[4,2,256,512]{3,2,1,0:T(8,128)(2,1)}, bf16[4,2,256,512]{3,2,1,0:T(8,128)(2,1)}, u32[]{:S(2)}, u32[]{:S(2)}) collective-permute-start(bf16[4,2,256,512]{3,2,1,0:T(8,128)(2,1)} %shard_map.302.refs_12_.refs_4_.refs_15_.refs_13_), channel_id=1, source_target_pairs={{0,4},{4,0},{8,12},{12,8},{16,20},{20,16},{24,28},{28,24},{1,5},{5... | collective-permute-start | bytes 6291464 | tf_op jit(solution)/shard_map/ppermute | solution.py:685
  262.2 68.0 %collective-permute-start.11 = (bf16[4,2,256,512]{3,2,1,0:T(8,128)(2,1)}, bf16[4,2,256,512]{3,2,1,0:T(8,128)(2,1)S(1)}, u32[]{:S(2)}, u32[]{:S(2)}) collective-permute-start(bf16[4,2,256,512]{3,2,1,0:T(8,128)(2,1)} %shard_map.304.refs_7_.refs_4_.refs_17_.refs_15_), channel_id=1, source_target_pairs={{0,4},{4,0},{8,12},{12,8},{16,20},{20,16},{24,28},{28,24},{1,5},{5... | collective-permute-start | bytes 6291464 | tf_op jit(solution)/shard_map/ppermute | solution.py:685
  293.0 65.5 %collective-permute-start.12 = (bf16[4,2,256,512]{3,2,1,0:T(8,128)(2,1)}, bf16[4,2,256,512]{3,2,1,0:T(8,128)(2,1)}, u32[]{:S(2)}, u32[]{:S(2)}) collective-permute-start(bf16[4,2,256,512]{3,2,1,0:T(8,128)(2,1)} %shard_map.306.refs_6_.refs_4_.refs_19_.refs_17_), channel_id=1, source_target_pairs={{0,4},{4,0},{8,12},{12,8},{16,20},{20,16},{24,28},{28,24},{1,5},{5... | collective-permute-start | bytes 6291464 | tf_op jit(solution)/shard_map/ppermute | solution.py:685
  297.5 368.3 %reduce-scatter.4.cloned.1.call-start = ((), (), s32[]{:S(2)}) async-start(), calls=%async_computation.3 | async-start | bytes 5242880 | tf_op jit(solution)/shard_map/reduce_scatter | solution.py:806
  375.1 109.4 %collective-permute-start.14 = (bf16[4,1,4,256,512]{4,3,2,1,0:T(8,128)(2,1)}, bf16[4,1,4,256,512]{4,3,2,1,0:T(8,128)(2,1)}, u32[]{:S(2)}, u32[]{:S(2)}) collective-permute-start(bf16[4,1,4,256,512]{4,3,2,1,0:T(8,128)(2,1)} %shard_map.312.refs_6_), channel_id=1, source_target_pairs={{0,4},{4,0},{8,12},{12,8},{16,20},{20,16},{24,28},{28,24},{1,5},{5... | collective-permute-start | bytes 12582920 | tf_op jit(solution)/shard_map/ppermute | solution.py:685
  434.7 20.0 %collective-permute-start.15 = (bf16[1024,2048]{1,0:T(8,128)(2,1)}, bf16[1024,2048]{1,0:T(8,128)(2,1)}, u32[]{:S(2)}, u32[]{:S(2)}) collective-permute-start(bf16[1024,2048]{1,0:T(8,128)(2,1)} %shard_map.315.refs_19_), channel_id=1, source_target_pairs={{0,1},{1,0},{2,3},{3,2},{4,5},{5,4},{6,7},{7,6},{8,9},{9,8},{10,11... | collective-permute-start | bytes 12582920 | tf_op jit(solution)/shard_map/ppermute | solution.py:685
  454.2 47.2 %collective-permute-start.13 = (bf16[1024,2048]{1,0:T(8,128)(2,1)}, bf16[1024,2048]{1,0:T(8,128)(2,1)}, u32[]{:S(2)}, u32[]{:S(2)}) collective-permute-start(bf16[1024,2048]{1,0:T(8,128)(2,1)} %shard_map.316.refs_22_), channel_id=1, source_target_pairs={{0,1},{1,0},{2,3},{3,2},{4,5},{5,4},{6,7},{7,6},{8,9},{9,8},{10,11... | collective-permute-start | bytes 12582920 | tf_op jit(solution)/shard_map/ppermute | solution.py:685
  482.9 48.0 %collective-permute-start.17 = (bf16[512,2048]{1,0:T(8,128)(2,1)}, bf16[512,2048]{1,0:T(8,128)(2,1)}, u32[]{:S(2)}, u32[]{:S(2)}) collective-permute-start(bf16[512,2048]{1,0:T(8,128)(2,1)} %get-tuple-element.85.refs_8_), channel_id=1, source_target_pairs={{0,2},{1,3},{2,0},{3,1},{4,6},{5,7},{6,4},{7,5},{8,10},{9,11},{10,... | collective-permute-start | bytes 6291464 | tf_op jit(solution)/shard_map/ppermute | solution.py:685
  545.5 92.0 %collective-permute-start.21 = (bf16[4,1,4,256,512]{4,3,2,1,0:T(8,128)(2,1)}, bf16[4,1,4,256,512]{4,3,2,1,0:T(8,128)(2,1)}, u32[]{:S(2)}, u32[]{:S(2)}) collective-permute-start(bf16[4,1,4,256,512]{4,3,2,1,0:T(8,128)(2,1)} %shard_map.314.refs_21_), channel_id=1, source_target_pairs={{0,4},{4,0},{8,12},{12,8},{16,20},{20,16},{24,28},{28,24},{1,5},{5... | collective-permute-start | bytes 12582920 | tf_op jit(solution)/shard_map/ppermute | solution.py:685
  547.3 48.7 %collective-permute-start.16 = (bf16[512,2048]{1,0:T(8,128)(2,1)S(1)}, bf16[512,2048]{1,0:T(8,128)(2,1)}, u32[]{:S(2)}, u32[]{:S(2)}) collective-permute-start(bf16[512,2048]{1,0:T(8,128)(2,1)S(1)} %copy-done.24), channel_id=1, source_target_pairs={{0,2},{1,3},{2,0},{3,1},{4,6},{5,7},{6,4},{7,5},{8,10},{9,11},{10,... | collective-permute-start | bytes 6291464 | tf_op jit(solution)/shard_map/ppermute | solution.py:685
  548.8 181.2 %reduce-scatter.8.cloned.1.call-start = ((), (), s32[]{:S(2)}) async-start(), calls=%async_computation.5 | async-start | bytes 5242880 | tf_op jit(solution)/shard_map/reduce_scatter | solution.py:806
  548.9 137.6 %collective-permute-start.24 = (bf16[512,2048]{1,0:T(8,128)(2,1)}, bf16[512,2048]{1,0:T(8,128)(2,1)}, u32[]{:S(2)}, u32[]{:S(2)}) collective-permute-start(bf16[512,2048]{1,0:T(8,128)(2,1)} %get-tuple-element.91.refs_1_), channel_id=1, source_target_pairs={{0,1},{1,0},{2,3},{3,2},{4,5},{5,4},{6,7},{7,6},{8,9},{9,8},{10,11... | collective-permute-start | bytes 6291464 | tf_op jit(solution)/shard_map/ppermute | solution.py:685
  549.0 116.7 %collective-permute-start.22 = (bf16[512,2048]{1,0:T(8,128)(2,1)}, bf16[512,2048]{1,0:T(8,128)(2,1)}, u32[]{:S(2)}, u32[]{:S(2)}) collective-permute-start(bf16[512,2048]{1,0:T(8,128)(2,1)} %get-tuple-element.91.refs_1_), channel_id=1, source_target_pairs={{0,2},{1,3},{2,0},{3,1},{4,6},{5,7},{6,4},{7,5},{8,10},{9,11},{10,... | collective-permute-start | bytes 6291464 | tf_op jit(solution)/shard_map/ppermute | solution.py:685
  550.2 52.5 %collective-permute-start.29 = (f32[1,9728]{1,0:T(1,128)}, f32[1,9728]{1,0:T(1,128)}, u32[]{:S(2)}, u32[]{:S(2)}) collective-permute-start(f32[1,9728]{1,0:T(1,128)} %fusion.12), channel_id=1, source_target_pairs={{0,8},{4,12},{8,0},{12,4},{16,24},{20,28},{24,16},{28,20},{1,9},{5... | collective-permute-start | bytes 116744 | tf_op jit(solution)/shard_map/ppermute | solution.py:673
  601.1 82.1 %collective-permute-start.19 = (bf16[512,2048]{1,0:T(8,128)(2,1)}, bf16[512,2048]{1,0:T(8,128)(2,1)}, u32[]{:S(2)}, u32[]{:S(2)}) collective-permute-start(bf16[512,2048]{1,0:T(8,128)(2,1)} %shard_map.321.refs_8_.refs_1_), channel_id=1, source_target_pairs={{0,2},{1,3},{2,0},{3,1},{4,6},{5,7},{6,4},{7,5},{8,10},{9,11},{10,... | collective-permute-start | bytes 6291464 | tf_op jit(solution)/shard_map/ppermute | solution.py:685
  604.1 51.5 %collective-permute-start.30 = (f32[1,9728]{1,0:T(1,128)}, f32[1,9728]{1,0:T(1,128)}, u32[]{:S(2)}, u32[]{:S(2)}) collective-permute-start(f32[1,9728]{1,0:T(1,128)} %add.241), channel_id=1, source_target_pairs={{0,16},{4,20},{8,24},{12,28},{16,0},{20,4},{24,8},{28,12},{1,17},{... | collective-permute-start | bytes 116744 | tf_op jit(solution)/shard_map/ppermute | solution.py:673
  637.5 23.6 %collective-permute-start.20 = (bf16[4,256,512]{2,1,0:T(8,128)(2,1)}, bf16[4,256,512]{2,1,0:T(8,128)(2,1)}, u32[]{:S(2)}, u32[]{:S(2)}) collective-permute-start(bf16[4,256,512]{2,1,0:T(8,128)(2,1)} %get-tuple-element.111), channel_id=1, source_target_pairs={{0,4},{4,0},{8,12},{12,8},{16,20},{20,16},{24,28},{28,24},{1,5},{5... | collective-permute-start | bytes 3145736 | tf_op jit(solution)/shard_map/ppermute | solution.py:685
  655.6 41.7 %collective-permute-start.18 = (bf16[512,2048]{1,0:T(8,128)(2,1)}, bf16[512,2048]{1,0:T(8,128)(2,1)}, u32[]{:S(2)}, u32[]{:S(2)}) collective-permute-start(bf16[512,2048]{1,0:T(8,128)(2,1)} %shard_map.321.refs_8_.refs_1_), channel_id=1, source_target_pairs={{0,1},{1,0},{2,3},{3,2},{4,5},{5,4},{6,7},{7,6},{8,9},{9,8},{10,11... | collective-permute-start | bytes 6291464 | tf_op jit(solution)/shard_map/ppermute | solution.py:685
  665.7 20.8 %collective-permute-start.25 = (bf16[512,2048]{1,0:T(8,128)(2,1)}, bf16[512,2048]{1,0:T(8,128)(2,1)}, u32[]{:S(2)}, u32[]{:S(2)}) collective-permute-start(bf16[512,2048]{1,0:T(8,128)(2,1)} %shard_map.324.refs_3_), channel_id=1, source_target_pairs={{0,1},{1,0},{2,3},{3,2},{4,5},{5,4},{6,7},{7,6},{8,9},{9,8},{10,11... | collective-permute-start | bytes 6291464 | tf_op jit(solution)/shard_map/ppermute | solution.py:685
  (41 other events, 434.9 us)
Sparse Core Ops, SparseCore 0:
  10.2 49.5 all-gather.12
  61.9 44.6 all-gather.14
  108.8 44.6 all-gather.16
  154.9 44.6 all-gather.18
  201.0 44.6 all-gather.22
  247.1 44.6 all-gather.20
  297.6 142.6 reduce-scatter.5
  549.0 74.6 reduce-scatter.3
  655.8 74.2 reduce-scatter.7
